TPU v7x, 512 devices: a whole 4x8x8 slice. The times are simulated.
512 devices in a mesh: row: 64 (over z, y), blk: 8 (over x, core).
Axes of the slice: x: 4, y: 8, z: 8, core: 2. Of those that a mesh axis runs over, the one named last changes fastest.
Arguments:
- matrix: float32 [65536, 2048], P('row', 'blk'), may hold values from -24 to 24, as said below
- sender_slot: int32 [4, 8], P(None, 'blk'), may hold values from 0 to 1
Outputs:
- rotated_matrix: float32 [65536, 2048], P('row', 'blk')
Inputs may be any that keep to these rules, and one draw needn't show every extreme that they name: Each entry of the matrix has a column factor that differs from column to column.
All inputs are finite; a program needn't handle non-finite values.
Results may differ from a plain program's by a relative error of at most 0.0003.
Values sent between devices are 32-bit elements; how exact they have to be, the bound alone decides.
No kernel may reach another device: no remote copies, remote signals or barrier semaphores. Data moves between devices by JAX's collectives and lax.ppermute only.
A program may use at most 64 MiB of HBM per device.

v0:
```python
import jax
import jax.numpy as jnp
from jax import lax
from jax.experimental import pallas as pl
from jax.experimental.pallas import tpu as pltpu
from jax.sharding import PartitionSpec as P

STEPS = 4
ROUNDS = 8
N = 256
HALF = 128
TILES = 64
PERIOD = N - 1


def dot(left, right, over=(1, 0), precision=lax.Precision.HIGHEST):
    return lax.dot_general(
        left,
        right,
        (((over[0],), (over[1],)), ((), ())),
        precision=precision,
        preferred_element_type=jnp.float32,
    )


def seats(position, round_index):
    upper = position + round_index
    upper = jnp.where(upper >= PERIOD, upper - PERIOD, upper)
    lower = round_index - (position - HALF)
    lower = jnp.where(lower < 0, lower + PERIOD, lower)
    return jnp.where(position < HALF, upper, jnp.where(position == HALF, PERIOD, lower))


def placing(round_index, swapped=None):
    index = lax.broadcasted_iota(jnp.int32, (N, N), 0)
    if swapped is not None:
        index = jnp.where(swapped, jnp.where(index < HALF, index + HALF, index - HALF), index)
    position = lax.broadcasted_iota(jnp.int32, (N, N), 1)
    return (index == seats(position, round_index)).astype(jnp.bfloat16)


def thirds(values):
    high = values.astype(jnp.bfloat16)
    rest = values - high.astype(jnp.float32)
    middle = rest.astype(jnp.bfloat16)
    return high, middle, (rest - middle.astype(jnp.float32)).astype(jnp.bfloat16)


def placed(pieces, place, over):
    numbers = (((1,), (over,)), ((), ()))
    return [lax.dot_general(x, place, numbers, preferred_element_type=jnp.float32) for x in pieces]


def laid_both(values, place, over):
    columns = [x.astype(jnp.bfloat16) for x in placed(thirds(values), place, over)]
    numbers = (((over,), (0,)), ((), ()))
    return sum(lax.dot_general(place, x, numbers, preferred_element_type=jnp.float32) for x in columns)


def rotations(upper_diag, coupling, lower_diag, round_index):
    position = lax.broadcasted_iota(jnp.int32, (1, HALF), 1)
    is_lower = seats(position, round_index) < seats(position + HALF, round_index)
    difference = jnp.where(is_lower, lower_diag - upper_diag, upper_diag - lower_diag)
    x = jnp.abs(difference)
    y = jnp.where(difference >= 0.0, 2.0 * coupling, -2.0 * coupling)
    largest = jnp.maximum(x, jnp.abs(y))
    scale = jnp.where(largest > 0.0, largest, 1.0)
    x = jnp.where(largest > 0.0, x / scale, 1.0)
    y = y / scale
    tangent = y / (x + jnp.sqrt(x * x + y * y))
    cosine = 1.0 / jnp.sqrt(1.0 + tangent * tangent)
    sine = tangent * cosine
    return cosine, jnp.where(is_lower, -sine, sine)


def turn(upper, lower, cosine, sine):
    return cosine * upper + sine * lower, cosine * lower - sine * upper


def shift(upper, lower, axis):
    at = lax.broadcasted_iota(jnp.int32, upper.shape, axis)
    new_upper = jnp.where(at == HALF - 1, lower, pltpu.roll(upper, HALF - 1, axis))
    moved = pltpu.roll(jnp.where(at == 0, upper, lower), 1, axis)
    return new_upper, jnp.where(at == 0, lower, moved)


def jacobi(gram, offset, second, parts):
    uu, ul, lu, ll, qu, ql = parts
    start = placing(offset)
    laid_out = laid_both(gram, start, 0)
    uu[...] = laid_out[:HALF, :HALF]
    ul[...] = laid_out[:HALF, HALF:]
    lu[...] = laid_out[HALF:, :HALF]
    ll[...] = laid_out[HALF:, HALF:]
    qu[...] = start[:, :HALF].astype(jnp.float32)
    ql[...] = start[:, HALF:].astype(jnp.float32)
    shape = (HALF, HALF)
    eye = lax.broadcasted_iota(jnp.int32, shape, 0) == lax.broadcasted_iota(jnp.int32, shape, 1)

    def diagonal(ref):
        return jnp.sum(jnp.where(eye, ref[...], 0.0), axis=0, keepdims=True)

    def stood(row):
        return jnp.sum(jnp.where(eye, jnp.broadcast_to(row, shape), 0.0), axis=1, keepdims=True)

    for round_index in range(offset, offset + ROUNDS):
        cosine, sine = rotations(diagonal(uu), diagonal(ul), diagonal(ll), round_index)
        cosine_col, sine_col = stood(cosine), stood(sine)
        a, b = shift(*turn(uu[...], ul[...], cosine, sine), 1)
        c, d = shift(*turn(lu[...], ll[...], cosine, sine), 1)
        uu[...], lu[...] = shift(*turn(a, c, cosine_col, sine_col), 0)
        ul[...], ll[...] = shift(*turn(b, d, cosine_col, sine_col), 0)
        qu[...], ql[...] = shift(*turn(qu[...], ql[...], cosine, sine), 1)
    end = placing(offset + ROUNDS, second == 0)
    rotation = sum(placed(thirds(jnp.concatenate([qu[...], ql[...]], axis=1)), end, 1))
    upper = jnp.concatenate([uu[...], ul[...]], axis=1)
    lower = jnp.concatenate([lu[...], ll[...]], axis=1)
    rotated_gram = laid_both(jnp.concatenate([upper, lower], axis=0), end, 1)
    return rotation, rotated_gram


def joined(kept_gram, cross, moved_gram):
    upper = jnp.concatenate([kept_gram, cross], axis=1)
    lower = jnp.concatenate([cross.T, moved_gram], axis=1)
    return jnp.concatenate([upper, lower], axis=0)


def tiles(square):
    sides = [square[:, :HALF].reshape(-1, 1, 8, HALF), square[:, HALF:].reshape(-1, 1, 8, HALF)]
    return jnp.concatenate(sides, axis=1)


def square_of(received, place):
    count, height = received.shape[0], TILES // received.shape[0] * 8
    part = received[:, place * height : (place + 1) * height, :].reshape(TILES // 2, 2, 8, HALF)
    return jnp.concatenate([part[:, 0].reshape(N, HALF), part[:, 1].reshape(N, HALF)], axis=1)


def pack_kernel(skipped, received, *refs):
    *blocks, out = refs
    count, height = out.shape[0], TILES // out.shape[0] * 8
    if received is not None:
        spread = received.shape[1] - skipped * height
        own = jnp.sum(received[:, skipped * height :, :], axis=0, keepdims=True)
        out[:, :spread, :] = jnp.broadcast_to(own, (count, spread, HALF))
    else:
        spread = 0
    for number, block in enumerate(blocks):
        at = spread + number * height
        out[:, at : at + height, :] = tiles(block[...]).reshape(count, height, HALF)


def step0_kernel(second, received, out, h0, *parts):
    q0, h0[...] = jacobi(square_of(received, 0), 0, second[0, 0], parts)
    out[:N] = q0
    out[N:] = h0[HALF:]


def step1_kernel(second, received, out0, h0, in0, out, h1, r1, *parts):
    q0, q0_p = out0[:N], in0[:N]
    r1[...] = dot(dot(q0, square_of(received, 0), (0, 0)), q0_p)
    gram = joined(h0[:HALF, :HALF], r1[:HALF, HALF:], in0[N:, HALF:])
    q1, h1[...] = jacobi(gram, ROUNDS, second[1, 0], parts)
    out[:N] = q1
    out[N : N + HALF] = h1[HALF:]
    out[N + HALF : 2 * N] = r1[HALF:]
    out[2 * N :] = q0_p


def cross2_kernel(received, out0, in0, out1, in1, h1, r1, out, kept, gram):
    q0, q0_pp = out0[:N], in1[2 * N :]
    r2 = dot(dot(q0, square_of(received, 1), (0, 0)), q0_pp)
    q1, q1_p = out1[:N], in1[:N]
    upper = jnp.concatenate([r1[:HALF, :HALF], r2[:HALF, HALF:]], axis=1)
    lower = jnp.concatenate([in0[N:, :HALF], in1[N + HALF : 2 * N, HALF:]], axis=1)
    s1 = dot(dot(q1, jnp.concatenate([upper, lower], axis=0), (0, 0)), q1_p)
    gram[...] = joined(h1[:HALF, :HALF], s1[:HALF, HALF:], in1[N : N + HALF, HALF:])
    out[:HALF] = s1[HALF:, HALF:]
    out[HALF:N] = r2[HALF:, HALF:]
    out[N : 2 * N] = q1_p[:, HALF:]
    out[2 * N :] = q0_pp[:, HALF:]
    kept[:HALF] = s1[:HALF, :HALF]
    kept[HALF:] = r2[:HALF, :HALF]


def step2_kernel(second, gram, out, q2, h2, *parts):
    q2[...], h2[...] = jacobi(gram[...], 2 * ROUNDS, second[2, 0], parts)
    out[:N] = q2[:, HALF:]
    out[N:] = h2[HALF:, HALF:]


def cross3_kernel(out0, out1, in1, kept, q2, in2a, in2b, cross, left, right):
    q0_k, q1_k, q2_k = out0[:N, :HALF], out1[:N, :HALF], q2[:, :HALF]
    q2_p, q1_pp, q0_ppp = in2b[:N], in2a[N : 2 * N], in2a[2 * N :]
    upper = jnp.concatenate([kept[HALF:], jnp.zeros((HALF, HALF), jnp.float32)], axis=1)
    lower = jnp.concatenate([in1[N + HALF : 2 * N, :HALF], in2a[HALF:N]], axis=1)
    t = dot(dot(q1_k, jnp.concatenate([upper, lower], axis=0), (0, 0)), q1_pp)
    upper = jnp.concatenate([kept[:HALF], t], axis=1)
    lower = jnp.concatenate([in1[N : N + HALF, :HALF], in2a[:HALF]], axis=1)
    cross[...] = dot(dot(q2_k, jnp.concatenate([upper, lower], axis=0), (0, 0)), q2_p)
    left[...] = dot(q0_k, dot(q1_k[:HALF], q2_k[:HALF]))
    right[...] = dot(q0_ppp, dot(q1_pp[HALF:], q2_p[HALF:]))


def weights_kernel(in0, in1, in2a, in2b, out):
    q2_k, q2_m = in2b[:HALF], in2b[HALF:N]
    q1_pp, q0_pp = in2a[N : 2 * N], in1[2 * N :]
    out[:N] = dot(in0[:N, :HALF], dot(in1[:HALF, :HALF], q2_k))
    travelled = dot(q0_pp[:, HALF:], dot(in1[HALF:N, :HALF], q2_k))
    out[N : 2 * N] = travelled + dot(q0_pp[:, :HALF], dot(q1_pp[:HALF], q2_m))
    out[2 * N :] = dot(in2a[2 * N :], dot(q1_pp[HALF:], q2_m))


def step3_kernel(second, received, cross, left, right, h2, in2b, q3, *parts):
    total = cross[...] + dot(left[...], dot(square_of(received, 0), right[...]), (0, 0))
    gram = joined(h2[:HALF, :HALF], total, in2b[N:])
    q3[...], _ = jacobi(gram, 3 * ROUNDS, second[3, 0], parts)


JACOBI_PARTS = [pltpu.VMEM((HALF, HALF), jnp.float32)] * 4 + [pltpu.VMEM((N, HALF), jnp.float32)] * 2


def run(kernel, shapes, *operands, solves=True, last=()):
    vmem, smem = pl.BlockSpec(memory_space=pltpu.VMEM), pl.BlockSpec(memory_space=pltpu.SMEM)
    specs = [smem if x.dtype == jnp.int32 else vmem for x in operands] + [pl.BlockSpec(memory_space=pl.ANY)] * len(last)

    def body(*refs):
        given = len(operands)
        kernel(*refs[:given], *refs[given + len(last) :])

    return pl.pallas_call(
        body,
        out_shape=[jax.ShapeDtypeStruct(shape, jnp.float32) for shape in shapes],
        in_specs=specs,
        out_specs=[vmem] * len(shapes),
        scratch_shapes=JACOBI_PARTS if solves else [],
        compiler_params=pltpu.CompilerParams(vmem_limit_bytes=16 * 2**20),
        cost_estimate=pl.CostEstimate(flops=10**6, bytes_accessed=2**10, transcendentals=0),
    )(*operands, *last)


def product(left, right, over=(1, 0)):
    return dot(left, right, over, lax.Precision.HIGH)


def shards(matrix, sender_slot):
    devices, count = lax.axis_size("blk"), lax.axis_size("row")

    def onward(values, places=1):
        return lax.ppermute(values, "blk", [((i - places) % devices, i) for i in range(devices)])

    def exchange(received, skipped, *blocks, last=()):
        height = TILES // count * 8
        given = [] if received is None else [received]
        total = len(blocks) * height + (0 if received is None else received.shape[1] - skipped * height)

        def kernel(*refs):
            pack_kernel(skipped, refs[0] if given else None, *refs[len(given) :])

        (pieces,) = run(kernel, [(count, total, HALF)], *given, *blocks, solves=False, last=last)
        return lax.all_to_all(pieces, "row", 0, 0, tiled=True)

    def rotated(pair_cols, rotation):
        arrived = onward(product(pair_cols, rotation[:, HALF:]))
        return jnp.concatenate([product(pair_cols, rotation[:, :HALF]), arrived], axis=1)

    square, block = (N, N), (HALF, HALF)
    before1, before2 = onward(matrix), onward(matrix, 2)
    received = exchange(None, 0, product(matrix, matrix, (0, 0)))
    c1, c2 = product(matrix, before1, (0, 0)), product(matrix, before2, (0, 0))
    with_gram = exchange(received, 0, c1, c2)
    before3 = onward(before2)
    c3 = product(matrix, before3, (0, 0))
    with_c12 = exchange(with_gram, 1, c3)
    out0, h0 = run(step0_kernel, [(N + HALF, N), square], sender_slot, with_gram)
    in0 = onward(out0)
    pair_cols = rotated(matrix, out0[:N])
    out1, h1, r1 = run(step1_kernel, [(3 * N, N), square, square], sender_slot, with_c12, out0, h0, in0)
    in1 = onward(out1)
    with_c3 = exchange(with_c12, 2, last=(out1,))
    pair_cols = rotated(pair_cols, out1[:N])
    out2a, kept, gram2 = run(
        cross2_kernel, [(3 * N, HALF), (N, HALF), square], with_c12, out0, in0, out1, in1, h1, r1, solves=False
    )
    in2a = onward(out2a)
    out2b, q2, h2 = run(step2_kernel, [(N + HALF, HALF), square, square], sender_slot, gram2)
    in2b = onward(out2b)
    cross, left, right = run(
        cross3_kernel, [block, (N, HALF), (N, HALF)], out0, out1, in1, kept, q2, in2a, in2b, solves=False
    )
    (weights,) = run(weights_kernel, [(3 * N, HALF)], in0, in1, in2a, in2b, solves=False)
    arrived = (
        product(before1, weights[:N]) + product(before2, weights[N : 2 * N]) + product(before3, weights[2 * N :])
    )
    pair_cols = jnp.concatenate([product(pair_cols, q2[:, :HALF]), arrived], axis=1)
    (q3,) = run(step3_kernel, [square], sender_slot, with_c3, cross, left, right, h2, in2b)
    return rotated(pair_cols, q3)


def solution(mesh):
    return jax.shard_map(
        shards,
        mesh=mesh,
        in_specs=(P("row", "blk"), P(None, "blk")),
        out_specs=P("row", "blk"),
        check_vma=False,
    )
```

profile of v0, /device:TPU:8, one launch (start us, length us, event | category | flops | bytes accessed | tf_op | source)
XLA Modules:
  0.0 170.5 jit_solution(3534564862531754920)
XLA Ops:
  0.0 0.0 collective-permute-start
  0.0 3.4 %collective-permute-start.1 = (f32[1024,256]{1,0:T(8,128)}, f32[1024,256]{1,0:T(8,128)}, u32[]{:S(2)}, u32[]{:S(2)}) collective-permute-start(f32[1024,256]{1,0:T(8,128)} %param.2), channel_id=1, source_target_pairs={{6,0},{7,1},{0,2},{1,3},{2,4},{3,5},{4,6},{5,7},{14,8},{15,9},{8,1... | collective-permute-start | bytes 3145736 | tf_op jit(solution)/shard_map/ppermute | solution.py:250
  3.4 0.0 copy-start.5
  3.4 2.6 %fusion.25.refs_0_ = f32[256,256]{1,0:T(8,128)S(1)} fusion(f32[1024,256]{1,0:T(8,128)} %param.2), kind=kOutput, calls=%fused_computation.32 | convolution fusion | flops 402653184 | bytes 1310720 | tf_op jit(solution)/shard_map/dot_general | solution.py:17
  6.1 0.7 shard_map.28
  6.8 16.6 %all-to-all-start = ((f32[64,8,128]{2,1,0:T(8,128)}), f32[64,8,128]{2,1,0:T(8,128)S(1)}, u32[]{:S(2)}, u32[]{:S(2)}) async-start(f32[64,8,128]{2,1,0:T(8,128)} %shard_map.28), calls=%async_computation | async-start | bytes 524288 | tf_op jit(solution)/shard_map/all_to_all | solution.py:261
  23.4 1.0 collective-permute-done
  24.4 1.0 fusion.26.refs_1_
  25.4 4.1 %collective-permute-done.1 = f32[1024,256]{1,0:T(8,128)} collective-permute-done((f32[1024,256]{1,0:T(8,128)}, f32[1024,256]{1,0:T(8,128)}, u32[]{:S(2)}, u32[]{:S(2)}) %collective-permute-start.1) | collective-permute-done | bytes 1048608 | tf_op jit(solution)/shard_map/ppermute | solution.py:250
  29.5 2.2 %fusion.27.refs_2_ = f32[256,256]{1,0:T(8,128)S(1)} fusion(f32[1024,256]{1,0:T(8,128)S(1)} %copy-done.5, f32[1024,256]{1,0:T(8,128)} %collective-permute-done.1), kind=kOutput, calls=%fused_computation.34 | convolution fusion | flops 402653184 | bytes 2359296 | tf_op jit(solution)/shard_map/dot_general | solution.py:17
  31.8 6.8 %all-to-all-done.refs_0_ = f32[64,8,128]{2,1,0:T(8,128)S(1)} async-done(((f32[64,8,128]{2,1,0:T(8,128)}), f32[64,8,128]{2,1,0:T(8,128)S(1)}, u32[]{:S(2)}, u32[]{:S(2)}) %all-to-all-start) | async-done | bytes 262176 | tf_op jit(solution)/shard_map/all_to_all | solution.py:261
  38.6 1.0 shard_map.29
  39.6 9.8 %all-to-all-start.1 = ((f32[64,24,128]{2,1,0:T(8,128)}), f32[64,24,128]{2,1,0:T(8,128)S(1)}, u32[]{:S(2)}, u32[]{:S(2)}) async-start(f32[64,24,128]{2,1,0:T(8,128)} %shard_map.29), calls=%async_computation.1 | async-start | bytes 1572864 | tf_op jit(solution)/shard_map/all_to_all | solution.py:261
  49.3 8.0 %collective-permute-start.3 = (f32[1024,256]{1,0:T(8,128)}, f32[1024,256]{1,0:T(8,128)S(1)}, u32[]{:S(2)}, u32[]{:S(2)}) collective-permute-start(f32[1024,256]{1,0:T(8,128)} %collective-permute-done.1), channel_id=1, source_target_pairs={{7,0},{0,1},{1,2},{2,3},{3,4},{4,5},{5,6},{6,7},{15,8},{8,9},{9,10... | collective-permute-start | bytes 3145736 | tf_op jit(solution)/shard_map/ppermute | solution.py:250
  57.3 13.8 %collective-permute-done.3 = f32[1024,256]{1,0:T(8,128)S(1)} collective-permute-done((f32[1024,256]{1,0:T(8,128)}, f32[1024,256]{1,0:T(8,128)S(1)}, u32[]{:S(2)}, u32[]{:S(2)}) %collective-permute-start.3) | collective-permute-done | bytes 1048608 | tf_op jit(solution)/shard_map/ppermute | solution.py:250
  71.2 1.0 copy-done.11
  72.1 1.0 fusion.28.refs_1_
  73.2 0.0 all-to-all-done.1.refs_1_.refs_0_
  73.2 1.0 shard_map.31
  74.2 12.8 %all-to-all-start.2 = ((f32[64,24,128]{2,1,0:T(8,128)}), f32[64,24,128]{2,1,0:T(8,128)S(1)}, u32[]{:S(2)}, u32[]{:S(2)}) async-start(f32[64,24,128]{2,1,0:T(8,128)} %shard_map.31), calls=%async_computation.2 | async-start | bytes 1572864 | tf_op jit(solution)/shard_map/all_to_all | solution.py:261
  87.0 0.1 copy.3.refs_0_
  87.1 5.3 %shard_map.30 = (f32[384,256]{1,0:T(8,128)S(1)}, f32[256,256]{1,0:T(8,128)S(1)}) custom-call(s32[4,1]{1,0:T(4,128)S(1)} %copy.3.refs_0_, f32[64,24,128]{2,1,0:T(8,128)S(1)} %all-to-all-done.1.refs_1_.refs_0_), custom_call_target="tpu_custom_call" | custom-call | flops 1000000 | bytes 1024 | tf_op jit(solution)/shard_map/pallas_call | solution.py:231
  92.4 0.0 collective-permute-start.4
  92.4 2.7 %convolution_bitcast_fusion = f32[1024,128]{0,1:T(8,128)} fusion(f32[1024,256]{1,0:T(8,128)} %param.2, f32[384,256]{1,0:T(8,128)S(1)} %get-tuple-element.19.refs_2_.refs_1_.refs_0_), kind=kOutput, calls=%fused_computation.3 | convolution fusion | flops 201326592 | bytes 1703936 | tf_op jit(solution)/shard_map/dot_general | solution.py:17
  95.1 0.6 collective-permute-start.2
  95.7 5.1 %collective-permute-done.4.refs_4_.refs_2_.refs_0_ = f32[384,256]{1,0:T(8,128)S(1)} collective-permute-done((f32[384,256]{1,0:T(8,128)S(1)}, f32[384,256]{1,0:T(8,128)S(1)}, u32[]{:S(2)}, u32[]{:S(2)}) %collective-permute-start.4) | collective-permute-done | bytes 393248 | tf_op jit(solution)/shard_map/ppermute | solution.py:250
  100.8 9.6 %all-to-all-done.2.refs_1_.refs_0_ = f32[64,24,128]{2,1,0:T(8,128)S(1)} async-done(((f32[64,24,128]{2,1,0:T(8,128)}), f32[64,24,128]{2,1,0:T(8,128)S(1)}, u32[]{:S(2)}, u32[]{:S(2)}) %all-to-all-start.2) | async-done | bytes 786464 | tf_op jit(solution)/shard_map/all_to_all | solution.py:261
  110.4 5.5 %shard_map.32 = (f32[768,256]{1,0:T(8,128)S(1)}, f32[256,256]{1,0:T(8,128)S(1)}, f32[256,256]{1,0:T(8,128)S(1)}) custom-call(s32[4,1]{1,0:T(4,128)S(1)} %copy.3.refs_0_, f32[64,24,128]{2,1,0:T(8,128)S(1)} %all-to-all-done.2.refs_1_.refs_0_, f32[384,256]{1,0:T(8,128)S(1)} %get-tuple-element.19.refs_2_.refs_1_.refs_0_, ...), custom_call_target="tpu_custom_call" | custom-call | flops 1000000 | bytes 1024 | tf_op jit(solution)/shard_map/pallas_call | solution.py:231
  115.9 0.7 copy-done.1
  116.6 0.7 copy-done.3
  117.3 0.0 collective-permute-start.6
  117.3 1.9 %convolution_bitcast_fusion.1 = f32[1024,128]{0,1:T(8,128)S(1)} fusion(f32[1024,256]{1,0:T(8,128)} %param.2, f32[384,256]{1,0:T(8,128)S(1)} %get-tuple-element.19.refs_2_.refs_1_.refs_0_), kind=kOutput, calls=%fused_computation.4 | convolution fusion | flops 201326592 | bytes 1703936 | tf_op jit(solution)/shard_map/dot_general | solution.py:17
  119.2 0.0 collective-permute-done.2
  119.2 3.0 %fusion.7 = f32[1024,128]{1,0:T(8,128)} fusion(f32[1024,128]{0,1:T(8,128)} %collective-permute-done.2, f32[1024,128]{0,1:T(8,128)S(1)} %convolution_bitcast_fusion.1, f32[768,256]{1,0:T(8,128)S(1)} %get-tuple-element.21.refs_3_.refs_1_), kind=kOutput, calls=%fused_computation.14 | convolution fusion | flops 201588736 | bytes 1703936 | tf_op jit(solution)/shard_map/dot_general | solution.py:17
  122.2 0.4 collective-permute-start.5
  122.7 0.1 shard_map.36
  122.7 0.7 copy-done
  123.5 5.7 %all-to-all-start.3 = ((f32[64,8,128]{2,1,0:T(8,128)}), f32[64,8,128]{2,1,0:T(8,128)S(1)}, u32[]{:S(2)}, u32[]{:S(2)}) async-start(f32[64,8,128]{2,1,0:T(8,128)} %copy-done), calls=%async_computation.3 | async-start | bytes 524288 | tf_op jit(solution)/shard_map/all_to_all | solution.py:261
  129.2 0.7 collective-permute-done.6.refs_4_.refs_1_.refs_2_
  129.9 0.9 copy-done.2
  130.8 0.9 copy-done.4
  131.8 2.0 %shard_map.33 = (f32[768,128]{1,0:T(8,128)S(1)}, f32[256,128]{1,0:T(8,128)S(1)}, f32[256,256]{1,0:T(8,128)S(1)}) custom-call(f32[64,24,128]{2,1,0:T(8,128)S(1)} %all-to-all-done.2.refs_1_.refs_0_, f32[384,256]{1,0:T(8,128)S(1)} %get-tuple-element.19.refs_2_.refs_1_.refs_0_, f32[384,256]{1,0:T(8,128)S(1)} %collective-permute-done.4.refs_4_.refs_2_.refs_0_, ...), custom_call_target="tpu_custom_call" | custom-call | flops 1000000 | bytes 1024 | tf_op jit(solution)/shard_map/pallas_call | solution.py:231
  133.8 0.0 collective-permute-start.7
  133.9 2.1 %fusion.8 = f32[1024,128]{1,0:T(8,128)S(1)} fusion(f32[1024,128]{0,1:T(8,128)} %collective-permute-done.2, f32[1024,128]{0,1:T(8,128)S(1)} %copy-done.8, f32[768,256]{1,0:T(8,128)S(1)} %get-tuple-element.21.refs_3_.refs_1_), kind=kOutput, calls=%fused_computation.15 | convolution fusion | flops 201588736 | bytes 1703936 | tf_op jit(solution)/shard_map/dot_general | solution.py:17
  135.9 5.3 %shard_map.34 = (f32[384,128]{1,0:T(8,128)S(1)}, f32[256,256]{1,0:T(8,128)S(1)}, f32[256,256]{1,0:T(8,128)S(1)}) custom-call(s32[4,1]{1,0:T(4,128)S(1)} %copy.3.refs_0_, f32[256,256]{1,0:T(8,128)S(1)} %get-tuple-element.24.refs_1_), custom_call_target="tpu_custom_call" | custom-call | flops 1000000 | bytes 1024 | tf_op jit(solution)/shard_map/pallas_call | solution.py:231
  141.2 0.9 collective-permute-start.8
  142.1 0.0 collective-permute-done.5
  142.1 2.5 %fusion.1 = f32[1024,128]{0,1:T(8,128)} fusion(f32[1024,128]{1,0:T(8,128)} %collective-permute-done.5, f32[1024,128]{1,0:T(8,128)S(1)} %fusion.8, f32[256,256]{1,0:T(8,128)S(1)} %get-tuple-element.25.refs_4_), kind=kOutput, calls=%fused_computation.6 | convolution fusion | flops 201588736 | bytes 1703936 | tf_op jit(solution)/shard_map/dot_general | solution.py:17
  144.6 2.9 %collective-permute-done.8.refs_3_.refs_6_ = f32[384,128]{1,0:T(8,128)S(1)} collective-permute-done((f32[384,128]{1,0:T(8,128)S(1)}, f32[384,128]{1,0:T(8,128)S(1)}, u32[]{:S(2)}, u32[]{:S(2)}) %collective-permute-start.8) | collective-permute-done | bytes 196640 | tf_op jit(solution)/shard_map/ppermute | solution.py:250
  147.5 0.0 collective-permute-done.7.refs_2_.refs_5_
  147.5 1.0 shard_map.35
  148.5 1.9 %fusion.12 = f32[128,1024]{1,0:T(8,128)S(1)} fusion(f32[1024,256]{1,0:T(8,128)} %collective-permute-done.1, f32[768,128]{1,0:T(8,128)S(1)} %shard_map.35), kind=kOutput, calls=%fused_computation.19 | convolution fusion | flops 201326592 | bytes 1703936 | tf_op jit(solution)/shard_map/dot_general | solution.py:17
  150.4 0.0 copy-start.10
  150.4 1.5 shard_map.37
  151.9 0.7 convolution_add_fusion.1
  152.7 0.5 copy-done.12
  153.2 0.7 fusion
  153.9 4.9 %shard_map.38 = f32[256,256]{1,0:T(8,128)S(1)} custom-call(s32[4,1]{1,0:T(4,128)S(1)} %copy.3.refs_0_, f32[64,8,128]{2,1,0:T(8,128)S(1)} %all-to-all-done.3.refs_1_, f32[128,128]{1,0:T(8,128)S(1)} %get-tuple-element.29.refs_2_, f32[256,128]{1,0:T(8,128)S(1)} %get-tuple-element.30.refs_3_, f32[256,128]{1,0:T(8,128)S(1)} %get-tuple-element.31.refs_4_, ...), custom_call_target="tpu_custom_call" | custom-call | flops 1000000 | bytes 1024 | tf_op jit(solution)/shard_map/pallas_call | solution.py:231
  158.8 0.4 fusion.5
  159.3 0.0 collective-permute-start.9
  159.3 0.4 fusion.6
  159.7 9.4 %collective-permute-done.9 = f32[1024,128]{0,1:T(8,128)S(1)} collective-permute-done((f32[1024,128]{0,1:T(8,128)S(1)}, f32[1024,128]{0,1:T(8,128)S(1)}, u32[]{:S(2)}, u32[]{:S(2)}) %collective-permute-start.9) | collective-permute-done | bytes 524320 | tf_op jit(solution)/shard_map/ppermute | solution.py:250
  169.1 0.1 pad_maximum_fusion.2
  169.2 1.3 copy.8
  (20 shorter events, 0.0 us)
Async XLA Ops:
  0.0 24.4 %collective-permute-start = (f32[1024,256]{1,0:T(8,128)}, f32[1024,256]{1,0:T(8,128)S(1)}, u32[]{:S(2)}, u32[]{:S(2)}) collective-permute-start(f32[1024,256]{1,0:T(8,128)} %param.2), channel_id=1, source_target_pairs={{7,0},{0,1},{1,2},{2,3},{3,4},{4,5},{5,6},{6,7},{15,8},{8,9},{9,10... | collective-permute-start | bytes 3145736 | tf_op jit(solution)/shard_map/ppermute | solution.py:250
  0.0 29.5 %collective-permute-start.1 = (f32[1024,256]{1,0:T(8,128)}, f32[1024,256]{1,0:T(8,128)}, u32[]{:S(2)}, u32[]{:S(2)}) collective-permute-start(f32[1024,256]{1,0:T(8,128)} %param.2), channel_id=1, source_target_pairs={{6,0},{7,1},{0,2},{1,3},{2,4},{3,5},{4,6},{5,7},{14,8},{15,9},{8,1... | collective-permute-start | bytes 3145736 | tf_op jit(solution)/shard_map/ppermute | solution.py:250
  3.4 21.0 %copy-start.5 = (f32[1024,256]{1,0:T(8,128)S(1)}, f32[1024,256]{1,0:T(8,128)}, u32[]{:S(2)}) copy-start(f32[1024,256]{1,0:T(8,128)} %param.2) | copy-start | bytes 3145732
  6.8 31.8 %all-to-all-start = ((f32[64,8,128]{2,1,0:T(8,128)}), f32[64,8,128]{2,1,0:T(8,128)S(1)}, u32[]{:S(2)}, u32[]{:S(2)}) async-start(f32[64,8,128]{2,1,0:T(8,128)} %shard_map.28), calls=%async_computation | async-start | bytes 524288 | tf_op jit(solution)/shard_map/all_to_all | solution.py:261
  24.4 1.1 copy-start.9
  39.6 33.6 %all-to-all-start.1 = ((f32[64,24,128]{2,1,0:T(8,128)}), f32[64,24,128]{2,1,0:T(8,128)S(1)}, u32[]{:S(2)}, u32[]{:S(2)}) async-start(f32[64,24,128]{2,1,0:T(8,128)} %shard_map.29), calls=%async_computation.1 | async-start | bytes 1572864 | tf_op jit(solution)/shard_map/all_to_all | solution.py:261
  49.3 21.8 %collective-permute-start.3 = (f32[1024,256]{1,0:T(8,128)}, f32[1024,256]{1,0:T(8,128)S(1)}, u32[]{:S(2)}, u32[]{:S(2)}) collective-permute-start(f32[1024,256]{1,0:T(8,128)} %collective-permute-done.1), channel_id=1, source_target_pairs={{7,0},{0,1},{1,2},{2,3},{3,4},{4,5},{5,6},{6,7},{15,8},{8,9},{9,10... | collective-permute-start | bytes 3145736 | tf_op jit(solution)/shard_map/ppermute | solution.py:250
  71.2 1.0 copy-start.11
  74.2 12.8 %copy-start.13 = (s32[4,1]{0,1:T(1,128)S(1)}, s32[4,1]{0,1:T(1,128)}, u32[]{:S(2)}) copy-start(s32[4,1]{0,1:T(1,128)} %param.3) | copy-start | bytes 52
  74.2 36.2 %all-to-all-start.2 = ((f32[64,24,128]{2,1,0:T(8,128)}), f32[64,24,128]{2,1,0:T(8,128)S(1)}, u32[]{:S(2)}, u32[]{:S(2)}) async-start(f32[64,24,128]{2,1,0:T(8,128)} %shard_map.31), calls=%async_computation.2 | async-start | bytes 1572864 | tf_op jit(solution)/shard_map/all_to_all | solution.py:261
  92.4 8.4 %collective-permute-start.4 = (f32[384,256]{1,0:T(8,128)S(1)}, f32[384,256]{1,0:T(8,128)S(1)}, u32[]{:S(2)}, u32[]{:S(2)}) collective-permute-start(f32[384,256]{1,0:T(8,128)S(1)} %get-tuple-element.19.refs_2_.refs_1_.refs_0_), channel_id=1, source_target_pairs={{7,0},{0,1},{1,2},{2,3},{3,4},{4,5},{5,6},{6,7},{15,8},{8,9},{9,10... | collective-permute-start | bytes 1179656 | tf_op jit(solution)/shard_map/ppermute | solution.py:250
  95.1 24.1 %collective-permute-start.2 = (f32[1024,128]{0,1:T(8,128)}, f32[1024,128]{0,1:T(8,128)}, u32[]{:S(2)}, u32[]{:S(2)}) collective-permute-start(f32[1024,128]{0,1:T(8,128)} %convolution_bitcast_fusion), channel_id=1, source_target_pairs={{7,0},{0,1},{1,2},{2,3},{3,4},{4,5},{5,6},{6,7},{15,8},{8,9},{9,10... | collective-permute-start | bytes 1572872 | tf_op jit(solution)/shard_map/ppermute | solution.py:250
  115.9 0.7 copy-start.1
  116.6 0.7 copy-start.3
  117.3 12.6 %collective-permute-start.6 = (f32[768,256]{1,0:T(8,128)S(1)}, f32[768,256]{1,0:T(8,128)S(1)}, u32[]{:S(2)}, u32[]{:S(2)}) collective-permute-start(f32[768,256]{1,0:T(8,128)S(1)} %get-tuple-element.21.refs_3_.refs_1_), channel_id=1, source_target_pairs={{7,0},{0,1},{1,2},{2,3},{3,4},{4,5},{5,6},{6,7},{15,8},{8,9},{9,10... | collective-permute-start | bytes 2359304 | tf_op jit(solution)/shard_map/ppermute | solution.py:250
  119.2 3.1 %copy-start.7 = (f32[1024,128]{0,1:T(8,128)}, f32[1024,128]{0,1:T(8,128)S(1)}, u32[]{:S(2)}) copy-start(f32[1024,128]{0,1:T(8,128)S(1)} %convolution_bitcast_fusion.1) | copy-start | bytes 1572868
  122.2 19.9 %collective-permute-start.5 = (f32[1024,128]{1,0:T(8,128)}, f32[1024,128]{1,0:T(8,128)}, u32[]{:S(2)}, u32[]{:S(2)}) collective-permute-start(f32[1024,128]{1,0:T(8,128)} %fusion.7), channel_id=1, source_target_pairs={{7,0},{0,1},{1,2},{2,3},{3,4},{4,5},{5,6},{6,7},{15,8},{8,9},{9,10... | collective-permute-start | bytes 1572872 | tf_op jit(solution)/shard_map/ppermute | solution.py:250
  122.7 0.7 copy-start
  123.5 30.4 %all-to-all-start.3 = ((f32[64,8,128]{2,1,0:T(8,128)}), f32[64,8,128]{2,1,0:T(8,128)S(1)}, u32[]{:S(2)}, u32[]{:S(2)}) async-start(f32[64,8,128]{2,1,0:T(8,128)} %copy-done), calls=%async_computation.3 | async-start | bytes 524288 | tf_op jit(solution)/shard_map/all_to_all | solution.py:261
  129.9 1.0 copy-start.2
  130.8 0.9 copy-start.4
  131.8 2.1 %copy-start.8 = (f32[1024,128]{0,1:T(8,128)S(1)}, f32[1024,128]{0,1:T(8,128)}, u32[]{:S(2)}) copy-start(f32[1024,128]{0,1:T(8,128)} %copy-done.7) | copy-start | bytes 1572868
  133.8 13.7 %collective-permute-start.7 = (f32[768,128]{1,0:T(8,128)S(1)}, f32[768,128]{1,0:T(8,128)S(1)}, u32[]{:S(2)}, u32[]{:S(2)}) collective-permute-start(f32[768,128]{1,0:T(8,128)S(1)} %get-tuple-element.26), channel_id=1, source_target_pairs={{7,0},{0,1},{1,2},{2,3},{3,4},{4,5},{5,6},{6,7},{15,8},{8,9},{9,10... | collective-permute-start | bytes 1179656 | tf_op jit(solution)/shard_map/ppermute | solution.py:250
  141.2 6.3 %collective-permute-start.8 = (f32[384,128]{1,0:T(8,128)S(1)}, f32[384,128]{1,0:T(8,128)S(1)}, u32[]{:S(2)}, u32[]{:S(2)}) collective-permute-start(f32[384,128]{1,0:T(8,128)S(1)} %get-tuple-element.27), channel_id=1, source_target_pairs={{7,0},{0,1},{1,2},{2,3},{3,4},{4,5},{5,6},{6,7},{15,8},{8,9},{9,10... | collective-permute-start | bytes 589832 | tf_op jit(solution)/shard_map/ppermute | solution.py:250
  150.4 1.5 copy-start.10
  151.9 1.2 copy-start.12
  153.9 4.9 %copy-start.6 = (f32[1024,128]{0,1:T(8,128)S(1)}, f32[1024,128]{0,1:T(8,128)}, u32[]{:S(2)}) copy-start(f32[1024,128]{0,1:T(8,128)} %fusion.1) | copy-start | bytes 1572868
  159.3 9.8 %collective-permute-start.9 = (f32[1024,128]{0,1:T(8,128)S(1)}, f32[1024,128]{0,1:T(8,128)S(1)}, u32[]{:S(2)}, u32[]{:S(2)}) collective-permute-start(f32[1024,128]{0,1:T(8,128)S(1)} %fusion.5), channel_id=1, source_target_pairs={{7,0},{0,1},{1,2},{2,3},{3,4},{4,5},{5,6},{6,7},{15,8},{8,9},{9,10... | collective-permute-start | bytes 1572872 | tf_op jit(solution)/shard_map/ppermute | solution.py:250
where the time goes:
time: 171 us
  starting transfers between devices  58.3 us (34%)
  waiting for transfers between devices  53.3 us (31%)
  Pallas kernels  28.2 us (16%)
  matrix products  23.4 us (14%)
  local copies, waits for them, and re-layouts  6.89 us (4%)
    all_to_all x4, starting transfers between devices, exchange(): return lax.all_to_all(pieces, 'row', 0, 0, tiled=True)  44.9 us
    ppermute x10, waiting for transfers between devices, onward(): lax.ppermute(values, 'blk', [((i - places) % devices, i) for i in range(d...  36.9 us
    pallas_call x11, Pallas kernels, run(): pl.pallas_call(body, out_shape=[jax.ShapeDtypeStruct(shape, jnp.float32)...  28.2 us
    dot_general x14, matrix products, dot(): lax.dot_general(left, right, (((over[0],), (over[1],)), ((), ())), precis...  23.4 us
    all_to_all x4, waiting for transfers between devices, exchange(): return lax.all_to_all(pieces, 'row', 0, 0, tiled=True)  16.4 us
    ppermute x10, starting transfers between devices, onward(): lax.ppermute(values, 'blk', [((i - places) % devices, i) for i in range(d...  13.3 us
    unnamed x29, local copies, waits for them, and re-layouts  5.57 us
  transfers between devices with their start and end apart: 14, of which 9 were waited for; matrix products, arithmetic and copies ran while one was open for 14% of the time, Pallas kernels for 12%

commit v1 on v0

--- a/solution.py
+++ b/solution.py
@@ -1,3 +1,5 @@
+import functools
+
 import jax
 import jax.numpy as jnp
 from jax import lax
@@ -21,6 +23,18 @@
         precision=precision,
         preferred_element_type=jnp.float32,
     )
+
+
+def halved(values):
+    high = values.astype(jnp.bfloat16)
+    return high, (values - high.astype(jnp.float32)).astype(jnp.bfloat16)
+
+
+def cross_dot(left, right, over=(1, 0)):
+    numbers = (((over[0],), (over[1],)), ((), ()))
+    (a, b), (c, d) = halved(left), halved(right)
+    passes = [lax.dot_general(x, y, numbers, preferred_element_type=jnp.float32) for x, y in ((a, d), (b, c), (a, c))]
+    return passes[0] + passes[1] + passes[2]
 
 
 def seats(position, round_index):
@@ -65,8 +79,9 @@
     y = jnp.where(difference >= 0.0, 2.0 * coupling, -2.0 * coupling)
     largest = jnp.maximum(x, jnp.abs(y))
     scale = jnp.where(largest > 0.0, largest, 1.0)
-    x = jnp.where(largest > 0.0, x / scale, 1.0)
-    y = y / scale
+    inverse = 1.0 / scale
+    x = jnp.where(largest > 0.0, x * inverse, 1.0)
+    y = y * inverse
     tangent = y / (x + jnp.sqrt(x * x + y * y))
     cosine = 1.0 / jnp.sqrt(1.0 + tangent * tangent)
     sine = tangent * cosine
@@ -151,78 +166,121 @@
 
 
 def step0_kernel(second, received, out, h0, *parts):
-    q0, h0[...] = jacobi(square_of(received, 0), 0, second[0, 0], parts)
+    q0, rotated_gram = jacobi(square_of(received, 0), 0, second[0, 0], parts)
+    h0[...] = rotated_gram[:HALF, :HALF]
     out[:N] = q0
-    out[N:] = h0[HALF:]
-
-
-def step1_kernel(second, received, out0, h0, in0, out, h1, r1, *parts):
-    q0, q0_p = out0[:N], in0[:N]
-    r1[...] = dot(dot(q0, square_of(received, 0), (0, 0)), q0_p)
-    gram = joined(h0[:HALF, :HALF], r1[:HALF, HALF:], in0[N:, HALF:])
-    q1, h1[...] = jacobi(gram, ROUNDS, second[1, 0], parts)
+    out[N:] = rotated_gram[HALF:]
+
+
+def step1_kernel(second, received, out0, h0, in0, out, carried, *parts):
+    r1 = cross_dot(cross_dot(out0[:N], square_of(received, 1), (0, 0)), in0[:N])
+    out[N:, HALF:] = r1[HALF:, HALF:]
+    carried[:, HALF:] = r1[:, :HALF]
+    gram = joined(h0[...], r1[:HALF, HALF:], in0[N:, HALF:])
+    q1, h1 = jacobi(gram, ROUNDS, second[1, 0], parts)
     out[:N] = q1
-    out[N : N + HALF] = h1[HALF:]
-    out[N + HALF : 2 * N] = r1[HALF:]
-    out[2 * N :] = q0_p
-
-
-def cross2_kernel(received, out0, in0, out1, in1, h1, r1, out, kept, gram):
-    q0, q0_pp = out0[:N], in1[2 * N :]
-    r2 = dot(dot(q0, square_of(received, 1), (0, 0)), q0_pp)
-    q1, q1_p = out1[:N], in1[:N]
-    upper = jnp.concatenate([r1[:HALF, :HALF], r2[:HALF, HALF:]], axis=1)
-    lower = jnp.concatenate([in0[N:, :HALF], in1[N + HALF : 2 * N, HALF:]], axis=1)
-    s1 = dot(dot(q1, jnp.concatenate([upper, lower], axis=0), (0, 0)), q1_p)
-    gram[...] = joined(h1[:HALF, :HALF], s1[:HALF, HALF:], in1[N : N + HALF, HALF:])
+    out[N:, :HALF] = h1[HALF:, HALF:]
+    carried[:, :HALF] = h1[:, :HALF]
+
+
+def cross2_kernel(received, out0, in0, q0_pp, out1, in1, carried, out, kept, gram):
+    r2 = cross_dot(cross_dot(out0[:N], square_of(received, 0), (0, 0)), q0_pp[:N])
+    upper = jnp.concatenate([carried[:HALF, HALF:], r2[:HALF, HALF:]], axis=1)
+    lower = jnp.concatenate([in0[N:, :HALF], in1[N:, HALF:]], axis=1)
+    s1 = cross_dot(cross_dot(out1[:N], jnp.concatenate([upper, lower], axis=0), (0, 0)), in1[:N])
+    gram[...] = joined(carried[:HALF, :HALF], s1[:HALF, HALF:], in1[N:, :HALF])
     out[:HALF] = s1[HALF:, HALF:]
     out[HALF:N] = r2[HALF:, HALF:]
-    out[N : 2 * N] = q1_p[:, HALF:]
-    out[2 * N :] = q0_pp[:, HALF:]
+    out[N : N + HALF] = carried[HALF:, :HALF]
+    out[N + HALF : 2 * N] = carried[HALF:, HALF:]
+    out[2 * N : 3 * N] = in1[:N, HALF:]
+    out[3 * N :] = q0_pp[:N, HALF:]
     kept[:HALF] = s1[:HALF, :HALF]
     kept[HALF:] = r2[:HALF, :HALF]
 
 
-def step2_kernel(second, gram, out, q2, h2, *parts):
-    q2[...], h2[...] = jacobi(gram[...], 2 * ROUNDS, second[2, 0], parts)
+def step2_kernel(second, gram, out, own, *parts):
+    q2, h2 = jacobi(gram[...], 2 * ROUNDS, second[2, 0], parts)
     out[:N] = q2[:, HALF:]
     out[N:] = h2[HALF:, HALF:]
-
-
-def cross3_kernel(out0, out1, in1, kept, q2, in2a, in2b, cross, left, right):
-    q0_k, q1_k, q2_k = out0[:N, :HALF], out1[:N, :HALF], q2[:, :HALF]
-    q2_p, q1_pp, q0_ppp = in2b[:N], in2a[N : 2 * N], in2a[2 * N :]
+    own[:N] = q2[:, :HALF]
+    own[N:] = h2[:HALF, :HALF]
+
+
+def cross3_kernel(out0, out1, kept, own2, in2a, in2b, cross, left, right):
+    q0_k, q1_k, q2_k = out0[:N, :HALF], out1[:N, :HALF], own2[:N]
+    q2_p, q1_pp, q0_ppp = in2b[:N], in2a[2 * N : 3 * N], in2a[3 * N :]
     upper = jnp.concatenate([kept[HALF:], jnp.zeros((HALF, HALF), jnp.float32)], axis=1)
-    lower = jnp.concatenate([in1[N + HALF : 2 * N, :HALF], in2a[HALF:N]], axis=1)
-    t = dot(dot(q1_k, jnp.concatenate([upper, lower], axis=0), (0, 0)), q1_pp)
+    lower = jnp.concatenate([in2a[N + HALF : 2 * N], in2a[HALF:N]], axis=1)
+    t = cross_dot(cross_dot(q1_k, jnp.concatenate([upper, lower], axis=0), (0, 0)), q1_pp)
     upper = jnp.concatenate([kept[:HALF], t], axis=1)
-    lower = jnp.concatenate([in1[N : N + HALF, :HALF], in2a[:HALF]], axis=1)
-    cross[...] = dot(dot(q2_k, jnp.concatenate([upper, lower], axis=0), (0, 0)), q2_p)
-    left[...] = dot(q0_k, dot(q1_k[:HALF], q2_k[:HALF]))
-    right[...] = dot(q0_ppp, dot(q1_pp[HALF:], q2_p[HALF:]))
-
-
-def weights_kernel(in0, in1, in2a, in2b, out):
-    q2_k, q2_m = in2b[:HALF], in2b[HALF:N]
-    q1_pp, q0_pp = in2a[N : 2 * N], in1[2 * N :]
-    out[:N] = dot(in0[:N, :HALF], dot(in1[:HALF, :HALF], q2_k))
-    travelled = dot(q0_pp[:, HALF:], dot(in1[HALF:N, :HALF], q2_k))
-    out[N : 2 * N] = travelled + dot(q0_pp[:, :HALF], dot(q1_pp[:HALF], q2_m))
-    out[2 * N :] = dot(in2a[2 * N :], dot(q1_pp[HALF:], q2_m))
-
-
-def step3_kernel(second, received, cross, left, right, h2, in2b, q3, *parts):
-    total = cross[...] + dot(left[...], dot(square_of(received, 0), right[...]), (0, 0))
-    gram = joined(h2[:HALF, :HALF], total, in2b[N:])
+    lower = jnp.concatenate([in2a[N : N + HALF], in2a[:HALF]], axis=1)
+    cross[...] = cross_dot(cross_dot(q2_k, jnp.concatenate([upper, lower], axis=0), (0, 0)), q2_p)
+    left[...] = cross_dot(q0_k, cross_dot(q1_k[:HALF], q2_k[:HALF]))
+    right[...] = cross_dot(q0_ppp, cross_dot(q1_pp[HALF:], q2_p[HALF:]))
+
+
+def weights_kernel(out0, in0, q0_pp, out1, in1, in2a, own2, own, before):
+    q2_k, q2_m = own2[:HALF], own2[HALF:N]
+    q1_kk, q1_mk, p1_kk, p1_mk = out1[:HALF, :HALF], out1[HALF:N, :HALF], in1[:HALF, :HALF], in1[HALF:N, :HALF]
+    p1_km, p1_mm = in1[:HALF, HALF:], in1[HALF:N, HALF:]
+    own[:N] = cross_dot(out0[:N, :HALF], cross_dot(q1_kk, q2_k))
+    travelled = cross_dot(in0[:N, HALF:], cross_dot(q1_mk, q2_k))
+    own[N : 2 * N] = travelled + cross_dot(in0[:N, :HALF], cross_dot(p1_km, q2_m))
+    own[2 * N :] = cross_dot(q0_pp[:N, HALF:], cross_dot(p1_mm, q2_m))
+    before[:N] = cross_dot(in0[:N, :HALF], p1_kk)
+    before[N : 2 * N] = cross_dot(q0_pp[:N, HALF:], p1_mk)
+    before[2 * N : 3 * N] = cross_dot(q0_pp[:N, :HALF], in2a[2 * N : 2 * N + HALF])
+    before[3 * N :] = cross_dot(in2a[3 * N :], in2a[2 * N + HALF : 3 * N])
+
+
+def products_kernel(left, right, out):
+    step = min(N, left.shape[0])
+    out[...] = jnp.zeros(out.shape, jnp.float32)
+
+    def some_rows(number, carry):
+        rows = pl.ds(pl.multiple_of(number * step, step), step)
+        out[...] += cross_dot(left[rows, :], right[rows, :], (0, 0))
+        return carry
+
+    lax.fori_loop(0, left.shape[0] // step, some_rows, 0)
+
+
+def columns_kernel(x0, x1, x2, x3, own, before, kept, left, right):
+    step = min(N, kept.shape[0])
+
+    def some_rows(number, carry):
+        rows = pl.ds(pl.multiple_of(number * step, step), step)
+        first, second, third, fourth = x0[rows, :], x1[rows, :], x2[rows, :], x3[rows, :]
+        kept[rows, :] = cross_dot(first, own[:N]) + cross_dot(second, own[N : 2 * N]) + cross_dot(third, own[2 * N :])
+        left[rows, :] = cross_dot(second, before[:N]) + cross_dot(third, before[N : 2 * N])
+        right[rows, :] = cross_dot(third, before[2 * N : 3 * N]) + cross_dot(fourth, before[3 * N :])
+        return carry
+
+    lax.fori_loop(0, kept.shape[0] // step, some_rows, 0)
+
+
+def last_kernel(place, pair_cols, rotation, out):
+    out[...] = cross_dot(pair_cols[...], rotation[:, place : place + HALF])
+
+
+def pair_kernel(kept, left, right, in2b, out):
+    out[:, :HALF] = kept[...]
+    out[:, HALF:] = cross_dot(left[...], in2b[:HALF]) + cross_dot(right[...], in2b[HALF:N])
+
+
+def step3_kernel(second, received, cross, left, right, own2, in2b, q3, *parts):
+    total = cross[...] + cross_dot(left[...], cross_dot(square_of(received, 0), right[...]), (0, 0))
+    gram = joined(own2[N:], total, in2b[N:])
     q3[...], _ = jacobi(gram, 3 * ROUNDS, second[3, 0], parts)
 
 
 JACOBI_PARTS = [pltpu.VMEM((HALF, HALF), jnp.float32)] * 4 + [pltpu.VMEM((N, HALF), jnp.float32)] * 2
 
 
-def run(kernel, shapes, *operands, solves=True, last=()):
-    vmem, smem = pl.BlockSpec(memory_space=pltpu.VMEM), pl.BlockSpec(memory_space=pltpu.SMEM)
-    specs = [smem if x.dtype == jnp.int32 else vmem for x in operands] + [pl.BlockSpec(memory_space=pl.ANY)] * len(last)
+def run(kernel, shapes, *operands, solves=True, last=(), vmem=8):
+    whole, smem = pl.BlockSpec(memory_space=pltpu.VMEM), pl.BlockSpec(memory_space=pltpu.SMEM)
+    specs = [smem if x.dtype == jnp.int32 else whole for x in operands] + [pl.BlockSpec(memory_space=pl.ANY)] * len(last)
 
     def body(*refs):
         given = len(operands)
@@ -232,22 +290,21 @@
         body,
         out_shape=[jax.ShapeDtypeStruct(shape, jnp.float32) for shape in shapes],
         in_specs=specs,
-        out_specs=[vmem] * len(shapes),
+        out_specs=[whole] * len(shapes),
         scratch_shapes=JACOBI_PARTS if solves else [],
-        compiler_params=pltpu.CompilerParams(vmem_limit_bytes=16 * 2**20),
+        compiler_params=pltpu.CompilerParams(vmem_limit_bytes=vmem * 2**20),
         cost_estimate=pl.CostEstimate(flops=10**6, bytes_accessed=2**10, transcendentals=0),
     )(*operands, *last)
 
 
-def product(left, right, over=(1, 0)):
-    return dot(left, right, over, lax.Precision.HIGH)
-
-
 def shards(matrix, sender_slot):
     devices, count = lax.axis_size("blk"), lax.axis_size("row")
 
     def onward(values, places=1):
         return lax.ppermute(values, "blk", [((i - places) % devices, i) for i in range(devices)])
+
+    def products(other):
+        return run(products_kernel, [(N, N)], matrix, other, solves=False)[0]
 
     def exchange(received, skipped, *blocks, last=()):
         height = TILES // count * 8
@@ -260,41 +317,50 @@
         (pieces,) = run(kernel, [(count, total, HALF)], *given, *blocks, solves=False, last=last)
         return lax.all_to_all(pieces, "row", 0, 0, tiled=True)
 
-    def rotated(pair_cols, rotation):
-        arrived = onward(product(pair_cols, rotation[:, HALF:]))
-        return jnp.concatenate([product(pair_cols, rotation[:, :HALF]), arrived], axis=1)
-
     square, block = (N, N), (HALF, HALF)
-    before1, before2 = onward(matrix), onward(matrix, 2)
-    received = exchange(None, 0, product(matrix, matrix, (0, 0)))
-    c1, c2 = product(matrix, before1, (0, 0)), product(matrix, before2, (0, 0))
-    with_gram = exchange(received, 0, c1, c2)
+    before1 = onward(matrix)
+    received = exchange(None, 0, products(matrix), products(before1))
+    before2 = onward(before1)
+    with_c1 = exchange(received, 0, products(before2))
     before3 = onward(before2)
-    c3 = product(matrix, before3, (0, 0))
-    with_c12 = exchange(with_gram, 1, c3)
-    out0, h0 = run(step0_kernel, [(N + HALF, N), square], sender_slot, with_gram)
+    with_c2 = exchange(with_c1, 2, products(before3))
+    out0, h0 = run(step0_kernel, [(N + HALF, N), block], sender_slot, with_c1)
     in0 = onward(out0)
-    pair_cols = rotated(matrix, out0[:N])
-    out1, h1, r1 = run(step1_kernel, [(3 * N, N), square, square], sender_slot, with_c12, out0, h0, in0)
+    q0_pp = onward(in0)
+    out1, carried = run(step1_kernel, [(N + HALF, N), square], sender_slot, with_c1, out0, h0, in0)
     in1 = onward(out1)
-    with_c3 = exchange(with_c12, 2, last=(out1,))
-    pair_cols = rotated(pair_cols, out1[:N])
+    with_c3 = exchange(with_c2, 1, last=(out1,))
     out2a, kept, gram2 = run(
-        cross2_kernel, [(3 * N, HALF), (N, HALF), square], with_c12, out0, in0, out1, in1, h1, r1, solves=False
+        cross2_kernel,
+        [(4 * N, HALF), (N, HALF), square],
+        *(with_c2, out0, in0, q0_pp, out1, in1, carried),
+        solves=False,
     )
     in2a = onward(out2a)
-    out2b, q2, h2 = run(step2_kernel, [(N + HALF, HALF), square, square], sender_slot, gram2)
+    out2b, own2 = run(step2_kernel, [(N + HALF, HALF), (N + HALF, HALF)], sender_slot, gram2)
     in2b = onward(out2b)
+    own, before = run(
+        weights_kernel, [(3 * N, HALF), (4 * N, HALF)], out0, in0, q0_pp, out1, in1, in2a, own2, solves=False
+    )
+    kept_cols, left_cols, right_cols = run(
+        columns_kernel, [(matrix.shape[0], HALF)] * 3, matrix, before1, before2, before3, own, before, solves=False, vmem=12
+    )
     cross, left, right = run(
-        cross3_kernel, [block, (N, HALF), (N, HALF)], out0, out1, in1, kept, q2, in2a, in2b, solves=False
-    )
-    (weights,) = run(weights_kernel, [(3 * N, HALF)], in0, in1, in2a, in2b, solves=False)
-    arrived = (
-        product(before1, weights[:N]) + product(before2, weights[N : 2 * N]) + product(before3, weights[2 * N :])
-    )
-    pair_cols = jnp.concatenate([product(pair_cols, q2[:, :HALF]), arrived], axis=1)
-    (q3,) = run(step3_kernel, [square], sender_slot, with_c3, cross, left, right, h2, in2b)
-    return rotated(pair_cols, q3)
+        cross3_kernel,
+        [block, (N, HALF), (N, HALF)],
+        *(out0, out1, kept, own2, in2a, in2b),
+        solves=False,
+        last=(kept_cols,),
+    )
+    (pair_cols,) = run(pair_kernel, [matrix.shape], kept_cols, left_cols, right_cols, in2b, solves=False)
+    (q3,) = run(step3_kernel, [square], sender_slot, with_c3, cross, left, right, own2, in2b, last=(pair_cols,))
+
+    def last_columns(place):
+        return run(functools.partial(last_kernel, place), [(matrix.shape[0], HALF)], pair_cols, q3, solves=False)[0]
+
+    arrived = onward(last_columns(HALF))
+    kept = last_columns(0)
+    return jnp.concatenate([kept, arrived], axis=1)
 
 
 def solution(mesh):

time: 171 us -> 175 us (1.023)
  waiting for transfers between devices: 53.3 us -> 79.9 us
  matrix products: 23.4 us -> 0 us
  starting transfers between devices: 58.3 us -> 42.5 us
  Pallas kernels: 28.2 us -> 37.5 us
  local copies, waits for them, and re-layouts: 6.89 us -> 13.1 us
    dot_general x14 -> x0, matrix products: 23.4 us -> none  [dot(): lax.dot_general(left, right, (((over[0],), (over[1],)), ((), ())), precis...]
    ppermute x10 -> x9, waiting for transfers between devices: 36.9 us -> 55.8 us  [onward(): lax.ppermute(values, 'blk', [((i - places) % devices, i) for i in range(d...]
    ppermute x10 -> x9, starting transfers between devices: 13.3 us -> 0.64 us  [onward(): lax.ppermute(values, 'blk', [((i - places) % devices, i) for i in range(d...]
    pallas_call x11 -> x19, Pallas kernels: 28.2 us -> 37.5 us  [run(): pl.pallas_call(body, out_shape=[jax.ShapeDtypeStruct(shape, jnp.float32)...]
    all_to_all x4, waiting for transfers between devices: 16.4 us -> 24.1 us  [exchange(): return lax.all_to_all(pieces, 'row', 0, 0, tiled=True)]
    unnamed x29 -> x45, local copies, waits for them, and re-layouts: 5.57 us -> 13.1 us
    all_to_all x4, starting transfers between devices: 44.9 us -> 41.8 us  [exchange(): return lax.all_to_all(pieces, 'row', 0, 0, tiled=True)]
  transfers between devices with their start and end apart: 14 -> 13, of which waited for: 9 -> 8; matrix products, arithmetic and copies ran while one was open for 14% -> 0% of each run, Pallas kernels for 12% -> 16%
where the time goes in v1:
time: 175 us; the launch traced here: 174 us
  waiting for transfers between devices  79.9 us (46%)
  starting transfers between devices  42.5 us (24%)
  Pallas kernels  37.5 us (21%)
  local copies, waits for them, and re-layouts  13.1 us (7%)
    ppermute x9, waiting for transfers between devices, onward(): lax.ppermute(values, 'blk', [((i - places) % devices, i) for i in range(d...  55.8 us
    all_to_all x4, starting transfers between devices, exchange(): return lax.all_to_all(pieces, 'row', 0, 0, tiled=True)  41.8 us
    pallas_call x19, Pallas kernels, run(): pl.pallas_call(body, out_shape=[jax.ShapeDtypeStruct(shape, jnp.float32)...  37.5 us
    all_to_all x4, waiting for transfers between devices, exchange(): return lax.all_to_all(pieces, 'row', 0, 0, tiled=True)  24.1 us
    unnamed x45, local copies, waits for them, and re-layouts  13.1 us
  transfers between devices with their start and end apart: 13, of which 8 were waited for; matrix products, arithmetic and copies ran while one was open for 0% of the time, Pallas kernels for 16%

profile of v1, /device:TPU:8, one launch (start us, length us, event | category | flops | bytes accessed | tf_op | source)
XLA Modules:
  0.0 174.3 jit_solution(3845858281623701895)
XLA Ops:
  0.0 0.0 collective-permute-start
  0.0 15.6 %collective-permute-done.refs_1_ = f32[1024,256]{1,0:T(8,128)S(1)} collective-permute-done((f32[1024,256]{1,0:T(8,128)}, f32[1024,256]{1,0:T(8,128)S(1)}, u32[]{:S(2)}, u32[]{:S(2)}) %collective-permute-start) | collective-permute-done | bytes 1048608 | tf_op jit(solution)/shard_map/ppermute | solution.py:304
  15.6 0.0 collective-permute-start.1
  15.7 1.6 copy-done
  17.3 1.3 shard_map.28.refs_0_
  18.6 1.3 shard_map.29.refs_1_
  19.9 0.0 copy-start.1
  20.0 0.8 copy-done.9
  20.7 16.8 %all-to-all-start = ((f32[64,16,128]{2,1,0:T(8,128)}), f32[64,16,128]{2,1,0:T(8,128)}, u32[]{:S(2)}, u32[]{:S(2)}) async-start(f32[64,16,128]{2,1,0:T(8,128)} %copy-done.9), calls=%async_computation | async-start | bytes 1048576 | tf_op jit(solution)/shard_map/all_to_all | solution.py:318
  37.5 0.0 collective-permute-done.1.refs_1_.refs_2_
  37.6 1.3 shard_map.31.refs_1_
  38.9 18.1 %all-to-all-done.refs_0_ = f32[64,16,128]{2,1,0:T(8,128)} async-done(((f32[64,16,128]{2,1,0:T(8,128)}), f32[64,16,128]{2,1,0:T(8,128)}, u32[]{:S(2)}, u32[]{:S(2)}) %all-to-all-start) | async-done | bytes 524320 | tf_op jit(solution)/shard_map/all_to_all | solution.py:318
  56.9 1.1 shard_map.32
  58.1 0.9 copy-done.8
  59.0 5.4 %all-to-all-start.1 = ((f32[64,24,128]{2,1,0:T(8,128)}), f32[64,24,128]{2,1,0:T(8,128)S(1)}, u32[]{:S(2)}, u32[]{:S(2)}) async-start(f32[64,24,128]{2,1,0:T(8,128)} %copy-done.8), calls=%async_computation.1 | async-start | bytes 1572864 | tf_op jit(solution)/shard_map/all_to_all | solution.py:318
  64.4 0.0 collective-permute-start.2
  64.4 15.4 %collective-permute-done.2.refs_1_.refs_3_ = f32[1024,256]{1,0:T(8,128)S(1)} collective-permute-done((f32[1024,256]{1,0:T(8,128)S(1)}, f32[1024,256]{1,0:T(8,128)S(1)}, u32[]{:S(2)}, u32[]{:S(2)}) %collective-permute-start.2) | collective-permute-done | bytes 1048608 | tf_op jit(solution)/shard_map/ppermute | solution.py:304
  79.9 1.3 shard_map.35.refs_1_
  81.2 1.0 copy-done.6
  82.2 6.1 %all-to-all-done.1.refs_1_.refs_0_ = f32[64,24,128]{2,1,0:T(8,128)S(1)} async-done(((f32[64,24,128]{2,1,0:T(8,128)}), f32[64,24,128]{2,1,0:T(8,128)S(1)}, u32[]{:S(2)}, u32[]{:S(2)}) %all-to-all-start.1) | async-done | bytes 786464 | tf_op jit(solution)/shard_map/all_to_all | solution.py:318
  88.2 0.9 shard_map.36
  89.1 6.8 %all-to-all-start.2 = ((f32[64,16,128]{2,1,0:T(8,128)}), f32[64,16,128]{2,1,0:T(8,128)S(1)}, u32[]{:S(2)}, u32[]{:S(2)}) async-start(f32[64,16,128]{2,1,0:T(8,128)} %shard_map.36), calls=%async_computation.2 | async-start | bytes 1048576 | tf_op jit(solution)/shard_map/all_to_all | solution.py:318
  95.9 0.1 copy.3.refs_0_
  96.0 5.3 %shard_map.33 = (f32[384,256]{1,0:T(8,128)S(1)}, f32[128,128]{1,0:T(8,128)S(1)}) custom-call(s32[4,1]{1,0:T(4,128)S(1)} %copy.3.refs_0_, f32[64,24,128]{2,1,0:T(8,128)S(1)} %all-to-all-done.1.refs_1_.refs_0_), custom_call_target="tpu_custom_call" | custom-call | flops 1000000 | bytes 1024 | tf_op jit(solution)/shard_map/pallas_call | solution.py:289
  101.3 0.0 collective-permute-start.3
  101.3 8.4 %collective-permute-done.3.refs_4_.refs_2_.refs_1_ = f32[384,256]{1,0:T(8,128)S(1)} collective-permute-done((f32[384,256]{1,0:T(8,128)S(1)}, f32[384,256]{1,0:T(8,128)S(1)}, u32[]{:S(2)}, u32[]{:S(2)}) %collective-permute-start.3) | collective-permute-done | bytes 393248 | tf_op jit(solution)/shard_map/ppermute | solution.py:304
  109.7 0.0 collective-permute-start.4
  109.7 5.4 %shard_map.34 = (f32[384,256]{1,0:T(8,128)S(1)}, f32[256,256]{1,0:T(8,128)S(1)}) custom-call(s32[4,1]{1,0:T(4,128)S(1)} %copy.3.refs_0_, f32[64,24,128]{2,1,0:T(8,128)S(1)} %all-to-all-done.1.refs_1_.refs_0_, f32[384,256]{1,0:T(8,128)S(1)} %get-tuple-element.22.refs_2_.refs_1_.refs_0_, f32[128,128]{1,0:T(8,128)S(1)} %get-tuple-element.23.refs_3_, ...), custom_call_target="tpu_custom_call" | custom-call | flops 1000000 | bytes 1024 | tf_op jit(solution)/shard_map/pallas_call | solution.py:289
  115.1 0.7 copy-done.17
  115.8 0.6 collective-permute-start.5
  116.4 1.7 collective-permute-done.4.refs_3_.refs_2_
  118.1 0.8 copy-done.10
  118.8 5.4 %collective-permute-done.5.refs_5_.refs_4_ = f32[384,256]{1,0:T(8,128)S(1)} collective-permute-done((f32[384,256]{1,0:T(8,128)S(1)}, f32[384,256]{1,0:T(8,128)S(1)}, u32[]{:S(2)}, u32[]{:S(2)}) %collective-permute-start.5) | collective-permute-done | bytes 393248 | tf_op jit(solution)/shard_map/ppermute | solution.py:304
  124.2 0.0 all-to-all-done.2.refs_0_
  124.2 1.1 copy-done.11
  125.4 0.9 copy-done.18
  126.3 2.0 %shard_map.37 = (f32[1024,128]{1,0:T(8,128)}, f32[256,128]{1,0:T(8,128)S(1)}, f32[256,256]{1,0:T(8,128)S(1)}) custom-call(f32[64,16,128]{2,1,0:T(8,128)S(1)} %all-to-all-done.2.refs_0_, f32[384,256]{1,0:T(8,128)S(1)} %get-tuple-element.22.refs_2_.refs_1_.refs_0_, f32[384,256]{1,0:T(8,128)S(1)} %collective-permute-done.3.refs_4_.refs_2_.refs_1_, ...), custom_call_target="tpu_custom_call" | custom-call | flops 1000000 | bytes 1024 | tf_op jit(solution)/shard_map/pallas_call | solution.py:289
  128.3 0.7 copy-done.15
  129.0 0.7 copy-done.19
  129.7 0.0 collective-permute-start.6
  129.7 0.8 shard_map.42
  130.4 12.8 %all-to-all-start.3 = ((f32[64,8,128]{2,1,0:T(8,128)}), f32[64,8,128]{2,1,0:T(8,128)S(1)}, u32[]{:S(2)}, u32[]{:S(2)}) async-start(f32[64,8,128]{2,1,0:T(8,128)} %shard_map.42), calls=%async_computation.3 | async-start | bytes 524288 | tf_op jit(solution)/shard_map/all_to_all | solution.py:318
  143.3 0.0 copy-done.16
  143.3 5.2 %shard_map.38 = (f32[384,128]{1,0:T(8,128)S(1)}, f32[384,128]{1,0:T(8,128)S(1)}) custom-call(s32[4,1]{1,0:T(4,128)S(1)} %copy.3.refs_0_, f32[256,256]{1,0:T(8,128)S(1)} %copy-done.16), custom_call_target="tpu_custom_call" | custom-call | flops 1000000 | bytes 1024 | tf_op jit(solution)/shard_map/pallas_call | solution.py:289
  148.5 0.0 collective-permute-start.7
  148.6 0.0 collective-permute-done.6.refs_5_.refs_4_
  148.6 0.0 copy-start.12
  148.6 1.0 copy-done.12
  149.6 1.0 copy-done.14
  150.6 0.9 shard_map.39
  151.5 0.3 copy-done.3
  151.8 0.3 copy-done.5
  152.1 1.2 copy-done.7
  153.3 3.5 %shard_map.40 = (f32[1024,128]{1,0:T(8,128)S(1)}, f32[1024,128]{1,0:T(8,128)S(1)}, f32[1024,128]{1,0:T(8,128)S(1)}) custom-call(f32[1024,256]{1,0:T(8,128)S(1)} %copy-done.1, f32[1024,256]{1,0:T(8,128)S(1)} %copy-done.3, f32[1024,256]{1,0:T(8,128)S(1)} %copy-done.5, f32[1024,256]{1,0:T(8,128)S(1)} %copy-done.7, f32[768,128]{1,0:T(8,128)S(1)} %get-tuple-element.29.refs_4_, ...), custom_call_target="tpu_custom_call" | custom-call | flops 1000000 | bytes 1024 | tf_op jit(solution)/shard_map/pallas_call | solution.py:289
  156.8 0.0 collective-permute-done.7.refs_3_.refs_5_.refs_6_
  156.9 1.0 shard_map.43
  157.9 0.6 shard_map.41.refs_7_.refs_0_
  158.4 0.0 all-to-all-done.3.refs_1_
  158.4 4.3 %shard_map.44.refs_1_ = f32[256,256]{1,0:T(8,128)S(1)} custom-call(s32[4,1]{1,0:T(4,128)S(1)} %copy.3.refs_0_, f32[64,8,128]{2,1,0:T(8,128)S(1)} %all-to-all-done.3.refs_1_, f32[128,128]{1,0:T(8,128)S(1)} %get-tuple-element.36.refs_2_, f32[256,128]{1,0:T(8,128)S(1)} %get-tuple-element.37.refs_3_, f32[256,128]{1,0:T(8,128)S(1)} %get-tuple-element.38.refs_4_, ...), custom_call_target="tpu_custom_call" | custom-call | flops 1000000 | bytes 1024 | tf_op jit(solution)/shard_map/pallas_call | solution.py:289
  162.8 0.6 shard_map.46
  163.4 0.0 collective-permute-start.8
  163.4 0.6 shard_map.45
  164.0 9.2 %collective-permute-done.8 = f32[1024,128]{1,0:T(8,128)S(1)} collective-permute-done((f32[1024,128]{1,0:T(8,128)S(1)}, f32[1024,128]{1,0:T(8,128)S(1)}, u32[]{:S(2)}, u32[]{:S(2)}) %collective-permute-start.8) | collective-permute-done | bytes 524320 | tf_op jit(solution)/shard_map/ppermute | solution.py:304
  173.2 1.0 pad_maximum_fusion
  (27 shorter events, 0.1 us)
Async XLA Ops:
  0.0 15.6 %collective-permute-start = (f32[1024,256]{1,0:T(8,128)}, f32[1024,256]{1,0:T(8,128)S(1)}, u32[]{:S(2)}, u32[]{:S(2)}) collective-permute-start(f32[1024,256]{1,0:T(8,128)} %refs_0_.13), channel_id=1, source_target_pairs={{7,0},{0,1},{1,2},{2,3},{3,4},{4,5},{5,6},{6,7},{15,8},{8,9},{9,10... | collective-permute-start | bytes 3145736 | tf_op jit(solution)/shard_map/ppermute | solution.py:304
  15.6 2.9 %copy-start.2 = (f32[1024,256]{1,0:T(8,128)}, f32[1024,256]{1,0:T(8,128)S(1)}, u32[]{:S(2)}) copy-start(f32[1024,256]{1,0:T(8,128)S(1)} %collective-permute-done.refs_1_) | copy-start | bytes 3145732
  15.6 21.9 %collective-permute-start.1 = (f32[1024,256]{1,0:T(8,128)S(1)}, f32[1024,256]{1,0:T(8,128)S(1)}, u32[]{:S(2)}, u32[]{:S(2)}) collective-permute-start(f32[1024,256]{1,0:T(8,128)S(1)} %collective-permute-done.refs_1_), channel_id=1, source_target_pairs={{7,0},{0,1},{1,2},{2,3},{3,4},{4,5},{5,6},{6,7},{15,8},{8,9},{9,10... | collective-permute-start | bytes 3145736 | tf_op jit(solution)/shard_map/ppermute | solution.py:304
  15.7 1.6 copy-start
  19.9 17.7 %copy-start.1 = (f32[1024,256]{1,0:T(8,128)S(1)}, f32[1024,256]{1,0:T(8,128)}, u32[]{:S(2)}) copy-start(f32[1024,256]{1,0:T(8,128)} %refs_0_.13) | copy-start | bytes 3145732
  19.9 0.8 copy-start.9
  20.7 36.2 %all-to-all-start = ((f32[64,16,128]{2,1,0:T(8,128)}), f32[64,16,128]{2,1,0:T(8,128)}, u32[]{:S(2)}, u32[]{:S(2)}) async-start(f32[64,16,128]{2,1,0:T(8,128)} %copy-done.9), calls=%async_computation | async-start | bytes 1048576 | tf_op jit(solution)/shard_map/all_to_all | solution.py:318
  37.5 26.9 %copy-start.4 = (f32[1024,256]{1,0:T(8,128)}, f32[1024,256]{1,0:T(8,128)S(1)}, u32[]{:S(2)}) copy-start(f32[1024,256]{1,0:T(8,128)S(1)} %collective-permute-done.1.refs_1_.refs_2_) | copy-start | bytes 3145732
  58.1 0.9 copy-start.8
  59.0 29.3 %all-to-all-start.1 = ((f32[64,24,128]{2,1,0:T(8,128)}), f32[64,24,128]{2,1,0:T(8,128)S(1)}, u32[]{:S(2)}, u32[]{:S(2)}) async-start(f32[64,24,128]{2,1,0:T(8,128)} %copy-done.8), calls=%async_computation.1 | async-start | bytes 1572864 | tf_op jit(solution)/shard_map/all_to_all | solution.py:318
  64.4 15.4 %collective-permute-start.2 = (f32[1024,256]{1,0:T(8,128)S(1)}, f32[1024,256]{1,0:T(8,128)S(1)}, u32[]{:S(2)}, u32[]{:S(2)}) collective-permute-start(f32[1024,256]{1,0:T(8,128)S(1)} %collective-permute-done.1.refs_1_.refs_2_), channel_id=1, source_target_pairs={{7,0},{0,1},{1,2},{2,3},{3,4},{4,5},{5,6},{6,7},{15,8},{8,9},{9,10... | collective-permute-start | bytes 3145736 | tf_op jit(solution)/shard_map/ppermute | solution.py:304
  81.2 1.0 copy-start.6
  89.1 6.8 %copy-start.21 = (s32[4,1]{0,1:T(1,128)S(1)}, s32[4,1]{0,1:T(1,128)}, u32[]{:S(2)}) copy-start(s32[4,1]{0,1:T(1,128)} %param.3) | copy-start | bytes 52
  89.1 35.1 %all-to-all-start.2 = ((f32[64,16,128]{2,1,0:T(8,128)}), f32[64,16,128]{2,1,0:T(8,128)S(1)}, u32[]{:S(2)}, u32[]{:S(2)}) async-start(f32[64,16,128]{2,1,0:T(8,128)} %shard_map.36), calls=%async_computation.2 | async-start | bytes 1048576 | tf_op jit(solution)/shard_map/all_to_all | solution.py:318
  101.3 8.4 %collective-permute-start.3 = (f32[384,256]{1,0:T(8,128)S(1)}, f32[384,256]{1,0:T(8,128)S(1)}, u32[]{:S(2)}, u32[]{:S(2)}) collective-permute-start(f32[384,256]{1,0:T(8,128)S(1)} %get-tuple-element.22.refs_2_.refs_1_.refs_0_), channel_id=1, source_target_pairs={{7,0},{0,1},{1,2},{2,3},{3,4},{4,5},{5,6},{6,7},{15,8},{8,9},{9,10... | collective-permute-start | bytes 1179656 | tf_op jit(solution)/shard_map/ppermute | solution.py:304
  109.7 8.4 %collective-permute-start.4 = (f32[384,256]{1,0:T(8,128)S(1)}, f32[384,256]{1,0:T(8,128)S(1)}, u32[]{:S(2)}, u32[]{:S(2)}) collective-permute-start(f32[384,256]{1,0:T(8,128)S(1)} %collective-permute-done.3.refs_4_.refs_2_.refs_1_), channel_id=1, source_target_pairs={{7,0},{0,1},{1,2},{2,3},{3,4},{4,5},{5,6},{6,7},{15,8},{8,9},{9,10... | collective-permute-start | bytes 1179656 | tf_op jit(solution)/shard_map/ppermute | solution.py:304
  115.1 0.7 copy-start.17
  115.8 8.4 %collective-permute-start.5 = (f32[384,256]{1,0:T(8,128)S(1)}, f32[384,256]{1,0:T(8,128)S(1)}, u32[]{:S(2)}, u32[]{:S(2)}) collective-permute-start(f32[384,256]{1,0:T(8,128)S(1)} %get-tuple-element.24.refs_4_.refs_3_.refs_1_), channel_id=1, source_target_pairs={{7,0},{0,1},{1,2},{2,3},{3,4},{4,5},{5,6},{6,7},{15,8},{8,9},{9,10... | collective-permute-start | bytes 1179656 | tf_op jit(solution)/shard_map/ppermute | solution.py:304
  118.1 0.8 copy-start.10
  124.2 4.1 %copy-start.13 = (f32[384,256]{1,0:T(8,128)}, f32[384,256]{1,0:T(8,128)S(1)}, u32[]{:S(2)}) copy-start(f32[384,256]{1,0:T(8,128)S(1)} %collective-permute-done.5.refs_5_.refs_4_) | copy-start | bytes 1179652
  124.2 1.1 copy-start.11
  125.4 0.9 copy-start.18
  128.3 0.7 copy-start.15
  129.0 0.7 copy-start.19
  129.7 18.9 %collective-permute-start.6 = (f32[1024,128]{1,0:T(8,128)}, f32[1024,128]{1,0:T(8,128)S(1)}, u32[]{:S(2)}, u32[]{:S(2)}) collective-permute-start(f32[1024,128]{1,0:T(8,128)} %get-tuple-element.26), channel_id=1, source_target_pairs={{7,0},{0,1},{1,2},{2,3},{3,4},{4,5},{5,6},{6,7},{15,8},{8,9},{9,10... | collective-permute-start | bytes 1572872 | tf_op jit(solution)/shard_map/ppermute | solution.py:304
  130.4 12.9 %copy-start.16 = (f32[256,256]{1,0:T(8,128)S(1)}, f32[256,256]{1,0:T(8,128)}, u32[]{:S(2)}) copy-start(f32[256,256]{1,0:T(8,128)} %copy-done.15) | copy-start | bytes 786436
  130.4 28.0 %all-to-all-start.3 = ((f32[64,8,128]{2,1,0:T(8,128)}), f32[64,8,128]{2,1,0:T(8,128)S(1)}, u32[]{:S(2)}, u32[]{:S(2)}) async-start(f32[64,8,128]{2,1,0:T(8,128)} %shard_map.42), calls=%async_computation.3 | async-start | bytes 524288 | tf_op jit(solution)/shard_map/all_to_all | solution.py:318
  148.5 8.3 %collective-permute-start.7 = (f32[384,128]{1,0:T(8,128)S(1)}, f32[384,128]{1,0:T(8,128)S(1)}, u32[]{:S(2)}, u32[]{:S(2)}) collective-permute-start(f32[384,128]{1,0:T(8,128)S(1)} %get-tuple-element.34), channel_id=1, source_target_pairs={{7,0},{0,1},{1,2},{2,3},{3,4},{4,5},{5,6},{6,7},{15,8},{8,9},{9,10... | collective-permute-start | bytes 589832 | tf_op jit(solution)/shard_map/ppermute | solution.py:304
  148.6 1.0 copy-start.12
  149.6 1.0 copy-start.14
  150.6 1.2 copy-start.3
  150.6 1.5 copy-start.5
  152.1 1.2 copy-start.7
  153.3 3.5 %copy-start.20 = (f32[256,128]{1,0:T(8,128)S(1)}, f32[256,128]{1,0:T(8,128)}, u32[]{:S(2)}) copy-start(f32[256,128]{1,0:T(8,128)} %copy-done.19) | copy-start | bytes 393220
  163.4 9.8 %collective-permute-start.8 = (f32[1024,128]{1,0:T(8,128)S(1)}, f32[1024,128]{1,0:T(8,128)S(1)}, u32[]{:S(2)}, u32[]{:S(2)}) collective-permute-start(f32[1024,128]{1,0:T(8,128)S(1)} %shard_map.46), channel_id=1, source_target_pairs={{7,0},{0,1},{1,2},{2,3},{3,4},{4,5},{5,6},{6,7},{15,8},{8,9},{9,10... | collective-permute-start | bytes 1572872 | tf_op jit(solution)/shard_map/ppermute | solution.py:304

commit v2 on v1

--- a/solution.py
+++ b/solution.py
@@ -172,7 +172,7 @@
     out[N:] = rotated_gram[HALF:]
 
 
-def step1_kernel(second, received, out0, h0, in0, out, carried, *parts):
+def step1_kernel(second, received, h0, out0, in0, out, carried, *parts):
     r1 = cross_dot(cross_dot(out0[:N], square_of(received, 1), (0, 0)), in0[:N])
     out[N:, HALF:] = r1[HALF:, HALF:]
     carried[:, HALF:] = r1[:, :HALF]
@@ -207,31 +207,53 @@
     own[N:] = h2[:HALF, :HALF]
 
 
-def cross3_kernel(out0, out1, kept, own2, in2a, in2b, cross, left, right):
+def shadow_kernel(received, in2a, kept, own2, out0, in0, q0_pp, out1, in1, *refs):
+    x0, x1, x2, x3, left_of_cross, kept_cols, left_cols, right_cols, weights = refs
     q0_k, q1_k, q2_k = out0[:N, :HALF], out1[:N, :HALF], own2[:N]
-    q2_p, q1_pp, q0_ppp = in2b[:N], in2a[2 * N : 3 * N], in2a[3 * N :]
-    upper = jnp.concatenate([kept[HALF:], jnp.zeros((HALF, HALF), jnp.float32)], axis=1)
+    q1_pp, q0_ppp = in2a[2 * N : 3 * N], in2a[3 * N :]
+    r3 = cross_dot(q0_k, cross_dot(square_of(received, 1), q0_ppp), (0, 0))
+    upper = jnp.concatenate([kept[HALF:], r3], axis=1)
     lower = jnp.concatenate([in2a[N + HALF : 2 * N], in2a[HALF:N]], axis=1)
-    t = cross_dot(cross_dot(q1_k, jnp.concatenate([upper, lower], axis=0), (0, 0)), q1_pp)
+    t = cross_dot(q1_k, cross_dot(jnp.concatenate([upper, lower], axis=0), q1_pp), (0, 0))
     upper = jnp.concatenate([kept[:HALF], t], axis=1)
     lower = jnp.concatenate([in2a[N : N + HALF], in2a[:HALF]], axis=1)
-    cross[...] = cross_dot(cross_dot(q2_k, jnp.concatenate([upper, lower], axis=0), (0, 0)), q2_p)
-    left[...] = cross_dot(q0_k, cross_dot(q1_k[:HALF], q2_k[:HALF]))
-    right[...] = cross_dot(q0_ppp, cross_dot(q1_pp[HALF:], q2_p[HALF:]))
-
-
-def weights_kernel(out0, in0, q0_pp, out1, in1, in2a, own2, own, before):
-    q2_k, q2_m = own2[:HALF], own2[HALF:N]
-    q1_kk, q1_mk, p1_kk, p1_mk = out1[:HALF, :HALF], out1[HALF:N, :HALF], in1[:HALF, :HALF], in1[HALF:N, :HALF]
-    p1_km, p1_mm = in1[:HALF, HALF:], in1[HALF:N, HALF:]
-    own[:N] = cross_dot(out0[:N, :HALF], cross_dot(q1_kk, q2_k))
-    travelled = cross_dot(in0[:N, HALF:], cross_dot(q1_mk, q2_k))
-    own[N : 2 * N] = travelled + cross_dot(in0[:N, :HALF], cross_dot(p1_km, q2_m))
-    own[2 * N :] = cross_dot(q0_pp[:N, HALF:], cross_dot(p1_mm, q2_m))
-    before[:N] = cross_dot(in0[:N, :HALF], p1_kk)
-    before[N : 2 * N] = cross_dot(q0_pp[:N, HALF:], p1_mk)
-    before[2 * N : 3 * N] = cross_dot(q0_pp[:N, :HALF], in2a[2 * N : 2 * N + HALF])
-    before[3 * N :] = cross_dot(in2a[3 * N :], in2a[2 * N + HALF : 3 * N])
+    left_of_cross[...] = cross_dot(q2_k, jnp.concatenate([upper, lower], axis=0), (0, 0))
+
+    q2_kk, q2_mk = own2[:HALF], own2[HALF:N]
+    p1_kk, p1_mk, p1_km, p1_mm = in1[:HALF, :HALF], in1[HALF:N, :HALF], in1[:HALF, HALF:], in1[HALF:N, HALF:]
+    weights[:, :HALF] = cross_dot(q0_k, cross_dot(out1[:HALF, :HALF], q2_kk))
+    travelled = cross_dot(in0[:N, HALF:], cross_dot(out1[HALF:N, :HALF], q2_kk))
+    weights[:, HALF:N] = travelled + cross_dot(in0[:N, :HALF], cross_dot(p1_km, q2_mk))
+    weights[:, N : N + HALF] = cross_dot(in0[:N, :HALF], p1_kk)
+    weights[:, N + HALF : 2 * N] = cross_dot(q0_pp[:N, HALF:], cross_dot(p1_mm, q2_mk))
+    weights[:, 2 * N : 2 * N + HALF] = cross_dot(q0_pp[:N, HALF:], p1_mk)
+    weights[:, 2 * N + HALF : 3 * N] = cross_dot(q0_pp[:N, :HALF], q1_pp[:HALF])
+    weights[:, 3 * N :] = cross_dot(q0_ppp, q1_pp[HALF:])
+    step = min(N, kept_cols.shape[0])
+
+    def some_rows(number, carry):
+        rows = pl.ds(pl.multiple_of(number * step, step), step)
+        both = cross_dot(x1[rows, :], weights[:, HALF : N + HALF])
+        three = cross_dot(x2[rows, :], weights[:, N + HALF : 3 * N])
+        kept_cols[rows, :] = cross_dot(x0[rows, :], weights[:, :HALF]) + both[:, :HALF] + three[:, :HALF]
+        left_cols[rows, :] = both[:, HALF:] + three[:, HALF:N]
+        right_cols[rows, :] = three[:, N:] + cross_dot(x3[rows, :], weights[:, 3 * N :])
+        return carry
+
+    lax.fori_loop(0, kept_cols.shape[0] // step, some_rows, 0)
+
+
+def last_kernel(place, kept_cols, left_cols, right_cols, in2b, q3, out):
+    kept_weight, weight = q3[:HALF, place : place + HALF], q3[HALF:, place : place + HALF]
+    left_weight, right_weight = cross_dot(in2b[:HALF], weight), cross_dot(in2b[HALF:N], weight)
+    both = jnp.concatenate([kept_cols[...], left_cols[...]], axis=1)
+    total = cross_dot(both, jnp.concatenate([kept_weight, left_weight], axis=0))
+    out[...] = total + cross_dot(right_cols[...], right_weight)
+
+
+def step3_kernel(second, left_of_cross, own2, in2b, q3, *parts):
+    gram = joined(own2[N:], cross_dot(left_of_cross[...], in2b[:N]), in2b[N:])
+    q3[...], _ = jacobi(gram, 3 * ROUNDS, second[3, 0], parts)
 
 
 def products_kernel(left, right, out):
@@ -246,53 +268,24 @@
     lax.fori_loop(0, left.shape[0] // step, some_rows, 0)
 
 
-def columns_kernel(x0, x1, x2, x3, own, before, kept, left, right):
-    step = min(N, kept.shape[0])
-
-    def some_rows(number, carry):
-        rows = pl.ds(pl.multiple_of(number * step, step), step)
-        first, second, third, fourth = x0[rows, :], x1[rows, :], x2[rows, :], x3[rows, :]
-        kept[rows, :] = cross_dot(first, own[:N]) + cross_dot(second, own[N : 2 * N]) + cross_dot(third, own[2 * N :])
-        left[rows, :] = cross_dot(second, before[:N]) + cross_dot(third, before[N : 2 * N])
-        right[rows, :] = cross_dot(third, before[2 * N : 3 * N]) + cross_dot(fourth, before[3 * N :])
-        return carry
-
-    lax.fori_loop(0, kept.shape[0] // step, some_rows, 0)
-
-
-def last_kernel(place, pair_cols, rotation, out):
-    out[...] = cross_dot(pair_cols[...], rotation[:, place : place + HALF])
-
-
-def pair_kernel(kept, left, right, in2b, out):
-    out[:, :HALF] = kept[...]
-    out[:, HALF:] = cross_dot(left[...], in2b[:HALF]) + cross_dot(right[...], in2b[HALF:N])
-
-
-def step3_kernel(second, received, cross, left, right, own2, in2b, q3, *parts):
-    total = cross[...] + cross_dot(left[...], cross_dot(square_of(received, 0), right[...]), (0, 0))
-    gram = joined(own2[N:], total, in2b[N:])
-    q3[...], _ = jacobi(gram, 3 * ROUNDS, second[3, 0], parts)
-
-
 JACOBI_PARTS = [pltpu.VMEM((HALF, HALF), jnp.float32)] * 4 + [pltpu.VMEM((N, HALF), jnp.float32)] * 2
 
 
-def run(kernel, shapes, *operands, solves=True, last=(), vmem=8):
+def run(kernel, shapes, *operands, last=(), scratch=()):
     whole, smem = pl.BlockSpec(memory_space=pltpu.VMEM), pl.BlockSpec(memory_space=pltpu.SMEM)
-    specs = [smem if x.dtype == jnp.int32 else whole for x in operands] + [pl.BlockSpec(memory_space=pl.ANY)] * len(last)
+    specs = [smem if x.dtype == jnp.int32 else whole for x in operands]
+    specs += [pl.BlockSpec(memory_space=pl.ANY)] * len(last)
 
     def body(*refs):
-        given = len(operands)
-        kernel(*refs[:given], *refs[given + len(last) :])
+        kernel(*refs[: len(operands)], *refs[len(operands) + len(last) :])
 
     return pl.pallas_call(
         body,
         out_shape=[jax.ShapeDtypeStruct(shape, jnp.float32) for shape in shapes],
         in_specs=specs,
         out_specs=[whole] * len(shapes),
-        scratch_shapes=JACOBI_PARTS if solves else [],
-        compiler_params=pltpu.CompilerParams(vmem_limit_bytes=vmem * 2**20),
+        scratch_shapes=scratch,
+        compiler_params=pltpu.CompilerParams(vmem_limit_bytes=16 * 2**20),
         cost_estimate=pl.CostEstimate(flops=10**6, bytes_accessed=2**10, transcendentals=0),
     )(*operands, *last)
 
@@ -304,7 +297,7 @@
         return lax.ppermute(values, "blk", [((i - places) % devices, i) for i in range(devices)])
 
     def products(other):
-        return run(products_kernel, [(N, N)], matrix, other, solves=False)[0]
+        return run(products_kernel, [(N, N)], matrix, other)[0]
 
     def exchange(received, skipped, *blocks, last=()):
         height = TILES // count * 8
@@ -314,49 +307,44 @@
         def kernel(*refs):
             pack_kernel(skipped, refs[0] if given else None, *refs[len(given) :])
 
-        (pieces,) = run(kernel, [(count, total, HALF)], *given, *blocks, solves=False, last=last)
+        (pieces,) = run(kernel, [(count, total, HALF)], *given, *blocks, last=last)
         return lax.all_to_all(pieces, "row", 0, 0, tiled=True)
 
     square, block = (N, N), (HALF, HALF)
-    before1 = onward(matrix)
-    received = exchange(None, 0, products(matrix), products(before1))
-    before2 = onward(before1)
-    with_c1 = exchange(received, 0, products(before2))
-    before3 = onward(before2)
-    with_c2 = exchange(with_c1, 2, products(before3))
-    out0, h0 = run(step0_kernel, [(N + HALF, N), block], sender_slot, with_c1)
+    before1, gram = lax.optimization_barrier((onward(matrix), products(matrix)))
+    received = exchange(None, 0, gram, products(before1))
+    before2, before3 = onward(before1), onward(before1, 2)
+    with_c1 = exchange(received, 0, products(before2), products(before3))
+    out0, h0 = run(step0_kernel, [(N + HALF, N), block], sender_slot, with_c1, scratch=JACOBI_PARTS)
+    with_c3 = exchange(with_c1, 2)
     in0 = onward(out0)
     q0_pp = onward(in0)
-    out1, carried = run(step1_kernel, [(N + HALF, N), square], sender_slot, with_c1, out0, h0, in0)
+    out1, carried = run(
+        step1_kernel,
+        [(N + HALF, N), square],
+        *(sender_slot, with_c1, h0, out0, in0),
+        scratch=JACOBI_PARTS,
+    )
     in1 = onward(out1)
-    with_c3 = exchange(with_c2, 1, last=(out1,))
     out2a, kept, gram2 = run(
         cross2_kernel,
         [(4 * N, HALF), (N, HALF), square],
-        *(with_c2, out0, in0, q0_pp, out1, in1, carried),
-        solves=False,
+        *(with_c3, out0, in0, q0_pp, out1, in1, carried),
     )
     in2a = onward(out2a)
-    out2b, own2 = run(step2_kernel, [(N + HALF, HALF), (N + HALF, HALF)], sender_slot, gram2)
+    out2b, own2 = run(step2_kernel, [(N + HALF, HALF)] * 2, sender_slot, gram2, scratch=JACOBI_PARTS)
     in2b = onward(out2b)
-    own, before = run(
-        weights_kernel, [(3 * N, HALF), (4 * N, HALF)], out0, in0, q0_pp, out1, in1, in2a, own2, solves=False
-    )
-    kept_cols, left_cols, right_cols = run(
-        columns_kernel, [(matrix.shape[0], HALF)] * 3, matrix, before1, before2, before3, own, before, solves=False, vmem=12
-    )
-    cross, left, right = run(
-        cross3_kernel,
-        [block, (N, HALF), (N, HALF)],
-        *(out0, out1, kept, own2, in2a, in2b),
-        solves=False,
-        last=(kept_cols,),
-    )
-    (pair_cols,) = run(pair_kernel, [matrix.shape], kept_cols, left_cols, right_cols, in2b, solves=False)
-    (q3,) = run(step3_kernel, [square], sender_slot, with_c3, cross, left, right, own2, in2b, last=(pair_cols,))
+    rows = matrix.shape[0]
+    left_of_cross, *columns = run(
+        shadow_kernel,
+        [(HALF, N)] + [(rows, HALF)] * 3,
+        *(with_c3, in2a, kept, own2, out0, in0, q0_pp, out1, in1, matrix, before1, before2, before3),
+        scratch=[pltpu.VMEM((N, 3 * N + HALF), jnp.float32)],
+    )
+    (q3,) = run(step3_kernel, [square], sender_slot, left_of_cross, own2, in2b, scratch=JACOBI_PARTS)
 
     def last_columns(place):
-        return run(functools.partial(last_kernel, place), [(matrix.shape[0], HALF)], pair_cols, q3, solves=False)[0]
+        return run(functools.partial(last_kernel, place), [(rows, HALF)], *columns, in2b, q3)[0]
 
     arrived = onward(last_columns(HALF))
     kept = last_columns(0)

time: 175 us -> 174 us (level)
  blocking collectives: 0 us -> 43.9 us
  waiting for transfers between devices: 79.9 us -> 57.2 us
  starting transfers between devices: 42.5 us -> 25.7 us
  local copies, waits for them, and re-layouts: 13.1 us -> 7.25 us
    all_to_all x0 -> x1, blocking collectives: none -> 43.9 us  [exchange(): return lax.all_to_all(pieces, 'row', 0, 0, tiled=True)]
    all_to_all x4 -> x2, waiting for transfers between devices: 24.1 us -> 0.36 us  [exchange(): return lax.all_to_all(pieces, 'row', 0, 0, tiled=True)]
    all_to_all x4 -> x2, starting transfers between devices: 41.8 us -> 23.4 us  [exchange(): return lax.all_to_all(pieces, 'row', 0, 0, tiled=True)]
    unnamed x45 -> x33, local copies, waits for them, and re-layouts: 13.1 us -> 7.25 us
    pallas_call x19 -> x15, Pallas kernels: 37.5 us -> 37.8 us  [run(): pl.pallas_call(body, out_shape=[jax.ShapeDtypeStruct(shape, jnp.float32)...]
  transfers between devices with their start and end apart: 13 -> 11, of which waited for: 8 -> 9; matrix products, arithmetic and copies ran while one was open for 0% -> 0% of each run, Pallas kernels for 16% -> 17%
where the time goes in v2:
time: 174 us; the launch traced here: 173 us
  waiting for transfers between devices  57.2 us (33%)
  blocking collectives  43.9 us (25%)
  Pallas kernels  37.8 us (22%)
  starting transfers between devices  25.7 us (15%)
  local copies, waits for them, and re-layouts  7.25 us (4%)
    ppermute x9, waiting for transfers between devices, onward(): lax.ppermute(values, 'blk', [((i - places) % devices, i) for i in range(d...  56.8 us
    all_to_all x1, blocking collectives, exchange(): return lax.all_to_all(pieces, 'row', 0, 0, tiled=True)  43.9 us
    pallas_call x15, Pallas kernels, run(): pl.pallas_call(body, out_shape=[jax.ShapeDtypeStruct(shape, jnp.float32)...  37.8 us
    all_to_all x2, starting transfers between devices, exchange(): return lax.all_to_all(pieces, 'row', 0, 0, tiled=True)  23.4 us
    unnamed x33, local copies, waits for them, and re-layouts  7.25 us
  transfers between devices with their start and end apart: 11, of which 9 were waited for; matrix products, arithmetic and copies ran while one was open for 0% of the time, Pallas kernels for 17%

profile of v2, /device:TPU:8, one launch (start us, length us, event | category | flops | bytes accessed | tf_op | source)
XLA Modules:
  0.0 173.1 jit_solution(17935474763917096191)
XLA Ops:
  0.0 0.0 collective-permute-start
  0.0 0.0 copy-start
  0.0 1.2 copy-done
  1.2 1.3 shard_map.28.refs_0_
  2.5 13.1 %collective-permute-done.refs_1_.refs_10_ = f32[1024,256]{1,0:T(8,128)S(1)} collective-permute-done((f32[1024,256]{1,0:T(8,128)}, f32[1024,256]{1,0:T(8,128)S(1)}, u32[]{:S(2)}, u32[]{:S(2)}) %collective-permute-start) | collective-permute-done | bytes 1048608 | tf_op jit(solution)/shard_map/ppermute | solution.py:297
  15.6 0.0 copy-start.2
  15.6 2.2 %collective-permute-start.2 = (f32[1024,256]{1,0:T(8,128)S(1)}, f32[1024,256]{1,0:T(8,128)S(1)}, u32[]{:S(2)}, u32[]{:S(2)}) collective-permute-start(f32[1024,256]{1,0:T(8,128)S(1)} %collective-permute-done.refs_1_.refs_10_), channel_id=1, source_target_pairs={{6,0},{7,1},{0,2},{1,3},{2,4},{3,5},{4,6},{5,7},{14,8},{15,9},{8,1... | collective-permute-start | bytes 3145736 | tf_op jit(solution)/shard_map/ppermute | solution.py:297
  17.8 0.0 collective-permute-start.1
  17.9 1.3 shard_map.29.refs_1_
  19.2 0.0 copy-done.2
  19.2 0.0 copy-start.1
  19.2 0.0 copy-start.6
  19.2 0.8 copy-done.6
  20.0 16.8 %all-to-all-start = ((f32[64,16,128]{2,1,0:T(8,128)}), f32[64,16,128]{2,1,0:T(8,128)}, u32[]{:S(2)}, u32[]{:S(2)}) async-start(f32[64,16,128]{2,1,0:T(8,128)} %copy-done.6), calls=%async_computation | async-start | bytes 1048576 | tf_op jit(solution)/shard_map/all_to_all | solution.py:311
  36.8 8.0 %collective-permute-done.2.refs_1_.refs_12_ = f32[1024,256]{1,0:T(8,128)S(1)} collective-permute-done((f32[1024,256]{1,0:T(8,128)S(1)}, f32[1024,256]{1,0:T(8,128)S(1)}, u32[]{:S(2)}, u32[]{:S(2)}) %collective-permute-start.2) | collective-permute-done | bytes 1048608 | tf_op jit(solution)/shard_map/ppermute | solution.py:297
  44.8 0.0 copy-done.1
  44.8 0.0 copy-start.4
  44.8 1.3 shard_map.32.refs_2_
  46.1 0.0 copy-done.4
  46.2 7.0 %collective-permute-done.1.refs_1_.refs_11_ = f32[1024,256]{1,0:T(8,128)} collective-permute-done((f32[1024,256]{1,0:T(8,128)S(1)}, f32[1024,256]{1,0:T(8,128)}, u32[]{:S(2)}, u32[]{:S(2)}) %collective-permute-start.1) | collective-permute-done | bytes 1048608 | tf_op jit(solution)/shard_map/ppermute | solution.py:297
  53.2 2.5 %shard_map.31.refs_1_ = f32[256,256]{1,0:T(8,128)S(1)} custom-call(f32[1024,256]{1,0:T(8,128)S(1)} %copy-done.1, f32[1024,256]{1,0:T(8,128)} %collective-permute-done.1.refs_1_.refs_11_), custom_call_target="tpu_custom_call" | custom-call | flops 1000000 | bytes 1024 | tf_op jit(solution)/shard_map/pallas_call | solution.py:282
  55.7 0.4 all-to-all-done.refs_0_
  56.0 1.2 shard_map.33
  57.2 43.9 %all_to_all.15.refs_0_.refs_1_ = f32[64,32,128]{2,1,0:T(8,128)S(1)} all-to-all(f32[64,32,128]{2,1,0:T(8,128)S(1)} %shard_map.33), channel_id=1, replica_groups=mesh['row'=64,'blk'=8] {'row'}, dimensions={0} | all-to-all | bytes 2097152 | tf_op jit(solution)/shard_map/all_to_all | solution.py:311
  101.2 0.9 shard_map.34
  102.1 0.0 copy-start.15
  102.1 6.6 %all-to-all-start.2 = ((f32[64,16,128]{2,1,0:T(8,128)}), f32[64,16,128]{2,1,0:T(8,128)S(1)}, u32[]{:S(2)}, u32[]{:S(2)}) async-start(f32[64,16,128]{2,1,0:T(8,128)} %shard_map.34), calls=%async_computation.2 | async-start | bytes 1048576 | tf_op jit(solution)/shard_map/all_to_all | solution.py:311
  108.7 0.0 copy-done.15
  108.7 0.1 copy.3.refs_0_
  108.8 5.3 %shard_map.35 = (f32[384,256]{1,0:T(8,128)S(1)}, f32[128,128]{1,0:T(8,128)S(1)}) custom-call(s32[4,1]{1,0:T(4,128)S(1)} %copy.3.refs_0_, f32[64,32,128]{2,1,0:T(8,128)S(1)} %all_to_all.15.refs_0_.refs_1_), custom_call_target="tpu_custom_call" | custom-call | flops 1000000 | bytes 1024 | tf_op jit(solution)/shard_map/pallas_call | solution.py:282
  114.1 0.0 collective-permute-start.3
  114.1 8.4 %collective-permute-done.3.refs_4_.refs_2_.refs_5_ = f32[384,256]{1,0:T(8,128)S(1)} collective-permute-done((f32[384,256]{1,0:T(8,128)S(1)}, f32[384,256]{1,0:T(8,128)S(1)}, u32[]{:S(2)}, u32[]{:S(2)}) %collective-permute-start.3) | collective-permute-done | bytes 393248 | tf_op jit(solution)/shard_map/ppermute | solution.py:297
  122.5 0.0 collective-permute-start.4
  122.5 5.4 %shard_map.36 = (f32[384,256]{1,0:T(8,128)S(1)}, f32[256,256]{1,0:T(8,128)S(1)}) custom-call(s32[4,1]{1,0:T(4,128)S(1)} %copy.3.refs_0_, f32[64,32,128]{2,1,0:T(8,128)S(1)} %all_to_all.15.refs_0_.refs_1_, f32[128,128]{1,0:T(8,128)S(1)} %get-tuple-element.23.refs_2_, f32[384,256]{1,0:T(8,128)S(1)} %get-tuple-element.22.refs_3_.refs_1_.refs_4_, ...), custom_call_target="tpu_custom_call" | custom-call | flops 1000000 | bytes 1024 | tf_op jit(solution)/shard_map/pallas_call | solution.py:282
  127.9 0.0 copy-start.13
  127.9 0.7 copy-done.13
  128.6 0.0 collective-permute-start.5
  128.6 0.0 copy-start.10
  128.6 0.8 copy-done.10
  129.4 1.5 collective-permute-done.4.refs_3_.refs_6_
  130.9 0.0 copy-start.7
  130.9 0.7 copy-done.7
  131.6 5.4 %collective-permute-done.5.refs_5_.refs_8_ = f32[384,256]{1,0:T(8,128)S(1)} collective-permute-done((f32[384,256]{1,0:T(8,128)S(1)}, f32[384,256]{1,0:T(8,128)S(1)}, u32[]{:S(2)}, u32[]{:S(2)}) %collective-permute-start.5) | collective-permute-done | bytes 393248 | tf_op jit(solution)/shard_map/ppermute | solution.py:297
  137.0 0.0 all-to-all-done.2.refs_0_
  137.0 1.0 copy-done.8
  138.0 1.0 copy-done.11
  139.0 0.9 copy-done.14
  140.0 1.2 shard_map.37
  141.2 0.0 collective-permute-start.6
  141.3 5.2 %shard_map.38 = (f32[384,128]{1,0:T(8,128)S(1)}, f32[384,128]{1,0:T(8,128)S(1)}) custom-call(s32[4,1]{1,0:T(4,128)S(1)} %copy.3.refs_0_, f32[256,256]{1,0:T(8,128)S(1)} %get-tuple-element.28.refs_1_), custom_call_target="tpu_custom_call" | custom-call | flops 1000000 | bytes 1024 | tf_op jit(solution)/shard_map/pallas_call | solution.py:282
  146.5 0.0 collective-permute-start.7
  146.5 4.5 %collective-permute-done.6.refs_1_ = f32[1024,128]{1,0:T(8,128)S(1)} collective-permute-done((f32[1024,128]{1,0:T(8,128)S(1)}, f32[1024,128]{1,0:T(8,128)S(1)}, u32[]{:S(2)}, u32[]{:S(2)}) %collective-permute-start.6) | collective-permute-done | bytes 524320 | tf_op jit(solution)/shard_map/ppermute | solution.py:297
  151.1 0.0 copy-done.3
  151.1 0.0 copy-done.5
  151.1 0.0 copy-done.9
  151.1 0.0 copy-done.12
  151.1 5.9 %shard_map.39 = (f32[128,256]{1,0:T(8,128)S(1)}, f32[1024,128]{1,0:T(8,128)S(1)}, f32[1024,128]{1,0:T(8,128)S(1)}, f32[1024,128]{1,0:T(8,128)S(1)}) custom-call(f32[64,16,128]{2,1,0:T(8,128)S(1)} %all-to-all-done.2.refs_0_, f32[1024,128]{1,0:T(8,128)S(1)} %collective-permute-done.6.refs_1_, f32[256,128]{1,0:T(8,128)S(1)} %get-tuple-element.27.refs_2_, ...), custom_call_target="tpu_custom_call" | custom-call | flops 1000000 | bytes 1024 | tf_op jit(solution)/shard_map/pallas_call | solution.py:282
  157.0 0.0 collective-permute-done.7.refs_3_
  157.0 4.3 %shard_map.40.refs_4_ = f32[256,256]{1,0:T(8,128)S(1)} custom-call(s32[4,1]{1,0:T(4,128)S(1)} %copy.3.refs_0_, f32[128,256]{1,0:T(8,128)S(1)} %get-tuple-element.34.refs_1_, f32[384,128]{1,0:T(8,128)S(1)} %get-tuple-element.29.refs_3_.refs_2_, f32[384,128]{1,0:T(8,128)S(1)} %collective-permute-done.7.refs_3_), custom_call_target="tpu_custom_call" | custom-call | flops 1000000 | bytes 1024 | tf_op jit(solution)/shard_map/pallas_call | solution.py:282
  161.3 1.0 shard_map.42
  162.2 0.0 collective-permute-start.8
  162.3 1.0 shard_map.41
  163.2 8.8 %collective-permute-done.8 = f32[1024,128]{1,0:T(8,128)S(1)} collective-permute-done((f32[1024,128]{1,0:T(8,128)S(1)}, f32[1024,128]{1,0:T(8,128)S(1)}, u32[]{:S(2)}, u32[]{:S(2)}) %collective-permute-start.8) | collective-permute-done | bytes 524320 | tf_op jit(solution)/shard_map/ppermute | solution.py:297
  172.1 1.0 pad_maximum_fusion
  (8 shorter events, 0.0 us)
Async XLA Ops:
  0.0 15.6 %collective-permute-start = (f32[1024,256]{1,0:T(8,128)}, f32[1024,256]{1,0:T(8,128)S(1)}, u32[]{:S(2)}, u32[]{:S(2)}) collective-permute-start(f32[1024,256]{1,0:T(8,128)} %refs_9_.1), channel_id=1, source_target_pairs={{7,0},{0,1},{1,2},{2,3},{3,4},{4,5},{5,6},{6,7},{15,8},{8,9},{9,10... | collective-permute-start | bytes 3145736 | tf_op jit(solution)/shard_map/ppermute | solution.py:297
  0.0 1.2 copy-start
  15.6 3.5 %copy-start.2 = (f32[1024,256]{1,0:T(8,128)}, f32[1024,256]{1,0:T(8,128)S(1)}, u32[]{:S(2)}) copy-start(f32[1024,256]{1,0:T(8,128)S(1)} %collective-permute-done.refs_1_.refs_10_) | copy-start | bytes 3145732
  15.6 29.2 %collective-permute-start.2 = (f32[1024,256]{1,0:T(8,128)S(1)}, f32[1024,256]{1,0:T(8,128)S(1)}, u32[]{:S(2)}, u32[]{:S(2)}) collective-permute-start(f32[1024,256]{1,0:T(8,128)S(1)} %collective-permute-done.refs_1_.refs_10_), channel_id=1, source_target_pairs={{6,0},{7,1},{0,2},{1,3},{2,4},{3,5},{4,6},{5,7},{14,8},{15,9},{8,1... | collective-permute-start | bytes 3145736 | tf_op jit(solution)/shard_map/ppermute | solution.py:297
  17.8 35.3 %collective-permute-start.1 = (f32[1024,256]{1,0:T(8,128)S(1)}, f32[1024,256]{1,0:T(8,128)}, u32[]{:S(2)}, u32[]{:S(2)}) collective-permute-start(f32[1024,256]{1,0:T(8,128)S(1)} %collective-permute-done.refs_1_.refs_10_), channel_id=1, source_target_pairs={{7,0},{0,1},{1,2},{2,3},{3,4},{4,5},{5,6},{6,7},{15,8},{8,9},{9,10... | collective-permute-start | bytes 3145736 | tf_op jit(solution)/shard_map/ppermute | solution.py:297
  19.2 25.7 %copy-start.1 = (f32[1024,256]{1,0:T(8,128)S(1)}, f32[1024,256]{1,0:T(8,128)}, u32[]{:S(2)}) copy-start(f32[1024,256]{1,0:T(8,128)} %refs_9_.1) | copy-start | bytes 3145732
  19.2 0.8 copy-start.6
  20.0 36.0 %all-to-all-start = ((f32[64,16,128]{2,1,0:T(8,128)}), f32[64,16,128]{2,1,0:T(8,128)}, u32[]{:S(2)}, u32[]{:S(2)}) async-start(f32[64,16,128]{2,1,0:T(8,128)} %copy-done.6), calls=%async_computation | async-start | bytes 1048576 | tf_op jit(solution)/shard_map/all_to_all | solution.py:311
  44.8 1.3 copy-start.4
  102.1 6.6 %copy-start.15 = (s32[4,1]{0,1:T(1,128)S(1)}, s32[4,1]{0,1:T(1,128)}, u32[]{:S(2)}) copy-start(s32[4,1]{0,1:T(1,128)} %param.3) | copy-start | bytes 52
  102.1 35.0 %all-to-all-start.2 = ((f32[64,16,128]{2,1,0:T(8,128)}), f32[64,16,128]{2,1,0:T(8,128)S(1)}, u32[]{:S(2)}, u32[]{:S(2)}) async-start(f32[64,16,128]{2,1,0:T(8,128)} %shard_map.34), calls=%async_computation.2 | async-start | bytes 1048576 | tf_op jit(solution)/shard_map/all_to_all | solution.py:311
  114.1 8.4 %collective-permute-start.3 = (f32[384,256]{1,0:T(8,128)S(1)}, f32[384,256]{1,0:T(8,128)S(1)}, u32[]{:S(2)}, u32[]{:S(2)}) collective-permute-start(f32[384,256]{1,0:T(8,128)S(1)} %get-tuple-element.22.refs_3_.refs_1_.refs_4_), channel_id=1, source_target_pairs={{7,0},{0,1},{1,2},{2,3},{3,4},{4,5},{5,6},{6,7},{15,8},{8,9},{9,10... | collective-permute-start | bytes 1179656 | tf_op jit(solution)/shard_map/ppermute | solution.py:297
  122.5 8.4 %collective-permute-start.4 = (f32[384,256]{1,0:T(8,128)S(1)}, f32[384,256]{1,0:T(8,128)S(1)}, u32[]{:S(2)}, u32[]{:S(2)}) collective-permute-start(f32[384,256]{1,0:T(8,128)S(1)} %collective-permute-done.3.refs_4_.refs_2_.refs_5_), channel_id=1, source_target_pairs={{7,0},{0,1},{1,2},{2,3},{3,4},{4,5},{5,6},{6,7},{15,8},{8,9},{9,10... | collective-permute-start | bytes 1179656 | tf_op jit(solution)/shard_map/ppermute | solution.py:297
  127.9 0.7 copy-start.13
  128.6 8.4 %collective-permute-start.5 = (f32[384,256]{1,0:T(8,128)S(1)}, f32[384,256]{1,0:T(8,128)S(1)}, u32[]{:S(2)}, u32[]{:S(2)}) collective-permute-start(f32[384,256]{1,0:T(8,128)S(1)} %get-tuple-element.24.refs_4_.refs_7_), channel_id=1, source_target_pairs={{7,0},{0,1},{1,2},{2,3},{3,4},{4,5},{5,6},{6,7},{15,8},{8,9},{9,10... | collective-permute-start | bytes 1179656 | tf_op jit(solution)/shard_map/ppermute | solution.py:297
  128.6 0.8 copy-start.10
  130.9 0.7 copy-start.7
  137.0 1.0 copy-start.8
  138.0 1.0 copy-start.11
  139.0 0.9 copy-start.14
  140.0 11.1 %copy-start.3 = (f32[1024,256]{1,0:T(8,128)S(1)}, f32[1024,256]{1,0:T(8,128)}, u32[]{:S(2)}) copy-start(f32[1024,256]{1,0:T(8,128)} %copy-done.2) | copy-start | bytes 3145732
  140.0 11.1 %copy-start.5 = (f32[1024,256]{1,0:T(8,128)S(1)}, f32[1024,256]{1,0:T(8,128)}, u32[]{:S(2)}) copy-start(f32[1024,256]{1,0:T(8,128)} %copy-done.4) | copy-start | bytes 3145732
  140.0 11.1 %copy-start.9 = (f32[384,256]{1,0:T(8,128)S(1)}, f32[384,256]{1,0:T(8,128)}, u32[]{:S(2)}) copy-start(f32[384,256]{1,0:T(8,128)} %copy-done.7) | copy-start | bytes 1179652
  140.0 11.1 %copy-start.12 = (f32[384,256]{1,0:T(8,128)S(1)}, f32[384,256]{1,0:T(8,128)}, u32[]{:S(2)}) copy-start(f32[384,256]{1,0:T(8,128)} %copy-done.10) | copy-start | bytes 1179652
  141.2 9.8 %collective-permute-start.6 = (f32[1024,128]{1,0:T(8,128)S(1)}, f32[1024,128]{1,0:T(8,128)S(1)}, u32[]{:S(2)}, u32[]{:S(2)}) collective-permute-start(f32[1024,128]{1,0:T(8,128)S(1)} %get-tuple-element.26), channel_id=1, source_target_pairs={{7,0},{0,1},{1,2},{2,3},{3,4},{4,5},{5,6},{6,7},{15,8},{8,9},{9,10... | collective-permute-start | bytes 1572872 | tf_op jit(solution)/shard_map/ppermute | solution.py:297
  146.5 10.5 %collective-permute-start.7 = (f32[384,128]{1,0:T(8,128)S(1)}, f32[384,128]{1,0:T(8,128)S(1)}, u32[]{:S(2)}, u32[]{:S(2)}) collective-permute-start(f32[384,128]{1,0:T(8,128)S(1)} %get-tuple-element.33), channel_id=1, source_target_pairs={{7,0},{0,1},{1,2},{2,3},{3,4},{4,5},{5,6},{6,7},{15,8},{8,9},{9,10... | collective-permute-start | bytes 589832 | tf_op jit(solution)/shard_map/ppermute | solution.py:297
  162.2 9.8 %collective-permute-start.8 = (f32[1024,128]{1,0:T(8,128)S(1)}, f32[1024,128]{1,0:T(8,128)S(1)}, u32[]{:S(2)}, u32[]{:S(2)}) collective-permute-start(f32[1024,128]{1,0:T(8,128)S(1)} %shard_map.42), channel_id=1, source_target_pairs={{7,0},{0,1},{1,2},{2,3},{3,4},{4,5},{5,6},{6,7},{15,8},{8,9},{9,10... | collective-permute-start | bytes 1572872 | tf_op jit(solution)/shard_map/ppermute | solution.py:297

commit v3 on v2

--- a/solution.py
+++ b/solution.py
@@ -173,28 +173,28 @@
 
 
 def step1_kernel(second, received, h0, out0, in0, out, carried, *parts):
-    r1 = cross_dot(cross_dot(out0[:N], square_of(received, 1), (0, 0)), in0[:N])
-    out[N:, HALF:] = r1[HALF:, HALF:]
-    carried[:, HALF:] = r1[:, :HALF]
-    gram = joined(h0[...], r1[:HALF, HALF:], in0[N:, HALF:])
-    q1, h1 = jacobi(gram, ROUNDS, second[1, 0], parts)
+    q0_p = in0[:N]
+    r1 = cross_dot(cross_dot(out0[:N], square_of(received, 1), (0, 0)), q0_p)
+    out[N + HALF : 2 * N] = r1[HALF:]
+    out[2 * N :] = q0_p
+    carried[:, HALF:] = r1[:HALF, :HALF]
+    q1, h1 = jacobi(joined(h0[...], r1[:HALF, HALF:], in0[N:, HALF:]), ROUNDS, second[1, 0], parts)
     out[:N] = q1
-    out[N:, :HALF] = h1[HALF:, HALF:]
-    carried[:, :HALF] = h1[:, :HALF]
-
-
-def cross2_kernel(received, out0, in0, q0_pp, out1, in1, carried, out, kept, gram):
-    r2 = cross_dot(cross_dot(out0[:N], square_of(received, 0), (0, 0)), q0_pp[:N])
-    upper = jnp.concatenate([carried[:HALF, HALF:], r2[:HALF, HALF:]], axis=1)
-    lower = jnp.concatenate([in0[N:, :HALF], in1[N:, HALF:]], axis=1)
+    out[N : N + HALF] = h1[HALF:]
+    carried[:, :HALF] = h1[:HALF, :HALF]
+
+
+def cross2_kernel(received, out0, in0, out1, in1, carried, out, kept, gram):
+    q0_pp = in1[2 * N :]
+    r2 = cross_dot(cross_dot(out0[:N], square_of(received, 0), (0, 0)), q0_pp)
+    upper = jnp.concatenate([carried[:, HALF:], r2[:HALF, HALF:]], axis=1)
+    lower = jnp.concatenate([in0[N:, :HALF], in1[N + HALF : 2 * N, HALF:]], axis=1)
     s1 = cross_dot(cross_dot(out1[:N], jnp.concatenate([upper, lower], axis=0), (0, 0)), in1[:N])
-    gram[...] = joined(carried[:HALF, :HALF], s1[:HALF, HALF:], in1[N:, :HALF])
+    gram[...] = joined(carried[:, :HALF], s1[:HALF, HALF:], in1[N : N + HALF, HALF:])
     out[:HALF] = s1[HALF:, HALF:]
     out[HALF:N] = r2[HALF:, HALF:]
-    out[N : N + HALF] = carried[HALF:, :HALF]
-    out[N + HALF : 2 * N] = carried[HALF:, HALF:]
-    out[2 * N : 3 * N] = in1[:N, HALF:]
-    out[3 * N :] = q0_pp[:N, HALF:]
+    out[N : 2 * N] = in1[:N, HALF:]
+    out[2 * N :] = q0_pp[:, HALF:]
     kept[:HALF] = s1[:HALF, :HALF]
     kept[HALF:] = r2[:HALF, :HALF]
 
@@ -207,40 +207,51 @@
     own[N:] = h2[:HALF, :HALF]
 
 
-def shadow_kernel(received, in2a, kept, own2, out0, in0, q0_pp, out1, in1, *refs):
-    x0, x1, x2, x3, left_of_cross, kept_cols, left_cols, right_cols, weights = refs
-    q0_k, q1_k, q2_k = out0[:N, :HALF], out1[:N, :HALF], own2[:N]
-    q1_pp, q0_ppp = in2a[2 * N : 3 * N], in2a[3 * N :]
-    r3 = cross_dot(q0_k, cross_dot(square_of(received, 1), q0_ppp), (0, 0))
-    upper = jnp.concatenate([kept[HALF:], r3], axis=1)
-    lower = jnp.concatenate([in2a[N + HALF : 2 * N], in2a[HALF:N]], axis=1)
-    t = cross_dot(q1_k, cross_dot(jnp.concatenate([upper, lower], axis=0), q1_pp), (0, 0))
-    upper = jnp.concatenate([kept[:HALF], t], axis=1)
-    lower = jnp.concatenate([in2a[N : N + HALF], in2a[:HALF]], axis=1)
-    left_of_cross[...] = cross_dot(q2_k, jnp.concatenate([upper, lower], axis=0), (0, 0))
-
-    q2_kk, q2_mk = own2[:HALF], own2[HALF:N]
+def in_chunks(count, some_rows):
+    step = min(N, count)
+
+    def one(number, carry):
+        some_rows(pl.ds(pl.multiple_of(number * step, step), step))
+        return carry
+
+    lax.fori_loop(0, count // step, one, 0)
+
+
+def columns_kernel(out0, in0, out1, in1, own2, x0, x1, x2, kept_cols, left_cols, weights):
+    q2_kk, q2_mk, q0_pp = own2[:HALF], own2[HALF:N], in1[2 * N :]
     p1_kk, p1_mk, p1_km, p1_mm = in1[:HALF, :HALF], in1[HALF:N, :HALF], in1[:HALF, HALF:], in1[HALF:N, HALF:]
-    weights[:, :HALF] = cross_dot(q0_k, cross_dot(out1[:HALF, :HALF], q2_kk))
+    weights[:, :HALF] = cross_dot(out0[:N, :HALF], cross_dot(out1[:HALF, :HALF], q2_kk))
     travelled = cross_dot(in0[:N, HALF:], cross_dot(out1[HALF:N, :HALF], q2_kk))
     weights[:, HALF:N] = travelled + cross_dot(in0[:N, :HALF], cross_dot(p1_km, q2_mk))
     weights[:, N : N + HALF] = cross_dot(in0[:N, :HALF], p1_kk)
-    weights[:, N + HALF : 2 * N] = cross_dot(q0_pp[:N, HALF:], cross_dot(p1_mm, q2_mk))
-    weights[:, 2 * N : 2 * N + HALF] = cross_dot(q0_pp[:N, HALF:], p1_mk)
-    weights[:, 2 * N + HALF : 3 * N] = cross_dot(q0_pp[:N, :HALF], q1_pp[:HALF])
-    weights[:, 3 * N :] = cross_dot(q0_ppp, q1_pp[HALF:])
-    step = min(N, kept_cols.shape[0])
-
-    def some_rows(number, carry):
-        rows = pl.ds(pl.multiple_of(number * step, step), step)
-        both = cross_dot(x1[rows, :], weights[:, HALF : N + HALF])
-        three = cross_dot(x2[rows, :], weights[:, N + HALF : 3 * N])
-        kept_cols[rows, :] = cross_dot(x0[rows, :], weights[:, :HALF]) + both[:, :HALF] + three[:, :HALF]
-        left_cols[rows, :] = both[:, HALF:] + three[:, HALF:N]
-        right_cols[rows, :] = three[:, N:] + cross_dot(x3[rows, :], weights[:, 3 * N :])
-        return carry
-
-    lax.fori_loop(0, kept_cols.shape[0] // step, some_rows, 0)
+    weights[:, N + HALF : 2 * N] = cross_dot(q0_pp[:, HALF:], cross_dot(p1_mm, q2_mk))
+    weights[:, 2 * N :] = cross_dot(q0_pp[:, HALF:], p1_mk)
+
+    def some_rows(rows):
+        both = cross_dot(x1[rows, :], weights[:, HALF : N + HALF]) + cross_dot(x2[rows, :], weights[:, N + HALF :])
+        kept_cols[rows, :] = cross_dot(x0[rows, :], weights[:, :HALF]) + both[:, :HALF]
+        left_cols[rows, :] = both[:, HALF:]
+
+    in_chunks(kept_cols.shape[0], some_rows)
+
+
+def cross3_kernel(received, out0, out1, in1, in2a, kept, own2, x2, x3, left_of_cross, right_cols, weights):
+    q0_k, q1_k, q2_k = out0[:N, :HALF], out1[:N, :HALF], own2[:N]
+    q1_pp, q0_ppp = in2a[N : 2 * N], in2a[2 * N :]
+    r3 = cross_dot(q0_k, cross_dot(square_of(received, 0), q0_ppp), (0, 0))
+    upper = jnp.concatenate([kept[HALF:], r3], axis=1)
+    lower = jnp.concatenate([in1[N + HALF : 2 * N, :HALF], in2a[HALF:N]], axis=1)
+    t = cross_dot(q1_k, cross_dot(jnp.concatenate([upper, lower], axis=0), q1_pp), (0, 0))
+    upper = jnp.concatenate([kept[:HALF], t], axis=1)
+    lower = jnp.concatenate([in1[N : N + HALF, :HALF], in2a[:HALF]], axis=1)
+    left_of_cross[...] = cross_dot(q2_k, jnp.concatenate([upper, lower], axis=0), (0, 0))
+    weights[:, :HALF] = cross_dot(in1[2 * N :, :HALF], q1_pp[:HALF])
+    weights[:, HALF:] = cross_dot(q0_ppp, q1_pp[HALF:])
+
+    def some_rows(rows):
+        right_cols[rows, :] = cross_dot(x2[rows, :], weights[:, :HALF]) + cross_dot(x3[rows, :], weights[:, HALF:])
+
+    in_chunks(right_cols.shape[0], some_rows)
 
 
 def last_kernel(place, kept_cols, left_cols, right_cols, in2b, q3, out):
@@ -257,15 +268,12 @@
 
 
 def products_kernel(left, right, out):
-    step = min(N, left.shape[0])
     out[...] = jnp.zeros(out.shape, jnp.float32)
 
-    def some_rows(number, carry):
-        rows = pl.ds(pl.multiple_of(number * step, step), step)
+    def some_rows(rows):
         out[...] += cross_dot(left[rows, :], right[rows, :], (0, 0))
-        return carry
-
-    lax.fori_loop(0, left.shape[0] // step, some_rows, 0)
+
+    in_chunks(left.shape[0], some_rows)
 
 
 JACOBI_PARTS = [pltpu.VMEM((HALF, HALF), jnp.float32)] * 4 + [pltpu.VMEM((N, HALF), jnp.float32)] * 2
@@ -313,34 +321,43 @@
     square, block = (N, N), (HALF, HALF)
     before1, gram = lax.optimization_barrier((onward(matrix), products(matrix)))
     received = exchange(None, 0, gram, products(before1))
-    before2, before3 = onward(before1), onward(before1, 2)
-    with_c1 = exchange(received, 0, products(before2), products(before3))
+    before2 = onward(before1)
+    with_c1 = exchange(received, 0, products(before2))
+    before3 = onward(before2)
+    with_c2 = exchange(with_c1, 2, products(before3))
     out0, h0 = run(step0_kernel, [(N + HALF, N), block], sender_slot, with_c1, scratch=JACOBI_PARTS)
-    with_c3 = exchange(with_c1, 2)
     in0 = onward(out0)
-    q0_pp = onward(in0)
     out1, carried = run(
         step1_kernel,
-        [(N + HALF, N), square],
+        [(3 * N, N), (HALF, N)],
         *(sender_slot, with_c1, h0, out0, in0),
         scratch=JACOBI_PARTS,
     )
     in1 = onward(out1)
+    with_c3 = exchange(with_c2, 1, last=(out1,))
     out2a, kept, gram2 = run(
         cross2_kernel,
-        [(4 * N, HALF), (N, HALF), square],
-        *(with_c3, out0, in0, q0_pp, out1, in1, carried),
+        [(3 * N, HALF), (N, HALF), square],
+        *(with_c2, out0, in0, out1, in1, carried),
     )
     in2a = onward(out2a)
     out2b, own2 = run(step2_kernel, [(N + HALF, HALF)] * 2, sender_slot, gram2, scratch=JACOBI_PARTS)
     in2b = onward(out2b)
     rows = matrix.shape[0]
-    left_of_cross, *columns = run(
-        shadow_kernel,
-        [(HALF, N)] + [(rows, HALF)] * 3,
-        *(with_c3, in2a, kept, own2, out0, in0, q0_pp, out1, in1, matrix, before1, before2, before3),
-        scratch=[pltpu.VMEM((N, 3 * N + HALF), jnp.float32)],
-    )
+    kept_cols, left_cols = run(
+        columns_kernel,
+        [(rows, HALF)] * 2,
+        *(out0, in0, out1, in1, own2, matrix, before1, before2),
+        scratch=[pltpu.VMEM((N, 2 * N + HALF), jnp.float32)],
+    )
+    left_of_cross, right_cols = run(
+        cross3_kernel,
+        [(HALF, N), (rows, HALF)],
+        *(with_c3, out0, out1, in1, in2a, kept, own2, before2, before3),
+        scratch=[pltpu.VMEM((N, N), jnp.float32)],
+        last=(kept_cols,),
+    )
+    columns = (kept_cols, left_cols, right_cols)
     (q3,) = run(step3_kernel, [square], sender_slot, left_of_cross, own2, in2b, scratch=JACOBI_PARTS)
 
     def last_columns(place):

time: 174 us -> 172 us (0.989)
  blocking collectives: 43.9 us -> 0 us
  waiting for transfers between devices: 57.2 us -> 75.7 us
  starting transfers between devices: 25.7 us -> 38.2 us
  Pallas kernels: 37.8 us -> 48.2 us
    all_to_all x2 -> x4, waiting for transfers between devices: 0.36 us -> 54.6 us  [exchange(): return lax.all_to_all(pieces, 'row', 0, 0, tiled=True)]
    all_to_all x1 -> x0, blocking collectives: 43.9 us -> none  [exchange(): return lax.all_to_all(pieces, 'row', 0, 0, tiled=True)]
    ppermute x9 -> x8, waiting for transfers between devices: 56.8 us -> 21.1 us  [onward(): lax.ppermute(values, 'blk', [((i - places) % devices, i) for i in range(d...]
    all_to_all x2 -> x4, starting transfers between devices: 23.4 us -> 35.2 us  [exchange(): return lax.all_to_all(pieces, 'row', 0, 0, tiled=True)]
    pallas_call x15 -> x17, Pallas kernels: 37.8 us -> 48.2 us  [run(): pl.pallas_call(body, out_shape=[jax.ShapeDtypeStruct(shape, jnp.float32)...]
    unnamed x33 -> x27, local copies, waits for them, and re-layouts: 7.25 us -> 7.78 us
  transfers between devices with their start and end apart: 11 -> 12, of which waited for: 9 -> 5; matrix products, arithmetic and copies ran while one was open for 0% -> 0% of each run, Pallas kernels for 17% -> 24%
where the time goes in v3:
time: 172 us; the launch traced here: 171 us
  waiting for transfers between devices  75.7 us (44%)
  Pallas kernels  48.2 us (28%)
  starting transfers between devices  38.2 us (22%)
  local copies, waits for them, and re-layouts  7.78 us (5%)
    all_to_all x4, waiting for transfers between devices, exchange(): return lax.all_to_all(pieces, 'row', 0, 0, tiled=True)  54.6 us
    pallas_call x17, Pallas kernels, run(): pl.pallas_call(body, out_shape=[jax.ShapeDtypeStruct(shape, jnp.float32)...  48.2 us
    all_to_all x4, starting transfers between devices, exchange(): return lax.all_to_all(pieces, 'row', 0, 0, tiled=True)  35.2 us
    ppermute x8, waiting for transfers between devices, onward(): lax.ppermute(values, 'blk', [((i - places) % devices, i) for i in range(d...  21.1 us
    unnamed x27, local copies, waits for them, and re-layouts  7.78 us
  transfers between devices with their start and end apart: 12, of which 5 were waited for; matrix products, arithmetic and copies ran while one was open for 0% of the time, Pallas kernels for 24%

profile of v3, /device:TPU:8, one launch (start us, length us, event | category | flops | bytes accessed | tf_op | source)
XLA Modules:
  0.0 171.2 jit_solution(6182237966377269097)
XLA Ops:
  0.0 0.0 collective-permute-start
  0.0 0.0 copy-start
  0.0 1.2 copy-done
  1.2 1.3 shard_map.28.refs_0_
  2.5 13.2 %collective-permute-done.refs_1_.refs_6_ = f32[1024,256]{1,0:T(8,128)} collective-permute-done((f32[1024,256]{1,0:T(8,128)}, f32[1024,256]{1,0:T(8,128)}, u32[]{:S(2)}, u32[]{:S(2)}) %collective-permute-start) | collective-permute-done | bytes 1048608 | tf_op jit(solution)/shard_map/ppermute | solution.py:305
  15.8 0.0 collective-permute-start.1
  15.8 2.5 %shard_map.29.refs_1_ = f32[256,256]{1,0:T(8,128)S(1)} custom-call(f32[1024,256]{1,0:T(8,128)S(1)} %copy-done, f32[1024,256]{1,0:T(8,128)} %collective-permute-done.refs_1_.refs_6_), custom_call_target="tpu_custom_call" | custom-call | flops 1000000 | bytes 1024 | tf_op jit(solution)/shard_map/pallas_call | solution.py:290
  18.3 0.0 copy-start.1
  18.3 0.8 shard_map.30
  19.1 16.6 %all-to-all-start = ((f32[64,16,128]{2,1,0:T(8,128)}), f32[64,16,128]{2,1,0:T(8,128)S(1)}, u32[]{:S(2)}, u32[]{:S(2)}) async-start(f32[64,16,128]{2,1,0:T(8,128)} %shard_map.30), calls=%async_computation | async-start | bytes 1048576 | tf_op jit(solution)/shard_map/all_to_all | solution.py:319
  35.7 0.0 collective-permute-done.1.refs_1_.refs_7_
  35.7 0.0 copy-done.1
  35.7 0.0 copy-start.2
  35.8 1.3 shard_map.31.refs_1_
  37.1 18.5 %all-to-all-done.refs_0_ = f32[64,16,128]{2,1,0:T(8,128)S(1)} async-done(((f32[64,16,128]{2,1,0:T(8,128)}), f32[64,16,128]{2,1,0:T(8,128)S(1)}, u32[]{:S(2)}, u32[]{:S(2)}) %all-to-all-start) | async-done | bytes 524320 | tf_op jit(solution)/shard_map/all_to_all | solution.py:319
  55.6 0.1 shard_map.32
  55.7 0.0 copy-start.7
  55.7 0.9 copy-done.7
  56.6 0.0 copy-start.12
  56.6 5.6 %all-to-all-start.1 = ((f32[64,24,128]{2,1,0:T(8,128)}), f32[64,24,128]{2,1,0:T(8,128)S(1)}, u32[]{:S(2)}, u32[]{:S(2)}) async-start(f32[64,24,128]{2,1,0:T(8,128)} %copy-done.7), calls=%async_computation.1 | async-start | bytes 1572864 | tf_op jit(solution)/shard_map/all_to_all | solution.py:319
  62.2 0.0 copy-done.2
  62.2 0.0 collective-permute-start.4
  62.2 0.0 copy-done.12
  62.2 0.1 copy.3.refs_0_
  62.3 23.8 %all-to-all-done.1.refs_1_.refs_0_ = f32[64,24,128]{2,1,0:T(8,128)S(1)} async-done(((f32[64,24,128]{2,1,0:T(8,128)}), f32[64,24,128]{2,1,0:T(8,128)S(1)}, u32[]{:S(2)}, u32[]{:S(2)}) %all-to-all-start.1) | async-done | bytes 786464 | tf_op jit(solution)/shard_map/all_to_all | solution.py:319
  86.1 5.3 %shard_map.33 = (f32[384,256]{1,0:T(8,128)S(1)}, f32[128,128]{1,0:T(8,128)S(1)}) custom-call(s32[4,1]{1,0:T(4,128)S(1)} %copy.3.refs_0_, f32[64,24,128]{2,1,0:T(8,128)S(1)} %all-to-all-done.1.refs_1_.refs_0_), custom_call_target="tpu_custom_call" | custom-call | flops 1000000 | bytes 1024 | tf_op jit(solution)/shard_map/pallas_call | solution.py:290
  91.4 0.0 collective-permute-start.2
  91.4 0.0 collective-permute-done.4.refs_1_.refs_8_
  91.4 2.5 %shard_map.35.refs_1_ = f32[256,256]{1,0:T(8,128)S(1)} custom-call(f32[1024,256]{1,0:T(8,128)S(1)} %copy-done.1, f32[1024,256]{1,0:T(8,128)} %collective-permute-done.4.refs_1_.refs_8_), custom_call_target="tpu_custom_call" | custom-call | flops 1000000 | bytes 1024 | tf_op jit(solution)/shard_map/pallas_call | solution.py:290
  93.9 0.9 shard_map.36
  94.8 6.3 %all-to-all-start.2 = ((f32[64,16,128]{2,1,0:T(8,128)}), f32[64,16,128]{2,1,0:T(8,128)}, u32[]{:S(2)}, u32[]{:S(2)}) async-start(f32[64,16,128]{2,1,0:T(8,128)} %shard_map.36), calls=%async_computation.2 | async-start | bytes 1048576 | tf_op jit(solution)/shard_map/all_to_all | solution.py:319
  101.1 0.0 collective-permute-done.2.refs_4_.refs_2_.refs_1_
  101.1 5.9 %shard_map.34 = (f32[768,256]{1,0:T(8,128)S(1)}, f32[128,256]{1,0:T(8,128)S(1)}) custom-call(s32[4,1]{1,0:T(4,128)S(1)} %copy.3.refs_0_, f32[64,24,128]{2,1,0:T(8,128)S(1)} %all-to-all-done.1.refs_1_.refs_0_, f32[128,128]{1,0:T(8,128)S(1)} %get-tuple-element.23.refs_2_, f32[384,256]{1,0:T(8,128)S(1)} %get-tuple-element.22.refs_3_.refs_1_.refs_0_, ...), custom_call_target="tpu_custom_call" | custom-call | flops 1000000 | bytes 1024 | tf_op jit(solution)/shard_map/pallas_call | solution.py:290
  107.0 1.2 collective-permute-start.3
  108.2 12.3 %all-to-all-done.2.refs_0_ = f32[64,16,128]{2,1,0:T(8,128)} async-done(((f32[64,16,128]{2,1,0:T(8,128)}), f32[64,16,128]{2,1,0:T(8,128)}, u32[]{:S(2)}, u32[]{:S(2)}) %all-to-all-start.2) | async-done | bytes 524320 | tf_op jit(solution)/shard_map/all_to_all | solution.py:319
  120.4 1.8 %shard_map.40 = f32[64,8,128]{2,1,0:T(8,128)} custom-call(f32[64,16,128]{2,1,0:T(8,128)} %all-to-all-done.2.refs_0_, f32[768,256]{1,0:T(8,128)S(1)} %get-tuple-element.24.refs_3_.refs_2_.refs_1_), custom_call_target="tpu_custom_call" | custom-call | flops 1000000 | bytes 1024 | tf_op jit(solution)/shard_map/pallas_call | solution.py:290
  122.2 6.6 %all-to-all-start.3 = ((f32[64,8,128]{2,1,0:T(8,128)}), f32[64,8,128]{2,1,0:T(8,128)}, u32[]{:S(2)}, u32[]{:S(2)}) async-start(f32[64,8,128]{2,1,0:T(8,128)} %shard_map.40), calls=%async_computation.3 | async-start | bytes 524288 | tf_op jit(solution)/shard_map/all_to_all | solution.py:319
  128.9 0.0 collective-permute-done.3.refs_4_.refs_3_
  128.9 0.0 copy-start.3
  128.9 3.2 %shard_map.37 = (f32[768,128]{1,0:T(8,128)}, f32[256,128]{1,0:T(8,128)S(1)}, f32[256,256]{1,0:T(8,128)S(1)}) custom-call(f32[64,16,128]{2,1,0:T(8,128)} %all-to-all-done.2.refs_0_, f32[384,256]{1,0:T(8,128)S(1)} %get-tuple-element.22.refs_3_.refs_1_.refs_0_, f32[384,256]{1,0:T(8,128)} %collective-permute-done.2.refs_4_.refs_2_.refs_1_, ...), custom_call_target="tpu_custom_call" | custom-call | flops 1000000 | bytes 1024 | tf_op jit(solution)/shard_map/pallas_call | solution.py:290
  132.1 0.0 copy-start.10
  132.1 0.0 collective-permute-start.5
  132.1 5.9 %shard_map.38 = (f32[384,128]{1,0:T(8,128)}, f32[384,128]{1,0:T(8,128)S(1)}) custom-call(s32[4,1]{1,0:T(4,128)S(1)} %copy.3.refs_0_, f32[256,256]{1,0:T(8,128)S(1)} %get-tuple-element.26.refs_1_), custom_call_target="tpu_custom_call" | custom-call | flops 1000000 | bytes 1024 | tf_op jit(solution)/shard_map/pallas_call | solution.py:290
  138.1 0.0 copy-done.10
  138.1 1.8 %collective-permute-start.6 = (f32[384,128]{1,0:T(8,128)}, f32[384,128]{1,0:T(8,128)}, u32[]{:S(2)}, u32[]{:S(2)}) collective-permute-start(f32[384,128]{1,0:T(8,128)} %get-tuple-element.33), channel_id=1, source_target_pairs={{7,0},{0,1},{1,2},{2,3},{3,4},{4,5},{5,6},{6,7},{15,8},{8,9},{9,10... | collective-permute-start | bytes 589832 | tf_op jit(solution)/shard_map/ppermute | solution.py:305
  139.9 0.0 copy-done.3
  139.9 4.2 %shard_map.39 = (f32[1024,128]{1,0:T(8,128)S(1)}, f32[1024,128]{1,0:T(8,128)S(1)}) custom-call(f32[384,256]{1,0:T(8,128)S(1)} %get-tuple-element.22.refs_3_.refs_1_.refs_0_, f32[384,256]{1,0:T(8,128)} %collective-permute-done.2.refs_4_.refs_2_.refs_1_, f32[768,256]{1,0:T(8,128)S(1)} %get-tuple-element.24.refs_3_.refs_2_.refs_1_, ...), custom_call_target="tpu_custom_call" | custom-call | flops 1000000 | bytes 1024 | tf_op jit(solution)/shard_map/pallas_call | solution.py:290
  144.0 0.0 copy-start.5
  144.0 0.8 copy-done.5
  144.8 0.7 copy-done.8
  145.5 0.0 all-to-all-done.3.refs_0_
  145.5 0.0 collective-permute-done.5.refs_4_
  145.5 1.2 copy-done.4
  146.7 1.0 copy-done.6
  147.8 0.9 copy-done.9
  148.7 0.9 copy-done.11
  149.6 4.1 %shard_map.41 = (f32[128,256]{1,0:T(8,128)S(1)}, f32[1024,128]{1,0:T(8,128)S(1)}) custom-call(f32[64,8,128]{2,1,0:T(8,128)} %all-to-all-done.3.refs_0_, f32[384,256]{1,0:T(8,128)S(1)} %get-tuple-element.22.refs_3_.refs_1_.refs_0_, f32[768,256]{1,0:T(8,128)S(1)} %get-tuple-element.24.refs_3_.refs_2_.refs_1_, ...), custom_call_target="tpu_custom_call" | custom-call | flops 1000000 | bytes 1024 | tf_op jit(solution)/shard_map/pallas_call | solution.py:290
  153.8 0.0 collective-permute-done.6.refs_3_
  153.8 4.6 %shard_map.42.refs_4_ = f32[256,256]{1,0:T(8,128)S(1)} custom-call(s32[4,1]{1,0:T(4,128)S(1)} %copy.3.refs_0_, f32[128,256]{1,0:T(8,128)S(1)} %get-tuple-element.34.refs_1_, f32[384,128]{1,0:T(8,128)S(1)} %copy-done.9, f32[384,128]{1,0:T(8,128)} %collective-permute-done.6.refs_3_), custom_call_target="tpu_custom_call" | custom-call | flops 1000000 | bytes 1024 | tf_op jit(solution)/shard_map/pallas_call | solution.py:290
  158.4 1.9 %shard_map.44 = f32[1024,128]{1,0:T(8,128)S(1)} custom-call(f32[1024,128]{1,0:T(8,128)S(1)} %copy-done.6, f32[1024,128]{1,0:T(8,128)S(1)} %get-tuple-element.29.refs_1_, f32[1024,128]{1,0:T(8,128)S(1)} %get-tuple-element.32.refs_2_, f32[384,128]{1,0:T(8,128)} %collective-permute-done.6.refs_3_, f32[256,256]{1,0:T(8,128)S(1)} %shard_map.42.refs_4_), custom_call_target="tpu_custom_call" | custom-call | flops 1000000 | bytes 1024 | tf_op jit(solution)/shard_map/pallas_call | solution.py:290
  160.3 0.0 collective-permute-start.7
  160.3 1.9 %shard_map.43 = f32[1024,128]{1,0:T(8,128)S(1)} custom-call(f32[1024,128]{1,0:T(8,128)S(1)} %copy-done.6, f32[1024,128]{1,0:T(8,128)S(1)} %get-tuple-element.29.refs_1_, f32[1024,128]{1,0:T(8,128)S(1)} %get-tuple-element.32.refs_2_, f32[384,128]{1,0:T(8,128)} %collective-permute-done.6.refs_3_, f32[256,256]{1,0:T(8,128)S(1)} %shard_map.42.refs_4_), custom_call_target="tpu_custom_call" | custom-call | flops 1000000 | bytes 1024 | tf_op jit(solution)/shard_map/pallas_call | solution.py:290
  162.2 7.9 %collective-permute-done.7 = f32[1024,128]{1,0:T(8,128)S(1)} collective-permute-done((f32[1024,128]{1,0:T(8,128)S(1)}, f32[1024,128]{1,0:T(8,128)S(1)}, u32[]{:S(2)}, u32[]{:S(2)}) %collective-permute-start.7) | collective-permute-done | bytes 524320 | tf_op jit(solution)/shard_map/ppermute | solution.py:305
  170.1 1.0 pad_maximum_fusion
  (5 shorter events, 0.0 us)
Async XLA Ops:
  0.0 15.8 %collective-permute-start = (f32[1024,256]{1,0:T(8,128)}, f32[1024,256]{1,0:T(8,128)}, u32[]{:S(2)}, u32[]{:S(2)}) collective-permute-start(f32[1024,256]{1,0:T(8,128)} %refs_5_.1), channel_id=1, source_target_pairs={{7,0},{0,1},{1,2},{2,3},{3,4},{4,5},{5,6},{6,7},{15,8},{8,9},{9,10... | collective-permute-start | bytes 3145736 | tf_op jit(solution)/shard_map/ppermute | solution.py:305
  0.0 1.2 copy-start
  15.8 20.0 %collective-permute-start.1 = (f32[1024,256]{1,0:T(8,128)}, f32[1024,256]{1,0:T(8,128)S(1)}, u32[]{:S(2)}, u32[]{:S(2)}) collective-permute-start(f32[1024,256]{1,0:T(8,128)} %collective-permute-done.refs_1_.refs_6_), channel_id=1, source_target_pairs={{7,0},{0,1},{1,2},{2,3},{3,4},{4,5},{5,6},{6,7},{15,8},{8,9},{9,10... | collective-permute-start | bytes 3145736 | tf_op jit(solution)/shard_map/ppermute | solution.py:305
  18.3 17.5 %copy-start.1 = (f32[1024,256]{1,0:T(8,128)S(1)}, f32[1024,256]{1,0:T(8,128)}, u32[]{:S(2)}) copy-start(f32[1024,256]{1,0:T(8,128)} %refs_5_.1) | copy-start | bytes 3145732
  19.1 36.4 %all-to-all-start = ((f32[64,16,128]{2,1,0:T(8,128)}), f32[64,16,128]{2,1,0:T(8,128)S(1)}, u32[]{:S(2)}, u32[]{:S(2)}) async-start(f32[64,16,128]{2,1,0:T(8,128)} %shard_map.30), calls=%async_computation | async-start | bytes 1048576 | tf_op jit(solution)/shard_map/all_to_all | solution.py:319
  35.7 26.5 %copy-start.2 = (f32[1024,256]{1,0:T(8,128)}, f32[1024,256]{1,0:T(8,128)S(1)}, u32[]{:S(2)}) copy-start(f32[1024,256]{1,0:T(8,128)S(1)} %collective-permute-done.1.refs_1_.refs_7_) | copy-start | bytes 3145732
  55.7 0.9 copy-start.7
  56.6 5.7 %copy-start.12 = (s32[4,1]{0,1:T(1,128)S(1)}, s32[4,1]{0,1:T(1,128)}, u32[]{:S(2)}) copy-start(s32[4,1]{0,1:T(1,128)} %param.3) | copy-start | bytes 52
  56.6 29.6 %all-to-all-start.1 = ((f32[64,24,128]{2,1,0:T(8,128)}), f32[64,24,128]{2,1,0:T(8,128)S(1)}, u32[]{:S(2)}, u32[]{:S(2)}) async-start(f32[64,24,128]{2,1,0:T(8,128)} %copy-done.7), calls=%async_computation.1 | async-start | bytes 1572864 | tf_op jit(solution)/shard_map/all_to_all | solution.py:319
  62.2 29.2 %collective-permute-start.4 = (f32[1024,256]{1,0:T(8,128)S(1)}, f32[1024,256]{1,0:T(8,128)}, u32[]{:S(2)}, u32[]{:S(2)}) collective-permute-start(f32[1024,256]{1,0:T(8,128)S(1)} %collective-permute-done.1.refs_1_.refs_7_), channel_id=1, source_target_pairs={{7,0},{0,1},{1,2},{2,3},{3,4},{4,5},{5,6},{6,7},{15,8},{8,9},{9,10... | collective-permute-start | bytes 3145736 | tf_op jit(solution)/shard_map/ppermute | solution.py:305
  91.4 9.7 %collective-permute-start.2 = (f32[384,256]{1,0:T(8,128)S(1)}, f32[384,256]{1,0:T(8,128)}, u32[]{:S(2)}, u32[]{:S(2)}) collective-permute-start(f32[384,256]{1,0:T(8,128)S(1)} %get-tuple-element.22.refs_3_.refs_1_.refs_0_), channel_id=1, source_target_pairs={{7,0},{0,1},{1,2},{2,3},{3,4},{4,5},{5,6},{6,7},{15,8},{8,9},{9,10... | collective-permute-start | bytes 1179656 | tf_op jit(solution)/shard_map/ppermute | solution.py:305
  94.8 25.6 %all-to-all-start.2 = ((f32[64,16,128]{2,1,0:T(8,128)}), f32[64,16,128]{2,1,0:T(8,128)}, u32[]{:S(2)}, u32[]{:S(2)}) async-start(f32[64,16,128]{2,1,0:T(8,128)} %shard_map.36), calls=%async_computation.2 | async-start | bytes 1048576 | tf_op jit(solution)/shard_map/all_to_all | solution.py:319
  107.0 21.9 %collective-permute-start.3 = (f32[768,256]{1,0:T(8,128)S(1)}, f32[768,256]{1,0:T(8,128)S(1)}, u32[]{:S(2)}, u32[]{:S(2)}) collective-permute-start(f32[768,256]{1,0:T(8,128)S(1)} %get-tuple-element.24.refs_3_.refs_2_.refs_1_), channel_id=1, source_target_pairs={{7,0},{0,1},{1,2},{2,3},{3,4},{4,5},{5,6},{6,7},{15,8},{8,9},{9,10... | collective-permute-start | bytes 2359304 | tf_op jit(solution)/shard_map/ppermute | solution.py:305
  122.2 23.3 %all-to-all-start.3 = ((f32[64,8,128]{2,1,0:T(8,128)}), f32[64,8,128]{2,1,0:T(8,128)}, u32[]{:S(2)}, u32[]{:S(2)}) async-start(f32[64,8,128]{2,1,0:T(8,128)} %shard_map.40), calls=%async_computation.3 | async-start | bytes 524288 | tf_op jit(solution)/shard_map/all_to_all | solution.py:319
  128.9 11.0 %copy-start.3 = (f32[1024,256]{1,0:T(8,128)S(1)}, f32[1024,256]{1,0:T(8,128)}, u32[]{:S(2)}) copy-start(f32[1024,256]{1,0:T(8,128)} %copy-done.2) | copy-start | bytes 3145732
  132.1 5.9 %copy-start.10 = (f32[256,128]{1,0:T(8,128)}, f32[256,128]{1,0:T(8,128)S(1)}, u32[]{:S(2)}) copy-start(f32[256,128]{1,0:T(8,128)S(1)} %get-tuple-element.31.refs_5_) | copy-start | bytes 393220
  132.1 13.4 %collective-permute-start.5 = (f32[768,128]{1,0:T(8,128)}, f32[768,128]{1,0:T(8,128)}, u32[]{:S(2)}, u32[]{:S(2)}) collective-permute-start(f32[768,128]{1,0:T(8,128)} %get-tuple-element.30), channel_id=1, source_target_pairs={{7,0},{0,1},{1,2},{2,3},{3,4},{4,5},{5,6},{6,7},{15,8},{8,9},{9,10... | collective-permute-start | bytes 1179656 | tf_op jit(solution)/shard_map/ppermute | solution.py:305
  138.1 15.7 %collective-permute-start.6 = (f32[384,128]{1,0:T(8,128)}, f32[384,128]{1,0:T(8,128)}, u32[]{:S(2)}, u32[]{:S(2)}) collective-permute-start(f32[384,128]{1,0:T(8,128)} %get-tuple-element.33), channel_id=1, source_target_pairs={{7,0},{0,1},{1,2},{2,3},{3,4},{4,5},{5,6},{6,7},{15,8},{8,9},{9,10... | collective-permute-start | bytes 589832 | tf_op jit(solution)/shard_map/ppermute | solution.py:305
  144.0 0.8 copy-start.5
  144.8 0.7 copy-start.8
  145.5 1.2 copy-start.4
  146.7 1.0 copy-start.6
  147.8 0.9 copy-start.9
  148.7 0.9 copy-start.11
  160.3 9.8 %collective-permute-start.7 = (f32[1024,128]{1,0:T(8,128)S(1)}, f32[1024,128]{1,0:T(8,128)S(1)}, u32[]{:S(2)}, u32[]{:S(2)}) collective-permute-start(f32[1024,128]{1,0:T(8,128)S(1)} %shard_map.44), channel_id=1, source_target_pairs={{7,0},{0,1},{1,2},{2,3},{3,4},{4,5},{5,6},{6,7},{15,8},{8,9},{9,10... | collective-permute-start | bytes 1572872 | tf_op jit(solution)/shard_map/ppermute | solution.py:305

commit v4 on v3

--- a/solution.py
+++ b/solution.py
@@ -217,26 +217,9 @@
     lax.fori_loop(0, count // step, one, 0)
 
 
-def columns_kernel(out0, in0, out1, in1, own2, x0, x1, x2, kept_cols, left_cols, weights):
-    q2_kk, q2_mk, q0_pp = own2[:HALF], own2[HALF:N], in1[2 * N :]
-    p1_kk, p1_mk, p1_km, p1_mm = in1[:HALF, :HALF], in1[HALF:N, :HALF], in1[:HALF, HALF:], in1[HALF:N, HALF:]
-    weights[:, :HALF] = cross_dot(out0[:N, :HALF], cross_dot(out1[:HALF, :HALF], q2_kk))
-    travelled = cross_dot(in0[:N, HALF:], cross_dot(out1[HALF:N, :HALF], q2_kk))
-    weights[:, HALF:N] = travelled + cross_dot(in0[:N, :HALF], cross_dot(p1_km, q2_mk))
-    weights[:, N : N + HALF] = cross_dot(in0[:N, :HALF], p1_kk)
-    weights[:, N + HALF : 2 * N] = cross_dot(q0_pp[:, HALF:], cross_dot(p1_mm, q2_mk))
-    weights[:, 2 * N :] = cross_dot(q0_pp[:, HALF:], p1_mk)
-
-    def some_rows(rows):
-        both = cross_dot(x1[rows, :], weights[:, HALF : N + HALF]) + cross_dot(x2[rows, :], weights[:, N + HALF :])
-        kept_cols[rows, :] = cross_dot(x0[rows, :], weights[:, :HALF]) + both[:, :HALF]
-        left_cols[rows, :] = both[:, HALF:]
-
-    in_chunks(kept_cols.shape[0], some_rows)
-
-
-def cross3_kernel(received, out0, out1, in1, in2a, kept, own2, x2, x3, left_of_cross, right_cols, weights):
-    q0_k, q1_k, q2_k = out0[:N, :HALF], out1[:N, :HALF], own2[:N]
+def shadow_kernel(received, out0, in0, out1, in1, in2a, kept, own2, x0, x1, x2, x3, *refs):
+    left_of_cross, kept_cols, left_cols, right_cols, weights = refs
+    q0_k, q1_k, q2_k, q0_pp = out0[:N, :HALF], out1[:N, :HALF], own2[:N], in1[2 * N :]
     q1_pp, q0_ppp = in2a[N : 2 * N], in2a[2 * N :]
     r3 = cross_dot(q0_k, cross_dot(square_of(received, 0), q0_ppp), (0, 0))
     upper = jnp.concatenate([kept[HALF:], r3], axis=1)
@@ -245,13 +228,26 @@
     upper = jnp.concatenate([kept[:HALF], t], axis=1)
     lower = jnp.concatenate([in1[N : N + HALF, :HALF], in2a[:HALF]], axis=1)
     left_of_cross[...] = cross_dot(q2_k, jnp.concatenate([upper, lower], axis=0), (0, 0))
-    weights[:, :HALF] = cross_dot(in1[2 * N :, :HALF], q1_pp[:HALF])
-    weights[:, HALF:] = cross_dot(q0_ppp, q1_pp[HALF:])
+
+    q2_kk, q2_mk = own2[:HALF], own2[HALF:N]
+    p1_kk, p1_mk, p1_km, p1_mm = in1[:HALF, :HALF], in1[HALF:N, :HALF], in1[:HALF, HALF:], in1[HALF:N, HALF:]
+    weights[:, :HALF] = cross_dot(q0_k, cross_dot(out1[:HALF, :HALF], q2_kk))
+    travelled = cross_dot(in0[:N, HALF:], cross_dot(out1[HALF:N, :HALF], q2_kk))
+    weights[:, HALF:N] = travelled + cross_dot(in0[:N, :HALF], cross_dot(p1_km, q2_mk))
+    weights[:, N : N + HALF] = cross_dot(in0[:N, :HALF], p1_kk)
+    weights[:, N + HALF : 2 * N] = cross_dot(q0_pp[:, HALF:], cross_dot(p1_mm, q2_mk))
+    weights[:, 2 * N : 2 * N + HALF] = cross_dot(q0_pp[:, HALF:], p1_mk)
+    weights[:, 2 * N + HALF : 3 * N] = cross_dot(q0_pp[:, :HALF], q1_pp[:HALF])
+    weights[:, 3 * N :] = cross_dot(q0_ppp, q1_pp[HALF:])
 
     def some_rows(rows):
-        right_cols[rows, :] = cross_dot(x2[rows, :], weights[:, :HALF]) + cross_dot(x3[rows, :], weights[:, HALF:])
-
-    in_chunks(right_cols.shape[0], some_rows)
+        both = cross_dot(x1[rows, :], weights[:, HALF : N + HALF])
+        three = cross_dot(x2[rows, :], weights[:, N + HALF : 3 * N])
+        kept_cols[rows, :] = cross_dot(x0[rows, :], weights[:, :HALF]) + both[:, :HALF] + three[:, :HALF]
+        left_cols[rows, :] = both[:, HALF:] + three[:, HALF:N]
+        right_cols[rows, :] = three[:, N:] + cross_dot(x3[rows, :], weights[:, 3 * N :])
+
+    in_chunks(kept_cols.shape[0], some_rows)
 
 
 def last_kernel(place, kept_cols, left_cols, right_cols, in2b, q3, out):
@@ -324,8 +320,11 @@
     before2 = onward(before1)
     with_c1 = exchange(received, 0, products(before2))
     before3 = onward(before2)
-    with_c2 = exchange(with_c1, 2, products(before3))
-    out0, h0 = run(step0_kernel, [(N + HALF, N), block], sender_slot, with_c1, scratch=JACOBI_PARTS)
+    parts3 = products(before3)
+    with_c2 = exchange(with_c1, 2, parts3)
+    out0, h0 = run(
+        step0_kernel, [(N + HALF, N), block], sender_slot, with_c1, scratch=JACOBI_PARTS, last=(parts3,)
+    )
     in0 = onward(out0)
     out1, carried = run(
         step1_kernel,
@@ -344,20 +343,12 @@
     out2b, own2 = run(step2_kernel, [(N + HALF, HALF)] * 2, sender_slot, gram2, scratch=JACOBI_PARTS)
     in2b = onward(out2b)
     rows = matrix.shape[0]
-    kept_cols, left_cols = run(
-        columns_kernel,
-        [(rows, HALF)] * 2,
-        *(out0, in0, out1, in1, own2, matrix, before1, before2),
-        scratch=[pltpu.VMEM((N, 2 * N + HALF), jnp.float32)],
-    )
-    left_of_cross, right_cols = run(
-        cross3_kernel,
-        [(HALF, N), (rows, HALF)],
-        *(with_c3, out0, out1, in1, in2a, kept, own2, before2, before3),
-        scratch=[pltpu.VMEM((N, N), jnp.float32)],
-        last=(kept_cols,),
-    )
-    columns = (kept_cols, left_cols, right_cols)
+    left_of_cross, *columns = run(
+        shadow_kernel,
+        [(HALF, N)] + [(rows, HALF)] * 3,
+        *(with_c3, out0, in0, out1, in1, in2a, kept, own2, matrix, before1, before2, before3),
+        scratch=[pltpu.VMEM((N, 3 * N + HALF), jnp.float32)],
+    )
     (q3,) = run(step3_kernel, [square], sender_slot, left_of_cross, own2, in2b, scratch=JACOBI_PARTS)
 
     def last_columns(place):

time: 172 us -> 166 us (0.965)
  Pallas kernels: 48.2 us -> 40.4 us
  local copies, waits for them, and re-layouts: 7.78 us -> 11.8 us
    all_to_all x4, waiting for transfers between devices: 54.6 us -> 37.5 us  [exchange(): return lax.all_to_all(pieces, 'row', 0, 0, tiled=True)]
    ppermute x8, waiting for transfers between devices: 21.1 us -> 37.6 us  [onward(): lax.ppermute(values, 'blk', [((i - places) % devices, i) for i in range(d...]
    pallas_call x17 -> x16, Pallas kernels: 48.2 us -> 40.4 us  [run(): pl.pallas_call(body, out_shape=[jax.ShapeDtypeStruct(shape, jnp.float32)...]
    unnamed x27 -> x39, local copies, waits for them, and re-layouts: 7.78 us -> 11.8 us
  transfers between devices with their start and end apart: 12 -> 12, of which waited for: 5 -> 8; matrix products, arithmetic and copies ran while one was open for 0% -> 0% of each run, Pallas kernels for 24% -> 17%
where the time goes in v4:
time: 166 us; the launch traced here: 165 us
  waiting for transfers between devices  75.1 us (45%)
  Pallas kernels  40.4 us (24%)
  starting transfers between devices  36.9 us (22%)
  local copies, waits for them, and re-layouts  11.8 us (7%)
    pallas_call x16, Pallas kernels, run(): pl.pallas_call(body, out_shape=[jax.ShapeDtypeStruct(shape, jnp.float32)...  40.4 us
    ppermute x8, waiting for transfers between devices, onward(): lax.ppermute(values, 'blk', [((i - places) % devices, i) for i in range(d...  37.6 us
    all_to_all x4, waiting for transfers between devices, exchange(): return lax.all_to_all(pieces, 'row', 0, 0, tiled=True)  37.5 us
    all_to_all x4, starting transfers between devices, exchange(): return lax.all_to_all(pieces, 'row', 0, 0, tiled=True)  35.1 us
    unnamed x39, local copies, waits for them, and re-layouts  11.8 us
  transfers between devices with their start and end apart: 12, of which 8 were waited for; matrix products, arithmetic and copies ran while one was open for 0% of the time, Pallas kernels for 17%

profile of v4, /device:TPU:8, one launch (start us, length us, event | category | flops | bytes accessed | tf_op | source)
XLA Modules:
  0.0 165.5 jit_solution(7781824807858203864)
XLA Ops:
  0.0 0.0 collective-permute-start
  0.0 1.2 copy-done
  1.2 1.3 shard_map.28.refs_0_
  2.5 13.1 %collective-permute-done.refs_1_.refs_9_ = f32[1024,256]{1,0:T(8,128)S(1)} collective-permute-done((f32[1024,256]{1,0:T(8,128)}, f32[1024,256]{1,0:T(8,128)S(1)}, u32[]{:S(2)}, u32[]{:S(2)}) %collective-permute-start) | collective-permute-done | bytes 1048608 | tf_op jit(solution)/shard_map/ppermute | solution.py:301
  15.6 0.0 collective-permute-start.1
  15.7 1.3 shard_map.29.refs_1_
  17.0 0.0 copy-done.2
  17.0 0.0 copy-start.1
  17.0 0.0 copy-start.11
  17.0 0.8 copy-done.11
  17.8 16.8 %all-to-all-start = ((f32[64,16,128]{2,1,0:T(8,128)}), f32[64,16,128]{2,1,0:T(8,128)}, u32[]{:S(2)}, u32[]{:S(2)}) async-start(f32[64,16,128]{2,1,0:T(8,128)} %copy-done.11), calls=%async_computation | async-start | bytes 1048576 | tf_op jit(solution)/shard_map/all_to_all | solution.py:315
  34.6 0.0 collective-permute-done.1.refs_1_.refs_10_
  34.6 0.0 copy-done.1
  34.7 0.0 copy-start.4
  34.7 1.3 shard_map.31.refs_1_
  36.0 18.3 %all-to-all-done.refs_0_ = f32[64,16,128]{2,1,0:T(8,128)} async-done(((f32[64,16,128]{2,1,0:T(8,128)}), f32[64,16,128]{2,1,0:T(8,128)}, u32[]{:S(2)}, u32[]{:S(2)}) %all-to-all-start) | async-done | bytes 524320 | tf_op jit(solution)/shard_map/all_to_all | solution.py:315
  54.3 1.1 shard_map.32
  55.5 0.0 copy-start.9
  55.5 0.9 copy-done.9
  56.4 5.6 %all-to-all-start.1 = ((f32[64,24,128]{2,1,0:T(8,128)}), f32[64,24,128]{2,1,0:T(8,128)S(1)}, u32[]{:S(2)}, u32[]{:S(2)}) async-start(f32[64,24,128]{2,1,0:T(8,128)} %copy-done.9), calls=%async_computation.1 | async-start | bytes 1572864 | tf_op jit(solution)/shard_map/all_to_all | solution.py:315
  62.0 0.0 copy-done.4
  62.0 0.0 collective-permute-start.2
  62.0 0.0 copy-done.18
  62.0 0.1 copy.4.refs_0_
  62.1 15.4 %collective-permute-done.2.refs_1_.refs_11_ = f32[1024,256]{1,0:T(8,128)} collective-permute-done((f32[1024,256]{1,0:T(8,128)S(1)}, f32[1024,256]{1,0:T(8,128)}, u32[]{:S(2)}, u32[]{:S(2)}) %collective-permute-start.2) | collective-permute-done | bytes 1048608 | tf_op jit(solution)/shard_map/ppermute | solution.py:301
  77.5 2.5 %shard_map.33.refs_1_.refs_2_ = f32[256,256]{1,0:T(8,128)S(1)} custom-call(f32[1024,256]{1,0:T(8,128)S(1)} %copy-done.1, f32[1024,256]{1,0:T(8,128)} %collective-permute-done.2.refs_1_.refs_11_), custom_call_target="tpu_custom_call" | custom-call | flops 1000000 | bytes 1024 | tf_op jit(solution)/shard_map/pallas_call | solution.py:286
  80.1 5.9 %all-to-all-done.1.refs_0_.refs_1_ = f32[64,24,128]{2,1,0:T(8,128)S(1)} async-done(((f32[64,24,128]{2,1,0:T(8,128)}), f32[64,24,128]{2,1,0:T(8,128)S(1)}, u32[]{:S(2)}, u32[]{:S(2)}) %all-to-all-start.1) | async-done | bytes 786464 | tf_op jit(solution)/shard_map/all_to_all | solution.py:315
  85.9 5.3 %shard_map.35 = (f32[384,256]{1,0:T(8,128)S(1)}, f32[128,128]{1,0:T(8,128)S(1)}) custom-call(s32[4,1]{1,0:T(4,128)S(1)} %copy.4.refs_0_, f32[64,24,128]{2,1,0:T(8,128)S(1)} %all-to-all-done.1.refs_0_.refs_1_, f32[256,256]{1,0:T(8,128)S(1)} %shard_map.33.refs_1_.refs_2_), custom_call_target="tpu_custom_call" | custom-call | flops 1000000 | bytes 1024 | tf_op jit(solution)/shard_map/pallas_call | solution.py:286
  91.2 0.0 copy-start.16
  91.2 0.0 collective-permute-start.3
  91.2 0.1 shard_map.34
  91.3 0.5 copy-done.16
  91.8 0.8 copy-done.10
  92.6 6.9 %all-to-all-start.2 = ((f32[64,16,128]{2,1,0:T(8,128)}), f32[64,16,128]{2,1,0:T(8,128)S(1)}, u32[]{:S(2)}, u32[]{:S(2)}) async-start(f32[64,16,128]{2,1,0:T(8,128)} %copy-done.10), calls=%async_computation.2 | async-start | bytes 1048576 | tf_op jit(solution)/shard_map/all_to_all | solution.py:315
  99.4 0.2 collective-permute-done.3.refs_4_.refs_2_
  99.6 0.7 copy-done.6
  100.3 1.0 copy-done.7
  101.3 0.8 copy-done.17
  102.2 5.4 %shard_map.36 = (f32[768,256]{1,0:T(8,128)S(1)}, f32[128,256]{1,0:T(8,128)S(1)}) custom-call(s32[4,1]{1,0:T(4,128)S(1)} %copy.4.refs_0_, f32[64,24,128]{2,1,0:T(8,128)S(1)} %all-to-all-done.1.refs_0_.refs_1_, f32[128,128]{1,0:T(8,128)S(1)} %copy-done.17, f32[384,256]{1,0:T(8,128)S(1)} %get-tuple-element.23.refs_3_.refs_1_, f32[384,256]{1,0:T(8,128)S(1)} %copy-done.7), custom_call_target="tpu_custom_call" | custom-call | flops 1000000 | bytes 1024 | tf_op jit(solution)/shard_map/pallas_call | solution.py:286
  107.6 0.0 copy-start.14
  107.6 0.6 copy-done.14
  108.3 0.0 collective-permute-start.4
  108.3 11.1 %all-to-all-done.2.refs_0_ = f32[64,16,128]{2,1,0:T(8,128)S(1)} async-done(((f32[64,16,128]{2,1,0:T(8,128)}), f32[64,16,128]{2,1,0:T(8,128)S(1)}, u32[]{:S(2)}, u32[]{:S(2)}) %all-to-all-start.2) | async-done | bytes 524320 | tf_op jit(solution)/shard_map/all_to_all | solution.py:315
  119.4 0.8 shard_map.37
  120.2 5.8 %all-to-all-start.3 = ((f32[64,8,128]{2,1,0:T(8,128)}), f32[64,8,128]{2,1,0:T(8,128)}, u32[]{:S(2)}, u32[]{:S(2)}) async-start(f32[64,8,128]{2,1,0:T(8,128)} %shard_map.37), calls=%async_computation.3 | async-start | bytes 524288 | tf_op jit(solution)/shard_map/all_to_all | solution.py:315
  126.0 0.0 collective-permute-done.4.refs_4_
  126.0 0.9 copy-done.15
  126.9 3.1 %shard_map.38 = (f32[768,128]{1,0:T(8,128)}, f32[256,128]{1,0:T(8,128)S(1)}, f32[256,256]{1,0:T(8,128)S(1)}) custom-call(f32[64,16,128]{2,1,0:T(8,128)S(1)} %all-to-all-done.2.refs_0_, f32[384,256]{1,0:T(8,128)S(1)} %get-tuple-element.23.refs_3_.refs_1_, f32[384,256]{1,0:T(8,128)S(1)} %copy-done.8, f32[768,256]{1,0:T(8,128)S(1)} %get-tuple-element.24.refs_1_.refs_3_, ...), custom_call_target="tpu_custom_call" | custom-call | flops 1000000 | bytes 1024 | tf_op jit(solution)/shard_map/pallas_call | solution.py:286
  130.0 0.0 collective-permute-start.5
  130.0 5.9 %shard_map.39 = (f32[384,128]{1,0:T(8,128)}, f32[384,128]{1,0:T(8,128)S(1)}) custom-call(s32[4,1]{1,0:T(4,128)S(1)} %copy.4.refs_0_, f32[256,256]{1,0:T(8,128)S(1)} %get-tuple-element.28.refs_1_), custom_call_target="tpu_custom_call" | custom-call | flops 1000000 | bytes 1024 | tf_op jit(solution)/shard_map/pallas_call | solution.py:286
  135.9 1.8 %collective-permute-start.6 = (f32[384,128]{1,0:T(8,128)}, f32[384,128]{1,0:T(8,128)S(1)}, u32[]{:S(2)}, u32[]{:S(2)}) collective-permute-start(f32[384,128]{1,0:T(8,128)} %get-tuple-element.33), channel_id=1, source_target_pairs={{7,0},{0,1},{1,2},{2,3},{3,4},{4,5},{5,6},{6,7},{15,8},{8,9},{9,10... | collective-permute-start | bytes 589832 | tf_op jit(solution)/shard_map/ppermute | solution.py:301
  137.8 2.2 %all-to-all-done.3.refs_0_ = f32[64,8,128]{2,1,0:T(8,128)} async-done(((f32[64,8,128]{2,1,0:T(8,128)}), f32[64,8,128]{2,1,0:T(8,128)}, u32[]{:S(2)}, u32[]{:S(2)}) %all-to-all-start.3) | async-done | bytes 262176 | tf_op jit(solution)/shard_map/all_to_all | solution.py:315
  139.9 0.0 collective-permute-done.5.refs_5_
  139.9 1.2 copy-done.3
  141.1 1.2 copy-done.5
  142.4 0.9 copy-done.13
  143.3 6.1 %shard_map.40 = (f32[128,256]{1,0:T(8,128)S(1)}, f32[1024,128]{1,0:T(8,128)S(1)}, f32[1024,128]{1,0:T(8,128)S(1)}, f32[1024,128]{1,0:T(8,128)S(1)}) custom-call(f32[64,8,128]{2,1,0:T(8,128)} %all-to-all-done.3.refs_0_, f32[384,256]{1,0:T(8,128)S(1)} %get-tuple-element.23.refs_3_.refs_1_, f32[384,256]{1,0:T(8,128)S(1)} %copy-done.8, ...), custom_call_target="tpu_custom_call" | custom-call | flops 1000000 | bytes 1024 | tf_op jit(solution)/shard_map/pallas_call | solution.py:286
  149.4 0.0 collective-permute-done.6.refs_3_
  149.4 4.3 %shard_map.41.refs_4_ = f32[256,256]{1,0:T(8,128)S(1)} custom-call(s32[4,1]{1,0:T(4,128)S(1)} %copy.4.refs_0_, f32[128,256]{1,0:T(8,128)S(1)} %get-tuple-element.34.refs_1_, f32[384,128]{1,0:T(8,128)S(1)} %get-tuple-element.29.refs_7_.refs_2_, f32[384,128]{1,0:T(8,128)S(1)} %collective-permute-done.6.refs_3_), custom_call_target="tpu_custom_call" | custom-call | flops 1000000 | bytes 1024 | tf_op jit(solution)/shard_map/pallas_call | solution.py:286
  153.6 1.0 shard_map.43
  154.6 0.0 collective-permute-start.7
  154.6 1.0 shard_map.42
  155.6 8.8 %collective-permute-done.7 = f32[1024,128]{1,0:T(8,128)S(1)} collective-permute-done((f32[1024,128]{1,0:T(8,128)S(1)}, f32[1024,128]{1,0:T(8,128)S(1)}, u32[]{:S(2)}, u32[]{:S(2)}) %collective-permute-start.7) | collective-permute-done | bytes 524320 | tf_op jit(solution)/shard_map/ppermute | solution.py:301
  164.4 1.0 pad_maximum_fusion
  (16 shorter events, 0.1 us)
Async XLA Ops:
  0.0 15.6 %collective-permute-start = (f32[1024,256]{1,0:T(8,128)}, f32[1024,256]{1,0:T(8,128)S(1)}, u32[]{:S(2)}, u32[]{:S(2)}) collective-permute-start(f32[1024,256]{1,0:T(8,128)} %refs_8_.1), channel_id=1, source_target_pairs={{7,0},{0,1},{1,2},{2,3},{3,4},{4,5},{5,6},{6,7},{15,8},{8,9},{9,10... | collective-permute-start | bytes 3145736 | tf_op jit(solution)/shard_map/ppermute | solution.py:301
  0.0 1.2 copy-start
  15.6 1.3 copy-start.2
  15.6 19.0 %collective-permute-start.1 = (f32[1024,256]{1,0:T(8,128)S(1)}, f32[1024,256]{1,0:T(8,128)S(1)}, u32[]{:S(2)}, u32[]{:S(2)}) collective-permute-start(f32[1024,256]{1,0:T(8,128)S(1)} %collective-permute-done.refs_1_.refs_9_), channel_id=1, source_target_pairs={{7,0},{0,1},{1,2},{2,3},{3,4},{4,5},{5,6},{6,7},{15,8},{8,9},{9,10... | collective-permute-start | bytes 3145736 | tf_op jit(solution)/shard_map/ppermute | solution.py:301
  17.0 17.7 %copy-start.1 = (f32[1024,256]{1,0:T(8,128)S(1)}, f32[1024,256]{1,0:T(8,128)}, u32[]{:S(2)}) copy-start(f32[1024,256]{1,0:T(8,128)} %refs_8_.1) | copy-start | bytes 3145732
  17.0 0.8 copy-start.11
  17.8 36.5 %all-to-all-start = ((f32[64,16,128]{2,1,0:T(8,128)}), f32[64,16,128]{2,1,0:T(8,128)}, u32[]{:S(2)}, u32[]{:S(2)}) async-start(f32[64,16,128]{2,1,0:T(8,128)} %copy-done.11), calls=%async_computation | async-start | bytes 1048576 | tf_op jit(solution)/shard_map/all_to_all | solution.py:315
  34.7 27.3 %copy-start.4 = (f32[1024,256]{1,0:T(8,128)}, f32[1024,256]{1,0:T(8,128)S(1)}, u32[]{:S(2)}) copy-start(f32[1024,256]{1,0:T(8,128)S(1)} %collective-permute-done.1.refs_1_.refs_10_) | copy-start | bytes 3145732
  55.5 0.9 copy-start.9
  56.4 5.7 %copy-start.18 = (s32[4,1]{0,1:T(1,128)S(1)}, s32[4,1]{0,1:T(1,128)}, u32[]{:S(2)}) copy-start(s32[4,1]{0,1:T(1,128)} %param.3) | copy-start | bytes 52
  56.4 29.6 %all-to-all-start.1 = ((f32[64,24,128]{2,1,0:T(8,128)}), f32[64,24,128]{2,1,0:T(8,128)S(1)}, u32[]{:S(2)}, u32[]{:S(2)}) async-start(f32[64,24,128]{2,1,0:T(8,128)} %copy-done.9), calls=%async_computation.1 | async-start | bytes 1572864 | tf_op jit(solution)/shard_map/all_to_all | solution.py:315
  62.0 15.6 %collective-permute-start.2 = (f32[1024,256]{1,0:T(8,128)S(1)}, f32[1024,256]{1,0:T(8,128)}, u32[]{:S(2)}, u32[]{:S(2)}) collective-permute-start(f32[1024,256]{1,0:T(8,128)S(1)} %collective-permute-done.1.refs_1_.refs_10_), channel_id=1, source_target_pairs={{7,0},{0,1},{1,2},{2,3},{3,4},{4,5},{5,6},{6,7},{15,8},{8,9},{9,10... | collective-permute-start | bytes 3145736 | tf_op jit(solution)/shard_map/ppermute | solution.py:301
  91.2 0.6 copy-start.16
  91.2 8.4 %collective-permute-start.3 = (f32[384,256]{1,0:T(8,128)S(1)}, f32[384,256]{1,0:T(8,128)S(1)}, u32[]{:S(2)}, u32[]{:S(2)}) collective-permute-start(f32[384,256]{1,0:T(8,128)S(1)} %get-tuple-element.23.refs_3_.refs_1_), channel_id=1, source_target_pairs={{7,0},{0,1},{1,2},{2,3},{3,4},{4,5},{5,6},{6,7},{15,8},{8,9},{9,10... | collective-permute-start | bytes 1179656 | tf_op jit(solution)/shard_map/ppermute | solution.py:301
  91.8 0.8 copy-start.10
  92.6 26.8 %all-to-all-start.2 = ((f32[64,16,128]{2,1,0:T(8,128)}), f32[64,16,128]{2,1,0:T(8,128)S(1)}, u32[]{:S(2)}, u32[]{:S(2)}) async-start(f32[64,16,128]{2,1,0:T(8,128)} %copy-done.10), calls=%async_computation.2 | async-start | bytes 1048576 | tf_op jit(solution)/shard_map/all_to_all | solution.py:315
  99.6 0.7 copy-start.6
  100.3 1.0 copy-start.7
  101.3 0.8 copy-start.17
  107.6 0.7 copy-start.14
  108.3 17.7 %collective-permute-start.4 = (f32[768,256]{1,0:T(8,128)S(1)}, f32[768,256]{1,0:T(8,128)}, u32[]{:S(2)}, u32[]{:S(2)}) collective-permute-start(f32[768,256]{1,0:T(8,128)S(1)} %get-tuple-element.24.refs_1_.refs_3_), channel_id=1, source_target_pairs={{7,0},{0,1},{1,2},{2,3},{3,4},{4,5},{5,6},{6,7},{15,8},{8,9},{9,10... | collective-permute-start | bytes 2359304 | tf_op jit(solution)/shard_map/ppermute | solution.py:301
  120.2 5.8 %copy-start.8 = (f32[384,256]{1,0:T(8,128)S(1)}, f32[384,256]{1,0:T(8,128)}, u32[]{:S(2)}) copy-start(f32[384,256]{1,0:T(8,128)} %copy-done.6) | copy-start | bytes 1179652
  120.2 19.7 %all-to-all-start.3 = ((f32[64,8,128]{2,1,0:T(8,128)}), f32[64,8,128]{2,1,0:T(8,128)}, u32[]{:S(2)}, u32[]{:S(2)}) async-start(f32[64,8,128]{2,1,0:T(8,128)} %shard_map.37), calls=%async_computation.3 | async-start | bytes 524288 | tf_op jit(solution)/shard_map/all_to_all | solution.py:315
  126.0 0.9 copy-start.15
  130.0 5.9 %copy-start.12 = (f32[256,128]{1,0:T(8,128)}, f32[256,128]{1,0:T(8,128)S(1)}, u32[]{:S(2)}) copy-start(f32[256,128]{1,0:T(8,128)S(1)} %get-tuple-element.27.refs_6_) | copy-start | bytes 393220
  130.0 9.9 %collective-permute-start.5 = (f32[768,128]{1,0:T(8,128)}, f32[768,128]{1,0:T(8,128)S(1)}, u32[]{:S(2)}, u32[]{:S(2)}) collective-permute-start(f32[768,128]{1,0:T(8,128)} %get-tuple-element.26), channel_id=1, source_target_pairs={{7,0},{0,1},{1,2},{2,3},{3,4},{4,5},{5,6},{6,7},{15,8},{8,9},{9,10... | collective-permute-start | bytes 1179656 | tf_op jit(solution)/shard_map/ppermute | solution.py:301
  135.9 13.4 %collective-permute-start.6 = (f32[384,128]{1,0:T(8,128)}, f32[384,128]{1,0:T(8,128)S(1)}, u32[]{:S(2)}, u32[]{:S(2)}) collective-permute-start(f32[384,128]{1,0:T(8,128)} %get-tuple-element.33), channel_id=1, source_target_pairs={{7,0},{0,1},{1,2},{2,3},{3,4},{4,5},{5,6},{6,7},{15,8},{8,9},{9,10... | collective-permute-start | bytes 589832 | tf_op jit(solution)/shard_map/ppermute | solution.py:301
  139.9 1.2 copy-start.3
  141.1 1.2 copy-start.5
  142.4 0.9 copy-start.13
  154.6 9.8 %collective-permute-start.7 = (f32[1024,128]{1,0:T(8,128)S(1)}, f32[1024,128]{1,0:T(8,128)S(1)}, u32[]{:S(2)}, u32[]{:S(2)}) collective-permute-start(f32[1024,128]{1,0:T(8,128)S(1)} %shard_map.43), channel_id=1, source_target_pairs={{7,0},{0,1},{1,2},{2,3},{3,4},{4,5},{5,6},{6,7},{15,8},{8,9},{9,10... | collective-permute-start | bytes 1572872 | tf_op jit(solution)/shard_map/ppermute | solution.py:301

commit v5 on v4

--- a/solution.py
+++ b/solution.py
@@ -121,10 +121,12 @@
     for round_index in range(offset, offset + ROUNDS):
         cosine, sine = rotations(diagonal(uu), diagonal(ul), diagonal(ll), round_index)
         cosine_col, sine_col = stood(cosine), stood(sine)
-        a, b = shift(*turn(uu[...], ul[...], cosine, sine), 1)
-        c, d = shift(*turn(lu[...], ll[...], cosine, sine), 1)
-        uu[...], lu[...] = shift(*turn(a, c, cosine_col, sine_col), 0)
-        ul[...], ll[...] = shift(*turn(b, d, cosine_col, sine_col), 0)
+        a, c = turn(uu[...], lu[...], cosine_col, sine_col)
+        b, d = turn(ul[...], ll[...], cosine_col, sine_col)
+        a, b = shift(*turn(a, b, cosine, sine), 1)
+        c, d = shift(*turn(c, d, cosine, sine), 1)
+        uu[...], lu[...] = shift(a, c, 0)
+        ul[...], ll[...] = shift(b, d, 0)
         qu[...], ql[...] = shift(*turn(qu[...], ql[...], cosine, sine), 1)
     end = placing(offset + ROUNDS, second == 0)
     rotation = sum(placed(thirds(jnp.concatenate([qu[...], ql[...]], axis=1)), end, 1))
@@ -217,12 +219,11 @@
     lax.fori_loop(0, count // step, one, 0)
 
 
-def shadow_kernel(received, out0, in0, out1, in1, in2a, kept, own2, x0, x1, x2, x3, *refs):
-    left_of_cross, kept_cols, left_cols, right_cols, weights = refs
+def shadow_kernel(out0, in0, out1, in1, in2a, kept, own2, x0, x1, x2, x3, *refs):
+    left_of_cross, ends, kept_cols, left_cols, right_cols, weights = refs
     q0_k, q1_k, q2_k, q0_pp = out0[:N, :HALF], out1[:N, :HALF], own2[:N], in1[2 * N :]
     q1_pp, q0_ppp = in2a[N : 2 * N], in2a[2 * N :]
-    r3 = cross_dot(q0_k, cross_dot(square_of(received, 0), q0_ppp), (0, 0))
-    upper = jnp.concatenate([kept[HALF:], r3], axis=1)
+    upper = jnp.concatenate([kept[HALF:], jnp.zeros((HALF, HALF), jnp.float32)], axis=1)
     lower = jnp.concatenate([in1[N + HALF : 2 * N, :HALF], in2a[HALF:N]], axis=1)
     t = cross_dot(q1_k, cross_dot(jnp.concatenate([upper, lower], axis=0), q1_pp), (0, 0))
     upper = jnp.concatenate([kept[:HALF], t], axis=1)
@@ -239,6 +240,8 @@
     weights[:, 2 * N : 2 * N + HALF] = cross_dot(q0_pp[:, HALF:], p1_mk)
     weights[:, 2 * N + HALF : 3 * N] = cross_dot(q0_pp[:, :HALF], q1_pp[:HALF])
     weights[:, 3 * N :] = cross_dot(q0_ppp, q1_pp[HALF:])
+    ends[:, :HALF] = weights[:, :HALF]
+    ends[:, HALF:] = weights[:, 3 * N :]
 
     def some_rows(rows):
         both = cross_dot(x1[rows, :], weights[:, HALF : N + HALF])
@@ -258,8 +261,10 @@
     out[...] = total + cross_dot(right_cols[...], right_weight)
 
 
-def step3_kernel(second, left_of_cross, own2, in2b, q3, *parts):
-    gram = joined(own2[N:], cross_dot(left_of_cross[...], in2b[:N]), in2b[N:])
+def step3_kernel(second, received, left_of_cross, ends, own2, in2b, q3, *parts):
+    farthest = cross_dot(square_of(received, 0), cross_dot(ends[:, HALF:], in2b[HALF:N]))
+    cross = cross_dot(left_of_cross[...], in2b[:N]) + cross_dot(ends[:, :HALF], farthest, (0, 0))
+    gram = joined(own2[N:], cross, in2b[N:])
     q3[...], _ = jacobi(gram, 3 * ROUNDS, second[3, 0], parts)
 
 
@@ -343,13 +348,15 @@
     out2b, own2 = run(step2_kernel, [(N + HALF, HALF)] * 2, sender_slot, gram2, scratch=JACOBI_PARTS)
     in2b = onward(out2b)
     rows = matrix.shape[0]
-    left_of_cross, *columns = run(
+    left_of_cross, ends, *columns = run(
         shadow_kernel,
-        [(HALF, N)] + [(rows, HALF)] * 3,
-        *(with_c3, out0, in0, out1, in1, in2a, kept, own2, matrix, before1, before2, before3),
+        [(HALF, N), square] + [(rows, HALF)] * 3,
+        *(out0, in0, out1, in1, in2a, kept, own2, matrix, before1, before2, before3),
         scratch=[pltpu.VMEM((N, 3 * N + HALF), jnp.float32)],
     )
-    (q3,) = run(step3_kernel, [square], sender_slot, left_of_cross, own2, in2b, scratch=JACOBI_PARTS)
+    (q3,) = run(
+        step3_kernel, [square], *(sender_slot, with_c3, left_of_cross, ends, own2, in2b), scratch=JACOBI_PARTS
+    )
 
     def last_columns(place):
         return run(functools.partial(last_kernel, place), [(rows, HALF)], *columns, in2b, q3)[0]

time: 166 us -> 165 us (level)
  Pallas kernels: 40.4 us -> 37.2 us
    pallas_call x16, Pallas kernels: 40.4 us -> 37.2 us  [run(): pl.pallas_call(body, out_shape=[jax.ShapeDtypeStruct(shape, jnp.float32)...]
    ppermute x8, waiting for transfers between devices: 37.6 us -> 39.6 us  [onward(): lax.ppermute(values, 'blk', [((i - places) % devices, i) for i in range(d...]
    unnamed x39 -> x51, local copies, waits for them, and re-layouts: 11.8 us -> 13.2 us
  transfers between devices with their start and end apart: 12 -> 12, of which waited for: 8 -> 8; matrix products, arithmetic and copies ran while one was open for 0% -> 0% of each run, Pallas kernels for 17% -> 16%
where the time goes in v5:
time: 165 us; the launch traced here: 164 us
  waiting for transfers between devices  75.5 us (46%)
  Pallas kernels  37.2 us (23%)
  starting transfers between devices  36.9 us (22%)
  local copies, waits for them, and re-layouts  13.2 us (8%)
    ppermute x8, waiting for transfers between devices, onward(): lax.ppermute(values, 'blk', [((i - places) % devices, i) for i in range(d...  39.6 us
    pallas_call x16, Pallas kernels, run(): pl.pallas_call(body, out_shape=[jax.ShapeDtypeStruct(shape, jnp.float32)...  37.2 us
    all_to_all x4, waiting for transfers between devices, exchange(): return lax.all_to_all(pieces, 'row', 0, 0, tiled=True)  35.9 us
    all_to_all x4, starting transfers between devices, exchange(): return lax.all_to_all(pieces, 'row', 0, 0, tiled=True)  35.1 us
    unnamed x51, local copies, waits for them, and re-layouts  13.2 us
  transfers between devices with their start and end apart: 12, of which 8 were waited for; matrix products, arithmetic and copies ran while one was open for 0% of the time, Pallas kernels for 16%

profile of v5, /device:TPU:8, one launch (start us, length us, event | category | flops | bytes accessed | tf_op | source)
XLA Modules:
  0.0 164.3 jit_solution(8719414750084645621)
XLA Ops:
  0.0 0.0 collective-permute-start
  0.0 1.2 copy-done
  1.2 1.3 shard_map.28.refs_0_
  2.5 13.1 %collective-permute-done.refs_1_.refs_8_ = f32[1024,256]{1,0:T(8,128)S(1)} collective-permute-done((f32[1024,256]{1,0:T(8,128)}, f32[1024,256]{1,0:T(8,128)S(1)}, u32[]{:S(2)}, u32[]{:S(2)}) %collective-permute-start) | collective-permute-done | bytes 1048608 | tf_op jit(solution)/shard_map/ppermute | solution.py:306
  15.6 0.0 collective-permute-start.1
  15.7 1.3 shard_map.29.refs_1_
  17.0 0.0 copy-done.2
  17.0 0.0 copy-start.1
  17.0 0.0 copy-start.15
  17.0 0.8 copy-done.15
  17.8 16.8 %all-to-all-start = ((f32[64,16,128]{2,1,0:T(8,128)}), f32[64,16,128]{2,1,0:T(8,128)}, u32[]{:S(2)}, u32[]{:S(2)}) async-start(f32[64,16,128]{2,1,0:T(8,128)} %copy-done.15), calls=%async_computation | async-start | bytes 1048576 | tf_op jit(solution)/shard_map/all_to_all | solution.py:320
  34.6 0.0 collective-permute-done.1.refs_1_.refs_9_
  34.7 1.3 shard_map.31.refs_1_
  36.0 18.3 %all-to-all-done.refs_0_ = f32[64,16,128]{2,1,0:T(8,128)} async-done(((f32[64,16,128]{2,1,0:T(8,128)}), f32[64,16,128]{2,1,0:T(8,128)}, u32[]{:S(2)}, u32[]{:S(2)}) %all-to-all-start) | async-done | bytes 524320 | tf_op jit(solution)/shard_map/all_to_all | solution.py:320
  54.3 1.1 shard_map.32
  55.5 0.9 copy-done.9
  56.3 5.6 %all-to-all-start.1 = ((f32[64,24,128]{2,1,0:T(8,128)}), f32[64,24,128]{2,1,0:T(8,128)S(1)}, u32[]{:S(2)}, u32[]{:S(2)}) async-start(f32[64,24,128]{2,1,0:T(8,128)} %copy-done.9), calls=%async_computation.1 | async-start | bytes 1572864 | tf_op jit(solution)/shard_map/all_to_all | solution.py:320
  62.0 0.0 collective-permute-start.2
  62.0 0.1 copy.3.refs_0_
  62.1 15.4 %collective-permute-done.2.refs_1_.refs_10_ = f32[1024,256]{1,0:T(8,128)} collective-permute-done((f32[1024,256]{1,0:T(8,128)S(1)}, f32[1024,256]{1,0:T(8,128)}, u32[]{:S(2)}, u32[]{:S(2)}) %collective-permute-start.2) | collective-permute-done | bytes 1048608 | tf_op jit(solution)/shard_map/ppermute | solution.py:306
  77.5 2.5 %shard_map.33.refs_2_.refs_1_ = f32[256,256]{1,0:T(8,128)S(1)} custom-call(f32[1024,256]{1,0:T(8,128)S(1)} %copy-done.1, f32[1024,256]{1,0:T(8,128)} %collective-permute-done.2.refs_1_.refs_10_), custom_call_target="tpu_custom_call" | custom-call | flops 1000000 | bytes 1024 | tf_op jit(solution)/shard_map/pallas_call | solution.py:291
  80.0 5.9 %all-to-all-done.1.refs_1_.refs_0_ = f32[64,24,128]{2,1,0:T(8,128)S(1)} async-done(((f32[64,24,128]{2,1,0:T(8,128)}), f32[64,24,128]{2,1,0:T(8,128)S(1)}, u32[]{:S(2)}, u32[]{:S(2)}) %all-to-all-start.1) | async-done | bytes 786464 | tf_op jit(solution)/shard_map/all_to_all | solution.py:320
  85.9 4.5 %shard_map.34 = (f32[384,256]{1,0:T(8,128)S(1)}, f32[128,128]{1,0:T(8,128)S(1)}) custom-call(s32[4,1]{1,0:T(4,128)S(1)} %copy.3.refs_0_, f32[64,24,128]{2,1,0:T(8,128)S(1)} %all-to-all-done.1.refs_1_.refs_0_, f32[256,256]{1,0:T(8,128)S(1)} %shard_map.33.refs_2_.refs_1_), custom_call_target="tpu_custom_call" | custom-call | flops 1000000 | bytes 1024 | tf_op jit(solution)/shard_map/pallas_call | solution.py:291
  90.4 0.0 copy-start.22
  90.4 0.0 collective-permute-start.3
  90.4 0.1 shard_map.36
  90.5 0.5 copy-done.22
  91.0 0.8 copy-done.14
  91.8 6.9 %all-to-all-start.2 = ((f32[64,16,128]{2,1,0:T(8,128)}), f32[64,16,128]{2,1,0:T(8,128)S(1)}, u32[]{:S(2)}, u32[]{:S(2)}) async-start(f32[64,16,128]{2,1,0:T(8,128)} %copy-done.14), calls=%async_computation.2 | async-start | bytes 1048576 | tf_op jit(solution)/shard_map/all_to_all | solution.py:320
  98.7 0.1 collective-permute-done.3.refs_4_.refs_2_.refs_1_
  98.8 0.7 copy-done.6
  99.6 1.0 copy-done.7
  100.6 0.8 copy-done.23
  101.4 4.9 %shard_map.35 = (f32[768,256]{1,0:T(8,128)S(1)}, f32[128,256]{1,0:T(8,128)S(1)}) custom-call(s32[4,1]{1,0:T(4,128)S(1)} %copy.3.refs_0_, f32[64,24,128]{2,1,0:T(8,128)S(1)} %all-to-all-done.1.refs_1_.refs_0_, f32[128,128]{1,0:T(8,128)S(1)} %copy-done.23, f32[384,256]{1,0:T(8,128)S(1)} %get-tuple-element.23.refs_3_.refs_1_.refs_0_, f32[384,256]{1,0:T(8,128)S(1)} %copy-done.7), custom_call_target="tpu_custom_call" | custom-call | flops 1000000 | bytes 1024 | tf_op jit(solution)/shard_map/pallas_call | solution.py:291
  106.3 0.6 copy-done.18
  106.9 0.0 collective-permute-start.4
  106.9 11.7 %all-to-all-done.2.refs_0_ = f32[64,16,128]{2,1,0:T(8,128)S(1)} async-done(((f32[64,16,128]{2,1,0:T(8,128)}), f32[64,16,128]{2,1,0:T(8,128)S(1)}, u32[]{:S(2)}, u32[]{:S(2)}) %all-to-all-start.2) | async-done | bytes 524320 | tf_op jit(solution)/shard_map/all_to_all | solution.py:320
  118.7 0.8 shard_map.40
  119.5 5.8 %all-to-all-start.3 = ((f32[64,8,128]{2,1,0:T(8,128)}), f32[64,8,128]{2,1,0:T(8,128)}, u32[]{:S(2)}, u32[]{:S(2)}) async-start(f32[64,8,128]{2,1,0:T(8,128)} %shard_map.40), calls=%async_computation.3 | async-start | bytes 524288 | tf_op jit(solution)/shard_map/all_to_all | solution.py:320
  125.3 0.0 collective-permute-done.4.refs_4_.refs_3_
  125.3 0.0 copy-done.8
  125.3 0.0 copy-start.19
  125.3 0.9 copy-done.19
  126.2 2.5 %shard_map.37 = (f32[768,128]{1,0:T(8,128)S(1)}, f32[256,128]{1,0:T(8,128)S(1)}, f32[256,256]{1,0:T(8,128)S(1)}) custom-call(f32[64,16,128]{2,1,0:T(8,128)S(1)} %all-to-all-done.2.refs_0_, f32[384,256]{1,0:T(8,128)S(1)} %get-tuple-element.23.refs_3_.refs_1_.refs_0_, f32[384,256]{1,0:T(8,128)S(1)} %copy-done.8, ...), custom_call_target="tpu_custom_call" | custom-call | flops 1000000 | bytes 1024 | tf_op jit(solution)/shard_map/pallas_call | solution.py:291
  128.7 0.0 collective-permute-start.5
  128.7 4.5 %shard_map.38 = (f32[384,128]{1,0:T(8,128)S(1)}, f32[384,128]{1,0:T(8,128)S(1)}) custom-call(s32[4,1]{1,0:T(4,128)S(1)} %copy.3.refs_0_, f32[256,256]{1,0:T(8,128)S(1)} %get-tuple-element.29.refs_1_), custom_call_target="tpu_custom_call" | custom-call | flops 1000000 | bytes 1024 | tf_op jit(solution)/shard_map/pallas_call | solution.py:291
  133.2 1.8 %collective-permute-start.6 = (f32[384,128]{1,0:T(8,128)S(1)}, f32[384,128]{1,0:T(8,128)S(1)}, u32[]{:S(2)}, u32[]{:S(2)}) collective-permute-start(f32[384,128]{1,0:T(8,128)S(1)} %get-tuple-element.34), channel_id=1, source_target_pairs={{7,0},{0,1},{1,2},{2,3},{3,4},{4,5},{5,6},{6,7},{15,8},{8,9},{9,10... | collective-permute-start | bytes 589832 | tf_op jit(solution)/shard_map/ppermute | solution.py:306
  135.0 2.1 %collective-permute-done.5.refs_4_ = f32[768,128]{1,0:T(8,128)S(1)} collective-permute-done((f32[768,128]{1,0:T(8,128)S(1)}, f32[768,128]{1,0:T(8,128)S(1)}, u32[]{:S(2)}, u32[]{:S(2)}) %collective-permute-start.5) | collective-permute-done | bytes 393248 | tf_op jit(solution)/shard_map/ppermute | solution.py:306
  137.1 5.6 %shard_map.39 = (f32[128,256]{1,0:T(8,128)S(1)}, f32[256,256]{1,0:T(8,128)S(1)}, f32[1024,128]{1,0:T(8,128)S(1)}, f32[1024,128]{1,0:T(8,128)S(1)}, f32[1024,128]{1,0:T(8,128)S(1)}) custom-call(f32[384,256]{1,0:T(8,128)S(1)} %get-tuple-element.23.refs_3_.refs_1_.refs_0_, f32[384,256]{1,0:T(8,128)S(1)} %copy-done.8, ...), custom_call_target="tpu_custom_call" | custom-call | flops 1000000 | bytes 1024 | tf_op jit(solution)/shard_map/pallas_call | solution.py:291
  142.7 0.0 copy-start.10
  142.7 0.8 copy-done.10
  143.5 0.8 copy-done.12
  144.3 0.7 copy-done.16
  145.0 0.6 copy-done.20
  145.6 0.0 collective-permute-done.6.refs_5_.refs_3_
  145.6 0.0 all-to-all-done.3.refs_1_
  145.7 0.9 copy-done.17
  146.6 0.9 copy-done.21
  147.5 5.0 %shard_map.41.refs_4_ = f32[256,256]{1,0:T(8,128)S(1)} custom-call(s32[4,1]{1,0:T(4,128)S(1)} %copy.3.refs_0_, f32[64,8,128]{2,1,0:T(8,128)} %all-to-all-done.3.refs_1_, f32[128,256]{1,0:T(8,128)S(1)} %copy-done.21, f32[256,256]{1,0:T(8,128)S(1)} %copy-done.17, f32[384,128]{1,0:T(8,128)S(1)} %get-tuple-element.30.refs_6_.refs_4_, ...), custom_call_target="tpu_custom_call" | custom-call | flops 1000000 | bytes 1024 | tf_op jit(solution)/shard_map/pallas_call | solution.py:291
  152.5 1.0 shard_map.43
  153.5 0.0 collective-permute-start.7
  153.5 1.0 shard_map.42
  154.5 8.8 %collective-permute-done.7 = f32[1024,128]{1,0:T(8,128)S(1)} collective-permute-done((f32[1024,128]{1,0:T(8,128)S(1)}, f32[1024,128]{1,0:T(8,128)S(1)}, u32[]{:S(2)}, u32[]{:S(2)}) %collective-permute-start.7) | collective-permute-done | bytes 524320 | tf_op jit(solution)/shard_map/ppermute | solution.py:306
  163.3 1.0 pad_maximum_fusion
  (28 shorter events, 0.1 us)
Async XLA Ops:
  0.0 15.6 %collective-permute-start = (f32[1024,256]{1,0:T(8,128)}, f32[1024,256]{1,0:T(8,128)S(1)}, u32[]{:S(2)}, u32[]{:S(2)}) collective-permute-start(f32[1024,256]{1,0:T(8,128)} %refs_7_.1), channel_id=1, source_target_pairs={{7,0},{0,1},{1,2},{2,3},{3,4},{4,5},{5,6},{6,7},{15,8},{8,9},{9,10... | collective-permute-start | bytes 3145736 | tf_op jit(solution)/shard_map/ppermute | solution.py:306
  0.0 1.2 copy-start
  15.6 1.3 copy-start.2
  15.6 19.0 %collective-permute-start.1 = (f32[1024,256]{1,0:T(8,128)S(1)}, f32[1024,256]{1,0:T(8,128)S(1)}, u32[]{:S(2)}, u32[]{:S(2)}) collective-permute-start(f32[1024,256]{1,0:T(8,128)S(1)} %collective-permute-done.refs_1_.refs_8_), channel_id=1, source_target_pairs={{7,0},{0,1},{1,2},{2,3},{3,4},{4,5},{5,6},{6,7},{15,8},{8,9},{9,10... | collective-permute-start | bytes 3145736 | tf_op jit(solution)/shard_map/ppermute | solution.py:306
  17.0 17.7 %copy-start.1 = (f32[1024,256]{1,0:T(8,128)S(1)}, f32[1024,256]{1,0:T(8,128)}, u32[]{:S(2)}) copy-start(f32[1024,256]{1,0:T(8,128)} %refs_7_.1) | copy-start | bytes 3145732
  17.0 0.8 copy-start.15
  17.8 36.5 %all-to-all-start = ((f32[64,16,128]{2,1,0:T(8,128)}), f32[64,16,128]{2,1,0:T(8,128)}, u32[]{:S(2)}, u32[]{:S(2)}) async-start(f32[64,16,128]{2,1,0:T(8,128)} %copy-done.15), calls=%async_computation | async-start | bytes 1048576 | tf_op jit(solution)/shard_map/all_to_all | solution.py:320
  34.7 27.3 %copy-start.4 = (f32[1024,256]{1,0:T(8,128)}, f32[1024,256]{1,0:T(8,128)S(1)}, u32[]{:S(2)}) copy-start(f32[1024,256]{1,0:T(8,128)S(1)} %collective-permute-done.1.refs_1_.refs_9_) | copy-start | bytes 3145732
  55.5 0.9 copy-start.9
  56.3 5.7 %copy-start.24 = (s32[4,1]{0,1:T(1,128)S(1)}, s32[4,1]{0,1:T(1,128)}, u32[]{:S(2)}) copy-start(s32[4,1]{0,1:T(1,128)} %param.3) | copy-start | bytes 52
  56.3 29.6 %all-to-all-start.1 = ((f32[64,24,128]{2,1,0:T(8,128)}), f32[64,24,128]{2,1,0:T(8,128)S(1)}, u32[]{:S(2)}, u32[]{:S(2)}) async-start(f32[64,24,128]{2,1,0:T(8,128)} %copy-done.9), calls=%async_computation.1 | async-start | bytes 1572864 | tf_op jit(solution)/shard_map/all_to_all | solution.py:320
  62.0 15.6 %collective-permute-start.2 = (f32[1024,256]{1,0:T(8,128)S(1)}, f32[1024,256]{1,0:T(8,128)}, u32[]{:S(2)}, u32[]{:S(2)}) collective-permute-start(f32[1024,256]{1,0:T(8,128)S(1)} %collective-permute-done.1.refs_1_.refs_9_), channel_id=1, source_target_pairs={{7,0},{0,1},{1,2},{2,3},{3,4},{4,5},{5,6},{6,7},{15,8},{8,9},{9,10... | collective-permute-start | bytes 3145736 | tf_op jit(solution)/shard_map/ppermute | solution.py:306
  90.4 0.6 copy-start.22
  90.4 8.4 %collective-permute-start.3 = (f32[384,256]{1,0:T(8,128)S(1)}, f32[384,256]{1,0:T(8,128)S(1)}, u32[]{:S(2)}, u32[]{:S(2)}) collective-permute-start(f32[384,256]{1,0:T(8,128)S(1)} %get-tuple-element.23.refs_3_.refs_1_.refs_0_), channel_id=1, source_target_pairs={{7,0},{0,1},{1,2},{2,3},{3,4},{4,5},{5,6},{6,7},{15,8},{8,9},{9,10... | collective-permute-start | bytes 1179656 | tf_op jit(solution)/shard_map/ppermute | solution.py:306
  91.0 0.8 copy-start.14
  91.8 26.8 %all-to-all-start.2 = ((f32[64,16,128]{2,1,0:T(8,128)}), f32[64,16,128]{2,1,0:T(8,128)S(1)}, u32[]{:S(2)}, u32[]{:S(2)}) async-start(f32[64,16,128]{2,1,0:T(8,128)} %copy-done.14), calls=%async_computation.2 | async-start | bytes 1048576 | tf_op jit(solution)/shard_map/all_to_all | solution.py:320
  98.8 0.7 copy-start.6
  99.6 1.0 copy-start.7
  100.6 0.8 copy-start.23
  106.3 0.7 copy-start.18
  106.9 18.3 %collective-permute-start.4 = (f32[768,256]{1,0:T(8,128)S(1)}, f32[768,256]{1,0:T(8,128)}, u32[]{:S(2)}, u32[]{:S(2)}) collective-permute-start(f32[768,256]{1,0:T(8,128)S(1)} %get-tuple-element.25.refs_3_.refs_2_.refs_1_), channel_id=1, source_target_pairs={{7,0},{0,1},{1,2},{2,3},{3,4},{4,5},{5,6},{6,7},{15,8},{8,9},{9,10... | collective-permute-start | bytes 2359304 | tf_op jit(solution)/shard_map/ppermute | solution.py:306
  119.5 5.8 %copy-start.8 = (f32[384,256]{1,0:T(8,128)S(1)}, f32[384,256]{1,0:T(8,128)}, u32[]{:S(2)}) copy-start(f32[384,256]{1,0:T(8,128)} %copy-done.6) | copy-start | bytes 1179652
  119.5 26.2 %all-to-all-start.3 = ((f32[64,8,128]{2,1,0:T(8,128)}), f32[64,8,128]{2,1,0:T(8,128)}, u32[]{:S(2)}, u32[]{:S(2)}) async-start(f32[64,8,128]{2,1,0:T(8,128)} %shard_map.40), calls=%async_computation.3 | async-start | bytes 524288 | tf_op jit(solution)/shard_map/all_to_all | solution.py:320
  125.3 0.9 copy-start.19
  126.2 11.0 %copy-start.3 = (f32[1024,256]{1,0:T(8,128)S(1)}, f32[1024,256]{1,0:T(8,128)}, u32[]{:S(2)}) copy-start(f32[1024,256]{1,0:T(8,128)} %copy-done.2) | copy-start | bytes 3145732
  126.2 11.0 %copy-start.5 = (f32[1024,256]{1,0:T(8,128)S(1)}, f32[1024,256]{1,0:T(8,128)}, u32[]{:S(2)}) copy-start(f32[1024,256]{1,0:T(8,128)} %copy-done.4) | copy-start | bytes 3145732
  128.7 8.4 %collective-permute-start.5 = (f32[768,128]{1,0:T(8,128)S(1)}, f32[768,128]{1,0:T(8,128)S(1)}, u32[]{:S(2)}, u32[]{:S(2)}) collective-permute-start(f32[768,128]{1,0:T(8,128)S(1)} %get-tuple-element.27), channel_id=1, source_target_pairs={{7,0},{0,1},{1,2},{2,3},{3,4},{4,5},{5,6},{6,7},{15,8},{8,9},{9,10... | collective-permute-start | bytes 1179656 | tf_op jit(solution)/shard_map/ppermute | solution.py:306
  133.2 12.4 %collective-permute-start.6 = (f32[384,128]{1,0:T(8,128)S(1)}, f32[384,128]{1,0:T(8,128)S(1)}, u32[]{:S(2)}, u32[]{:S(2)}) collective-permute-start(f32[384,128]{1,0:T(8,128)S(1)} %get-tuple-element.34), channel_id=1, source_target_pairs={{7,0},{0,1},{1,2},{2,3},{3,4},{4,5},{5,6},{6,7},{15,8},{8,9},{9,10... | collective-permute-start | bytes 589832 | tf_op jit(solution)/shard_map/ppermute | solution.py:306
  142.7 0.8 copy-start.10
  143.5 0.8 copy-start.12
  144.3 0.7 copy-start.16
  145.0 0.6 copy-start.20
  145.6 1.0 copy-start.17
  146.6 0.9 copy-start.21
  147.5 5.0 %copy-start.11 = (f32[1024,128]{1,0:T(8,128)S(1)}, f32[1024,128]{1,0:T(8,128)}, u32[]{:S(2)}) copy-start(f32[1024,128]{1,0:T(8,128)} %copy-done.10) | copy-start | bytes 1572868
  147.5 5.0 %copy-start.13 = (f32[1024,128]{1,0:T(8,128)S(1)}, f32[1024,128]{1,0:T(8,128)}, u32[]{:S(2)}) copy-start(f32[1024,128]{1,0:T(8,128)} %copy-done.12) | copy-start | bytes 1572868
  153.5 9.8 %collective-permute-start.7 = (f32[1024,128]{1,0:T(8,128)S(1)}, f32[1024,128]{1,0:T(8,128)S(1)}, u32[]{:S(2)}, u32[]{:S(2)}) collective-permute-start(f32[1024,128]{1,0:T(8,128)S(1)} %shard_map.43), channel_id=1, source_target_pairs={{7,0},{0,1},{1,2},{2,3},{3,4},{4,5},{5,6},{6,7},{15,8},{8,9},{9,10... | collective-permute-start | bytes 1572872 | tf_op jit(solution)/shard_map/ppermute | solution.py:306

commit v6 on v5

--- a/solution.py
+++ b/solution.py
@@ -219,51 +219,54 @@
     lax.fori_loop(0, count // step, one, 0)
 
 
-def shadow_kernel(out0, in0, out1, in1, in2a, kept, own2, x0, x1, x2, x3, *refs):
-    left_of_cross, ends, kept_cols, left_cols, right_cols, weights = refs
-    q0_k, q1_k, q2_k, q0_pp = out0[:N, :HALF], out1[:N, :HALF], own2[:N], in1[2 * N :]
+def columns_kernel(out0, in0, out1, in1, own2, x0, x1, x2, pair, end, weights):
+    q2_kk, q2_mk, q0_pp = own2[:HALF], own2[HALF:N], in1[2 * N :]
+    p1_kk, p1_mk, p1_km, p1_mm = in1[:HALF, :HALF], in1[HALF:N, :HALF], in1[:HALF, HALF:], in1[HALF:N, HALF:]
+    end[...] = cross_dot(out0[:N, :HALF], cross_dot(out1[:HALF, :HALF], q2_kk))
+    travelled = cross_dot(in0[:N, HALF:], cross_dot(out1[HALF:N, :HALF], q2_kk))
+    weights[:, :HALF] = travelled + cross_dot(in0[:N, :HALF], cross_dot(p1_km, q2_mk))
+    weights[:, HALF:N] = cross_dot(in0[:N, :HALF], p1_kk)
+    weights[:, N : N + HALF] = cross_dot(q0_pp[:, HALF:], cross_dot(p1_mm, q2_mk))
+    weights[:, N + HALF :] = cross_dot(q0_pp[:, HALF:], p1_mk)
+
+    def some_rows(rows):
+        both = cross_dot(x1[rows, :], weights[:, :N]) + cross_dot(x2[rows, :], weights[:, N:])
+        pair[rows, :HALF] = cross_dot(x0[rows, :], end[...]) + both[:, :HALF]
+        pair[rows, HALF:] = both[:, HALF:]
+
+    in_chunks(pair.shape[0], some_rows)
+
+
+def cross3_kernel(out0, out1, in1, in2a, kept, own2, end, x2, x3, ends, right_cols, weights):
+    q1_k, q2_k = out1[:N, :HALF], own2[:N]
     q1_pp, q0_ppp = in2a[N : 2 * N], in2a[2 * N :]
     upper = jnp.concatenate([kept[HALF:], jnp.zeros((HALF, HALF), jnp.float32)], axis=1)
     lower = jnp.concatenate([in1[N + HALF : 2 * N, :HALF], in2a[HALF:N]], axis=1)
     t = cross_dot(q1_k, cross_dot(jnp.concatenate([upper, lower], axis=0), q1_pp), (0, 0))
     upper = jnp.concatenate([kept[:HALF], t], axis=1)
     lower = jnp.concatenate([in1[N : N + HALF, :HALF], in2a[:HALF]], axis=1)
-    left_of_cross[...] = cross_dot(q2_k, jnp.concatenate([upper, lower], axis=0), (0, 0))
-
-    q2_kk, q2_mk = own2[:HALF], own2[HALF:N]
-    p1_kk, p1_mk, p1_km, p1_mm = in1[:HALF, :HALF], in1[HALF:N, :HALF], in1[:HALF, HALF:], in1[HALF:N, HALF:]
-    weights[:, :HALF] = cross_dot(q0_k, cross_dot(out1[:HALF, :HALF], q2_kk))
-    travelled = cross_dot(in0[:N, HALF:], cross_dot(out1[HALF:N, :HALF], q2_kk))
-    weights[:, HALF:N] = travelled + cross_dot(in0[:N, :HALF], cross_dot(p1_km, q2_mk))
-    weights[:, N : N + HALF] = cross_dot(in0[:N, :HALF], p1_kk)
-    weights[:, N + HALF : 2 * N] = cross_dot(q0_pp[:, HALF:], cross_dot(p1_mm, q2_mk))
-    weights[:, 2 * N : 2 * N + HALF] = cross_dot(q0_pp[:, HALF:], p1_mk)
-    weights[:, 2 * N + HALF : 3 * N] = cross_dot(q0_pp[:, :HALF], q1_pp[:HALF])
-    weights[:, 3 * N :] = cross_dot(q0_ppp, q1_pp[HALF:])
-    ends[:, :HALF] = weights[:, :HALF]
-    ends[:, HALF:] = weights[:, 3 * N :]
+    ends[N:] = cross_dot(q2_k, jnp.concatenate([upper, lower], axis=0), (0, 0))
+    weights[:, :HALF] = cross_dot(in1[2 * N :, :HALF], q1_pp[:HALF])
+    weights[:, HALF:] = cross_dot(q0_ppp, q1_pp[HALF:])
+    ends[:N, :HALF] = end[...]
+    ends[:N, HALF:] = weights[:, HALF:]
 
     def some_rows(rows):
-        both = cross_dot(x1[rows, :], weights[:, HALF : N + HALF])
-        three = cross_dot(x2[rows, :], weights[:, N + HALF : 3 * N])
-        kept_cols[rows, :] = cross_dot(x0[rows, :], weights[:, :HALF]) + both[:, :HALF] + three[:, :HALF]
-        left_cols[rows, :] = both[:, HALF:] + three[:, HALF:N]
-        right_cols[rows, :] = three[:, N:] + cross_dot(x3[rows, :], weights[:, 3 * N :])
-
-    in_chunks(kept_cols.shape[0], some_rows)
-
-
-def last_kernel(place, kept_cols, left_cols, right_cols, in2b, q3, out):
+        right_cols[rows, :] = cross_dot(x2[rows, :], weights[:, :HALF]) + cross_dot(x3[rows, :], weights[:, HALF:])
+
+    in_chunks(right_cols.shape[0], some_rows)
+
+
+def last_kernel(place, pair, right_cols, in2b, q3, out):
     kept_weight, weight = q3[:HALF, place : place + HALF], q3[HALF:, place : place + HALF]
     left_weight, right_weight = cross_dot(in2b[:HALF], weight), cross_dot(in2b[HALF:N], weight)
-    both = jnp.concatenate([kept_cols[...], left_cols[...]], axis=1)
-    total = cross_dot(both, jnp.concatenate([kept_weight, left_weight], axis=0))
+    total = cross_dot(pair[...], jnp.concatenate([kept_weight, left_weight], axis=0))
     out[...] = total + cross_dot(right_cols[...], right_weight)
 
 
-def step3_kernel(second, received, left_of_cross, ends, own2, in2b, q3, *parts):
-    farthest = cross_dot(square_of(received, 0), cross_dot(ends[:, HALF:], in2b[HALF:N]))
-    cross = cross_dot(left_of_cross[...], in2b[:N]) + cross_dot(ends[:, :HALF], farthest, (0, 0))
+def step3_kernel(second, received, ends, own2, in2b, q3, *parts):
+    farthest = cross_dot(square_of(received, 0), cross_dot(ends[:N, HALF:], in2b[HALF:N]))
+    cross = cross_dot(ends[N:], in2b[:N]) + cross_dot(ends[:N, :HALF], farthest, (0, 0))
     gram = joined(own2[N:], cross, in2b[N:])
     q3[...], _ = jacobi(gram, 3 * ROUNDS, second[3, 0], parts)
 
@@ -348,18 +351,22 @@
     out2b, own2 = run(step2_kernel, [(N + HALF, HALF)] * 2, sender_slot, gram2, scratch=JACOBI_PARTS)
     in2b = onward(out2b)
     rows = matrix.shape[0]
-    left_of_cross, ends, *columns = run(
-        shadow_kernel,
-        [(HALF, N), square] + [(rows, HALF)] * 3,
-        *(out0, in0, out1, in1, in2a, kept, own2, matrix, before1, before2, before3),
-        scratch=[pltpu.VMEM((N, 3 * N + HALF), jnp.float32)],
-    )
-    (q3,) = run(
-        step3_kernel, [square], *(sender_slot, with_c3, left_of_cross, ends, own2, in2b), scratch=JACOBI_PARTS
-    )
+    pair, end = run(
+        columns_kernel,
+        [(rows, N), (N, HALF)],
+        *(out0, in0, out1, in1, own2, matrix, before1, before2),
+        scratch=[pltpu.VMEM((N, 2 * N), jnp.float32)],
+    )
+    ends, right_cols = run(
+        cross3_kernel,
+        [(N + HALF, N), (rows, HALF)],
+        *(out0, out1, in1, in2a, kept, own2, end, before2, before3),
+        scratch=[pltpu.VMEM((N, N), jnp.float32)],
+    )
+    (q3,) = run(step3_kernel, [square], *(sender_slot, with_c3, ends, own2, in2b), scratch=JACOBI_PARTS)
 
     def last_columns(place):
-        return run(functools.partial(last_kernel, place), [(rows, HALF)], *columns, in2b, q3)[0]
+        return run(functools.partial(last_kernel, place), [(rows, HALF)], pair, right_cols, in2b, q3)[0]
 
     arrived = onward(last_columns(HALF))
     kept = last_columns(0)

time: 165 us -> 162 us (0.982)
  local copies, waits for them, and re-layouts: 13.2 us -> 11.2 us
  waiting for transfers between devices: 75.5 us -> 73.6 us
    unnamed x51 -> x41, local copies, waits for them, and re-layouts: 13.2 us -> 11.2 us
    ppermute x8, waiting for transfers between devices: 39.6 us -> 37.6 us  [onward(): lax.ppermute(values, 'blk', [((i - places) % devices, i) for i in range(d...]
    pallas_call x16 -> x17, Pallas kernels: 37.2 us -> 38.5 us  [run(): pl.pallas_call(body, out_shape=[jax.ShapeDtypeStruct(shape, jnp.float32)...]
  transfers between devices with their start and end apart: 12 -> 12, of which waited for: 8 -> 7; matrix products, arithmetic and copies ran while one was open for 0% -> 0% of each run, Pallas kernels for 16% -> 17%
where the time goes in v6:
time: 162 us; the launch traced here: 161 us
  waiting for transfers between devices  73.6 us (45%)
  Pallas kernels  38.5 us (24%)
  starting transfers between devices  36.6 us (23%)
  local copies, waits for them, and re-layouts  11.2 us (7%)
    pallas_call x17, Pallas kernels, run(): pl.pallas_call(body, out_shape=[jax.ShapeDtypeStruct(shape, jnp.float32)...  38.5 us
    ppermute x8, waiting for transfers between devices, onward(): lax.ppermute(values, 'blk', [((i - places) % devices, i) for i in range(d...  37.6 us
    all_to_all x4, waiting for transfers between devices, exchange(): return lax.all_to_all(pieces, 'row', 0, 0, tiled=True)  36 us
    all_to_all x4, starting transfers between devices, exchange(): return lax.all_to_all(pieces, 'row', 0, 0, tiled=True)  34.8 us
    unnamed x41, local copies, waits for them, and re-layouts  11.2 us
  transfers between devices with their start and end apart: 12, of which 7 were waited for; matrix products, arithmetic and copies ran while one was open for 0% of the time, Pallas kernels for 17%

profile of v6, /device:TPU:8, one launch (start us, length us, event | category | flops | bytes accessed | tf_op | source)
XLA Modules:
  0.0 161.3 jit_solution(15589049500727896511)
XLA Ops:
  0.0 0.0 collective-permute-start
  0.0 1.2 copy-done
  1.2 1.3 shard_map.28.refs_0_
  2.5 13.2 %collective-permute-done.refs_1_.refs_6_ = f32[1024,256]{1,0:T(8,128)} collective-permute-done((f32[1024,256]{1,0:T(8,128)}, f32[1024,256]{1,0:T(8,128)}, u32[]{:S(2)}, u32[]{:S(2)}) %collective-permute-start) | collective-permute-done | bytes 1048608 | tf_op jit(solution)/shard_map/ppermute | solution.py:309
  15.8 0.0 collective-permute-start.1
  15.8 2.5 %shard_map.29.refs_1_ = f32[256,256]{1,0:T(8,128)S(1)} custom-call(f32[1024,256]{1,0:T(8,128)S(1)} %copy-done, f32[1024,256]{1,0:T(8,128)} %collective-permute-done.refs_1_.refs_6_), custom_call_target="tpu_custom_call" | custom-call | flops 1000000 | bytes 1024 | tf_op jit(solution)/shard_map/pallas_call | solution.py:294
  18.3 0.0 copy-start.1
  18.3 0.8 shard_map.30
  19.1 16.6 %all-to-all-start = ((f32[64,16,128]{2,1,0:T(8,128)}), f32[64,16,128]{2,1,0:T(8,128)S(1)}, u32[]{:S(2)}, u32[]{:S(2)}) async-start(f32[64,16,128]{2,1,0:T(8,128)} %shard_map.30), calls=%async_computation | async-start | bytes 1048576 | tf_op jit(solution)/shard_map/all_to_all | solution.py:323
  35.7 0.0 collective-permute-done.1.refs_1_.refs_7_
  35.7 0.0 copy-start.2
  35.7 1.3 shard_map.31.refs_1_
  37.1 18.5 %all-to-all-done.refs_0_ = f32[64,16,128]{2,1,0:T(8,128)S(1)} async-done(((f32[64,16,128]{2,1,0:T(8,128)}), f32[64,16,128]{2,1,0:T(8,128)S(1)}, u32[]{:S(2)}, u32[]{:S(2)}) %all-to-all-start) | async-done | bytes 524320 | tf_op jit(solution)/shard_map/all_to_all | solution.py:323
  55.6 0.1 shard_map.32
  55.7 0.9 copy-done.10
  56.6 5.6 %all-to-all-start.1 = ((f32[64,24,128]{2,1,0:T(8,128)}), f32[64,24,128]{2,1,0:T(8,128)S(1)}, u32[]{:S(2)}, u32[]{:S(2)}) async-start(f32[64,24,128]{2,1,0:T(8,128)} %copy-done.10), calls=%async_computation.1 | async-start | bytes 1572864 | tf_op jit(solution)/shard_map/all_to_all | solution.py:323
  62.2 0.0 copy-done.2
  62.2 0.0 collective-permute-start.2
  62.2 0.0 copy-done.19
  62.3 0.1 copy.3.refs_0_
  62.3 15.4 %collective-permute-done.2.refs_1_.refs_8_ = f32[1024,256]{1,0:T(8,128)} collective-permute-done((f32[1024,256]{1,0:T(8,128)S(1)}, f32[1024,256]{1,0:T(8,128)}, u32[]{:S(2)}, u32[]{:S(2)}) %collective-permute-start.2) | collective-permute-done | bytes 1048608 | tf_op jit(solution)/shard_map/ppermute | solution.py:309
  77.8 2.5 %shard_map.33.refs_2_.refs_1_ = f32[256,256]{1,0:T(8,128)S(1)} custom-call(f32[1024,256]{1,0:T(8,128)S(1)} %copy-done.1, f32[1024,256]{1,0:T(8,128)} %collective-permute-done.2.refs_1_.refs_8_), custom_call_target="tpu_custom_call" | custom-call | flops 1000000 | bytes 1024 | tf_op jit(solution)/shard_map/pallas_call | solution.py:294
  80.3 5.8 %all-to-all-done.1.refs_1_.refs_0_ = f32[64,24,128]{2,1,0:T(8,128)S(1)} async-done(((f32[64,24,128]{2,1,0:T(8,128)}), f32[64,24,128]{2,1,0:T(8,128)S(1)}, u32[]{:S(2)}, u32[]{:S(2)}) %all-to-all-start.1) | async-done | bytes 786464 | tf_op jit(solution)/shard_map/all_to_all | solution.py:323
  86.1 4.5 %shard_map.34 = (f32[384,256]{1,0:T(8,128)S(1)}, f32[128,128]{1,0:T(8,128)S(1)}) custom-call(s32[4,1]{1,0:T(4,128)S(1)} %copy.3.refs_0_, f32[64,24,128]{2,1,0:T(8,128)S(1)} %all-to-all-done.1.refs_1_.refs_0_, f32[256,256]{1,0:T(8,128)S(1)} %shard_map.33.refs_2_.refs_1_), custom_call_target="tpu_custom_call" | custom-call | flops 1000000 | bytes 1024 | tf_op jit(solution)/shard_map/pallas_call | solution.py:294
  90.6 0.0 collective-permute-start.3
  90.7 0.1 shard_map.36
  90.7 0.5 copy-done.17
  91.2 0.8 copy-done.11
  92.0 6.9 %all-to-all-start.2 = ((f32[64,16,128]{2,1,0:T(8,128)}), f32[64,16,128]{2,1,0:T(8,128)S(1)}, u32[]{:S(2)}, u32[]{:S(2)}) async-start(f32[64,16,128]{2,1,0:T(8,128)} %copy-done.11), calls=%async_computation.2 | async-start | bytes 1048576 | tf_op jit(solution)/shard_map/all_to_all | solution.py:323
  98.9 0.1 collective-permute-done.3.refs_4_.refs_2_.refs_1_
  99.1 0.7 copy-done.6
  99.8 1.0 copy-done.7
  100.8 0.8 copy-done.18
  101.6 4.9 %shard_map.35 = (f32[768,256]{1,0:T(8,128)S(1)}, f32[128,256]{1,0:T(8,128)S(1)}) custom-call(s32[4,1]{1,0:T(4,128)S(1)} %copy.3.refs_0_, f32[64,24,128]{2,1,0:T(8,128)S(1)} %all-to-all-done.1.refs_1_.refs_0_, f32[128,128]{1,0:T(8,128)S(1)} %copy-done.18, f32[384,256]{1,0:T(8,128)S(1)} %get-tuple-element.22.refs_3_.refs_1_.refs_0_, f32[384,256]{1,0:T(8,128)S(1)} %copy-done.7), custom_call_target="tpu_custom_call" | custom-call | flops 1000000 | bytes 1024 | tf_op jit(solution)/shard_map/pallas_call | solution.py:294
  106.5 0.6 copy-done.15
  107.1 0.0 collective-permute-start.4
  107.1 11.7 %all-to-all-done.2.refs_0_ = f32[64,16,128]{2,1,0:T(8,128)S(1)} async-done(((f32[64,16,128]{2,1,0:T(8,128)}), f32[64,16,128]{2,1,0:T(8,128)S(1)}, u32[]{:S(2)}, u32[]{:S(2)}) %all-to-all-start.2) | async-done | bytes 524320 | tf_op jit(solution)/shard_map/all_to_all | solution.py:323
  118.8 0.1 shard_map.41
  118.9 0.7 copy-done.12
  119.6 5.7 %all-to-all-start.3 = ((f32[64,8,128]{2,1,0:T(8,128)}), f32[64,8,128]{2,1,0:T(8,128)}, u32[]{:S(2)}, u32[]{:S(2)}) async-start(f32[64,8,128]{2,1,0:T(8,128)} %copy-done.12), calls=%async_computation.3 | async-start | bytes 524288 | tf_op jit(solution)/shard_map/all_to_all | solution.py:323
  125.3 0.0 collective-permute-done.4.refs_4_.refs_3_.refs_2_
  125.3 0.0 copy-start.8
  125.3 1.0 copy-done.8
  126.3 0.9 copy-done.16
  127.2 1.2 shard_map.37
  128.5 0.0 collective-permute-start.5
  128.5 4.5 %shard_map.38 = (f32[384,128]{1,0:T(8,128)S(1)}, f32[384,128]{1,0:T(8,128)S(1)}) custom-call(s32[4,1]{1,0:T(4,128)S(1)} %copy.3.refs_0_, f32[256,256]{1,0:T(8,128)S(1)} %get-tuple-element.26.refs_1_), custom_call_target="tpu_custom_call" | custom-call | flops 1000000 | bytes 1024 | tf_op jit(solution)/shard_map/pallas_call | solution.py:294
  133.0 1.7 %collective-permute-start.6 = (f32[384,128]{1,0:T(8,128)S(1)}, f32[384,128]{1,0:T(8,128)S(1)}, u32[]{:S(2)}, u32[]{:S(2)}) collective-permute-start(f32[384,128]{1,0:T(8,128)S(1)} %get-tuple-element.33), channel_id=1, source_target_pairs={{7,0},{0,1},{1,2},{2,3},{3,4},{4,5},{5,6},{6,7},{15,8},{8,9},{9,10... | collective-permute-start | bytes 589832 | tf_op jit(solution)/shard_map/ppermute | solution.py:309
  134.7 4.0 %shard_map.39 = (f32[1024,256]{1,0:T(8,128)S(1)}, f32[256,128]{1,0:T(8,128)S(1)}) custom-call(f32[384,256]{1,0:T(8,128)S(1)} %get-tuple-element.22.refs_3_.refs_1_.refs_0_, f32[384,256]{1,0:T(8,128)S(1)} %copy-done.9, f32[768,256]{1,0:T(8,128)S(1)} %get-tuple-element.24.refs_3_.refs_2_.refs_1_, ...), custom_call_target="tpu_custom_call" | custom-call | flops 1000000 | bytes 1024 | tf_op jit(solution)/shard_map/pallas_call | solution.py:294
  138.8 0.0 copy-start.4
  138.8 0.0 collective-permute-done.5.refs_3_
  138.8 3.9 %shard_map.40 = (f32[384,256]{1,0:T(8,128)S(1)}, f32[1024,128]{1,0:T(8,128)S(1)}) custom-call(f32[384,256]{1,0:T(8,128)S(1)} %get-tuple-element.22.refs_3_.refs_1_.refs_0_, f32[768,256]{1,0:T(8,128)S(1)} %get-tuple-element.24.refs_3_.refs_2_.refs_1_, f32[768,256]{1,0:T(8,128)S(1)} %collective-permute-done.4.refs_4_.refs_3_.refs_2_, ...), custom_call_target="tpu_custom_call" | custom-call | flops 1000000 | bytes 1024 | tf_op jit(solution)/shard_map/pallas_call | solution.py:294
  142.8 0.7 copy-done.13
  143.5 0.0 collective-permute-done.6.refs_4_.refs_2_
  143.5 0.0 all-to-all-done.3.refs_1_
  143.5 0.0 copy-start.14
  143.5 1.1 copy-done.14
  144.6 4.9 %shard_map.42.refs_3_ = f32[256,256]{1,0:T(8,128)S(1)} custom-call(s32[4,1]{1,0:T(4,128)S(1)} %copy.3.refs_0_, f32[64,8,128]{2,1,0:T(8,128)} %all-to-all-done.3.refs_1_, f32[384,256]{1,0:T(8,128)S(1)} %copy-done.14, f32[384,128]{1,0:T(8,128)S(1)} %get-tuple-element.27.refs_4_.refs_5_.refs_3_, f32[384,128]{1,0:T(8,128)S(1)} %collective-permute-done.6.refs_4_.refs_2_), custom_call_target="tpu_custom_call" | custom-call | flops 1000000 | bytes 1024 | tf_op jit(solution)/shard_map/pallas_call | solution.py:294
  149.5 0.0 copy-done.5
  149.5 1.0 shard_map.44
  150.4 0.0 collective-permute-start.7
  150.5 1.0 shard_map.43
  151.5 8.8 %collective-permute-done.7 = f32[1024,128]{1,0:T(8,128)S(1)} collective-permute-done((f32[1024,128]{1,0:T(8,128)S(1)}, f32[1024,128]{1,0:T(8,128)S(1)}, u32[]{:S(2)}, u32[]{:S(2)}) %collective-permute-start.7) | collective-permute-done | bytes 524320 | tf_op jit(solution)/shard_map/ppermute | solution.py:309
  160.3 1.0 pad_maximum_fusion
  (19 shorter events, 0.0 us)
Async XLA Ops:
  0.0 15.8 %collective-permute-start = (f32[1024,256]{1,0:T(8,128)}, f32[1024,256]{1,0:T(8,128)}, u32[]{:S(2)}, u32[]{:S(2)}) collective-permute-start(f32[1024,256]{1,0:T(8,128)} %refs_5_.1), channel_id=1, source_target_pairs={{7,0},{0,1},{1,2},{2,3},{3,4},{4,5},{5,6},{6,7},{15,8},{8,9},{9,10... | collective-permute-start | bytes 3145736 | tf_op jit(solution)/shard_map/ppermute | solution.py:309
  0.0 1.2 copy-start
  15.8 20.0 %collective-permute-start.1 = (f32[1024,256]{1,0:T(8,128)}, f32[1024,256]{1,0:T(8,128)S(1)}, u32[]{:S(2)}, u32[]{:S(2)}) collective-permute-start(f32[1024,256]{1,0:T(8,128)} %collective-permute-done.refs_1_.refs_6_), channel_id=1, source_target_pairs={{7,0},{0,1},{1,2},{2,3},{3,4},{4,5},{5,6},{6,7},{15,8},{8,9},{9,10... | collective-permute-start | bytes 3145736 | tf_op jit(solution)/shard_map/ppermute | solution.py:309
  18.3 17.4 %copy-start.1 = (f32[1024,256]{1,0:T(8,128)S(1)}, f32[1024,256]{1,0:T(8,128)}, u32[]{:S(2)}) copy-start(f32[1024,256]{1,0:T(8,128)} %refs_5_.1) | copy-start | bytes 3145732
  19.1 36.4 %all-to-all-start = ((f32[64,16,128]{2,1,0:T(8,128)}), f32[64,16,128]{2,1,0:T(8,128)S(1)}, u32[]{:S(2)}, u32[]{:S(2)}) async-start(f32[64,16,128]{2,1,0:T(8,128)} %shard_map.30), calls=%async_computation | async-start | bytes 1048576 | tf_op jit(solution)/shard_map/all_to_all | solution.py:323
  35.7 26.5 %copy-start.2 = (f32[1024,256]{1,0:T(8,128)}, f32[1024,256]{1,0:T(8,128)S(1)}, u32[]{:S(2)}) copy-start(f32[1024,256]{1,0:T(8,128)S(1)} %collective-permute-done.1.refs_1_.refs_7_) | copy-start | bytes 3145732
  55.7 0.9 copy-start.10
  56.6 5.7 %copy-start.19 = (s32[4,1]{0,1:T(1,128)S(1)}, s32[4,1]{0,1:T(1,128)}, u32[]{:S(2)}) copy-start(s32[4,1]{0,1:T(1,128)} %param.3) | copy-start | bytes 52
  56.6 29.6 %all-to-all-start.1 = ((f32[64,24,128]{2,1,0:T(8,128)}), f32[64,24,128]{2,1,0:T(8,128)S(1)}, u32[]{:S(2)}, u32[]{:S(2)}) async-start(f32[64,24,128]{2,1,0:T(8,128)} %copy-done.10), calls=%async_computation.1 | async-start | bytes 1572864 | tf_op jit(solution)/shard_map/all_to_all | solution.py:323
  62.2 15.6 %collective-permute-start.2 = (f32[1024,256]{1,0:T(8,128)S(1)}, f32[1024,256]{1,0:T(8,128)}, u32[]{:S(2)}, u32[]{:S(2)}) collective-permute-start(f32[1024,256]{1,0:T(8,128)S(1)} %collective-permute-done.1.refs_1_.refs_7_), channel_id=1, source_target_pairs={{7,0},{0,1},{1,2},{2,3},{3,4},{4,5},{5,6},{6,7},{15,8},{8,9},{9,10... | collective-permute-start | bytes 3145736 | tf_op jit(solution)/shard_map/ppermute | solution.py:309
  90.6 0.6 copy-start.17
  90.6 8.4 %collective-permute-start.3 = (f32[384,256]{1,0:T(8,128)S(1)}, f32[384,256]{1,0:T(8,128)S(1)}, u32[]{:S(2)}, u32[]{:S(2)}) collective-permute-start(f32[384,256]{1,0:T(8,128)S(1)} %get-tuple-element.22.refs_3_.refs_1_.refs_0_), channel_id=1, source_target_pairs={{7,0},{0,1},{1,2},{2,3},{3,4},{4,5},{5,6},{6,7},{15,8},{8,9},{9,10... | collective-permute-start | bytes 1179656 | tf_op jit(solution)/shard_map/ppermute | solution.py:309
  91.2 0.8 copy-start.11
  92.0 26.8 %all-to-all-start.2 = ((f32[64,16,128]{2,1,0:T(8,128)}), f32[64,16,128]{2,1,0:T(8,128)S(1)}, u32[]{:S(2)}, u32[]{:S(2)}) async-start(f32[64,16,128]{2,1,0:T(8,128)} %copy-done.11), calls=%async_computation.2 | async-start | bytes 1048576 | tf_op jit(solution)/shard_map/all_to_all | solution.py:323
  99.1 0.7 copy-start.6
  99.8 1.0 copy-start.7
  100.8 0.8 copy-start.18
  106.5 0.6 copy-start.15
  107.1 18.2 %collective-permute-start.4 = (f32[768,256]{1,0:T(8,128)S(1)}, f32[768,256]{1,0:T(8,128)S(1)}, u32[]{:S(2)}, u32[]{:S(2)}) collective-permute-start(f32[768,256]{1,0:T(8,128)S(1)} %get-tuple-element.24.refs_3_.refs_2_.refs_1_), channel_id=1, source_target_pairs={{7,0},{0,1},{1,2},{2,3},{3,4},{4,5},{5,6},{6,7},{15,8},{8,9},{9,10... | collective-permute-start | bytes 2359304 | tf_op jit(solution)/shard_map/ppermute | solution.py:309
  118.9 0.7 copy-start.12
  119.6 23.9 %all-to-all-start.3 = ((f32[64,8,128]{2,1,0:T(8,128)}), f32[64,8,128]{2,1,0:T(8,128)}, u32[]{:S(2)}, u32[]{:S(2)}) async-start(f32[64,8,128]{2,1,0:T(8,128)} %copy-done.12), calls=%async_computation.3 | async-start | bytes 524288 | tf_op jit(solution)/shard_map/all_to_all | solution.py:323
  125.3 1.0 copy-start.8
  126.3 0.9 copy-start.16
  127.2 7.5 %copy-start.3 = (f32[1024,256]{1,0:T(8,128)S(1)}, f32[1024,256]{1,0:T(8,128)}, u32[]{:S(2)}) copy-start(f32[1024,256]{1,0:T(8,128)} %copy-done.2) | copy-start | bytes 3145732
  127.2 7.5 %copy-start.9 = (f32[384,256]{1,0:T(8,128)S(1)}, f32[384,256]{1,0:T(8,128)}, u32[]{:S(2)}) copy-start(f32[384,256]{1,0:T(8,128)} %copy-done.6) | copy-start | bytes 1179652
  128.5 10.3 %collective-permute-start.5 = (f32[768,128]{1,0:T(8,128)S(1)}, f32[768,128]{1,0:T(8,128)S(1)}, u32[]{:S(2)}, u32[]{:S(2)}) collective-permute-start(f32[768,128]{1,0:T(8,128)S(1)} %get-tuple-element.29), channel_id=1, source_target_pairs={{7,0},{0,1},{1,2},{2,3},{3,4},{4,5},{5,6},{6,7},{15,8},{8,9},{9,10... | collective-permute-start | bytes 1179656 | tf_op jit(solution)/shard_map/ppermute | solution.py:309
  133.0 10.5 %collective-permute-start.6 = (f32[384,128]{1,0:T(8,128)S(1)}, f32[384,128]{1,0:T(8,128)S(1)}, u32[]{:S(2)}, u32[]{:S(2)}) collective-permute-start(f32[384,128]{1,0:T(8,128)S(1)} %get-tuple-element.33), channel_id=1, source_target_pairs={{7,0},{0,1},{1,2},{2,3},{3,4},{4,5},{5,6},{6,7},{15,8},{8,9},{9,10... | collective-permute-start | bytes 589832 | tf_op jit(solution)/shard_map/ppermute | solution.py:309
  138.8 4.0 %copy-start.4 = (f32[1024,256]{1,0:T(8,128)}, f32[1024,256]{1,0:T(8,128)S(1)}, u32[]{:S(2)}) copy-start(f32[1024,256]{1,0:T(8,128)S(1)} %get-tuple-element.28.refs_0_) | copy-start | bytes 3145732
  142.7 0.7 copy-start.13
  143.5 6.0 %copy-start.5 = (f32[1024,256]{1,0:T(8,128)S(1)}, f32[1024,256]{1,0:T(8,128)}, u32[]{:S(2)}) copy-start(f32[1024,256]{1,0:T(8,128)} %copy-done.4) | copy-start | bytes 3145732
  143.5 1.1 copy-start.14
  150.4 9.8 %collective-permute-start.7 = (f32[1024,128]{1,0:T(8,128)S(1)}, f32[1024,128]{1,0:T(8,128)S(1)}, u32[]{:S(2)}, u32[]{:S(2)}) collective-permute-start(f32[1024,128]{1,0:T(8,128)S(1)} %shard_map.44), channel_id=1, source_target_pairs={{7,0},{0,1},{1,2},{2,3},{3,4},{4,5},{5,6},{6,7},{15,8},{8,9},{9,10... | collective-permute-start | bytes 1572872 | tf_op jit(solution)/shard_map/ppermute | solution.py:309

commit v7 on v6

--- a/solution.py
+++ b/solution.py
@@ -264,6 +264,19 @@
     out[...] = total + cross_dot(right_cols[...], right_weight)
 
 
+def join_kernel(kept, arrived, out, sems):
+    step, copies = kept.shape[0] // 4, []
+    for number in range(4):
+        rows = pl.ds(number * step, step)
+        for side, half in enumerate((kept, arrived)):
+            target = out.at[rows, pl.ds(side * HALF, HALF)]
+            copies.append(pltpu.make_async_copy(half.at[rows, :], target, sems.at[2 * number + side]))
+    for copy in copies:
+        copy.start()
+    for copy in copies:
+        copy.wait()
+
+
 def step3_kernel(second, received, ends, own2, in2b, q3, *parts):
     farthest = cross_dot(square_of(received, 0), cross_dot(ends[:N, HALF:], in2b[HALF:N]))
     cross = cross_dot(ends[N:], in2b[:N]) + cross_dot(ends[:N, :HALF], farthest, (0, 0))
@@ -370,7 +383,14 @@
 
     arrived = onward(last_columns(HALF))
     kept = last_columns(0)
-    return jnp.concatenate([kept, arrived], axis=1)
+    return pl.pallas_call(
+        join_kernel,
+        out_shape=jax.ShapeDtypeStruct(matrix.shape, jnp.float32),
+        in_specs=[pl.BlockSpec(memory_space=pltpu.VMEM)] * 2,
+        out_specs=pl.BlockSpec(memory_space=pl.ANY),
+        scratch_shapes=[pltpu.SemaphoreType.DMA((8,))],
+        compiler_params=pltpu.CompilerParams(vmem_limit_bytes=16 * 2**20),
+    )(kept, arrived)
 
 
 def solution(mesh):

time: 162 us -> 162 us (level)
  no operation moved by 1% of the time
where the time goes in v7:
time: 162 us; the launch traced here: 161 us
  waiting for transfers between devices  73.6 us (45%)
  Pallas kernels  39.6 us (24%)
  starting transfers between devices  36.6 us (23%)
  local copies, waits for them, and re-layouts  11.2 us (7%)
    pallas_call x17, Pallas kernels, run(): pl.pallas_call(body, out_shape=[jax.ShapeDtypeStruct(shape, jnp.float32)...  38.5 us
    ppermute x8, waiting for transfers between devices, onward(): lax.ppermute(values, 'blk', [((i - places) % devices, i) for i in range(d...  37.6 us
    all_to_all x4, waiting for transfers between devices, exchange(): return lax.all_to_all(pieces, 'row', 0, 0, tiled=True)  36 us
    all_to_all x4, starting transfers between devices, exchange(): return lax.all_to_all(pieces, 'row', 0, 0, tiled=True)  34.8 us
    unnamed x41, local copies, waits for them, and re-layouts  11.2 us
  transfers between devices with their start and end apart: 12, of which 7 were waited for; matrix products, arithmetic and copies ran while one was open for 0% of the time, Pallas kernels for 17%

profile of v7, /device:TPU:8, one launch (start us, length us, event | category | flops | bytes accessed | tf_op | source)
XLA Modules:
  0.0 161.5 jit_solution(3143648229160372646)
XLA Ops:
  0.0 0.0 collective-permute-start
  0.0 1.2 copy-done
  1.2 1.3 shard_map.28.refs_0_
  2.5 13.2 %collective-permute-done.refs_1_.refs_6_ = f32[1024,256]{1,0:T(8,128)} collective-permute-done((f32[1024,256]{1,0:T(8,128)}, f32[1024,256]{1,0:T(8,128)}, u32[]{:S(2)}, u32[]{:S(2)}) %collective-permute-start) | collective-permute-done | bytes 1048608 | tf_op jit(solution)/shard_map/ppermute | solution.py:322
  15.8 0.0 collective-permute-start.1
  15.8 2.5 %shard_map.29.refs_1_ = f32[256,256]{1,0:T(8,128)S(1)} custom-call(f32[1024,256]{1,0:T(8,128)S(1)} %copy-done, f32[1024,256]{1,0:T(8,128)} %collective-permute-done.refs_1_.refs_6_), custom_call_target="tpu_custom_call" | custom-call | flops 1000000 | bytes 1024 | tf_op jit(solution)/shard_map/pallas_call | solution.py:307
  18.3 0.0 copy-start.1
  18.3 0.8 shard_map.30
  19.1 16.6 %all-to-all-start = ((f32[64,16,128]{2,1,0:T(8,128)}), f32[64,16,128]{2,1,0:T(8,128)S(1)}, u32[]{:S(2)}, u32[]{:S(2)}) async-start(f32[64,16,128]{2,1,0:T(8,128)} %shard_map.30), calls=%async_computation | async-start | bytes 1048576 | tf_op jit(solution)/shard_map/all_to_all | solution.py:336
  35.7 0.0 collective-permute-done.1.refs_1_.refs_7_
  35.7 0.0 copy-start.2
  35.7 1.3 shard_map.31.refs_1_
  37.1 18.5 %all-to-all-done.refs_0_ = f32[64,16,128]{2,1,0:T(8,128)S(1)} async-done(((f32[64,16,128]{2,1,0:T(8,128)}), f32[64,16,128]{2,1,0:T(8,128)S(1)}, u32[]{:S(2)}, u32[]{:S(2)}) %all-to-all-start) | async-done | bytes 524320 | tf_op jit(solution)/shard_map/all_to_all | solution.py:336
  55.6 0.1 shard_map.32
  55.7 0.9 copy-done.10
  56.6 5.6 %all-to-all-start.1 = ((f32[64,24,128]{2,1,0:T(8,128)}), f32[64,24,128]{2,1,0:T(8,128)S(1)}, u32[]{:S(2)}, u32[]{:S(2)}) async-start(f32[64,24,128]{2,1,0:T(8,128)} %copy-done.10), calls=%async_computation.1 | async-start | bytes 1572864 | tf_op jit(solution)/shard_map/all_to_all | solution.py:336
  62.2 0.0 copy-done.2
  62.2 0.0 collective-permute-start.2
  62.2 0.0 copy-done.19
  62.3 0.1 copy.3.refs_0_
  62.3 15.4 %collective-permute-done.2.refs_1_.refs_8_ = f32[1024,256]{1,0:T(8,128)} collective-permute-done((f32[1024,256]{1,0:T(8,128)S(1)}, f32[1024,256]{1,0:T(8,128)}, u32[]{:S(2)}, u32[]{:S(2)}) %collective-permute-start.2) | collective-permute-done | bytes 1048608 | tf_op jit(solution)/shard_map/ppermute | solution.py:322
  77.8 2.5 %shard_map.33.refs_2_.refs_1_ = f32[256,256]{1,0:T(8,128)S(1)} custom-call(f32[1024,256]{1,0:T(8,128)S(1)} %copy-done.1, f32[1024,256]{1,0:T(8,128)} %collective-permute-done.2.refs_1_.refs_8_), custom_call_target="tpu_custom_call" | custom-call | flops 1000000 | bytes 1024 | tf_op jit(solution)/shard_map/pallas_call | solution.py:307
  80.3 5.8 %all-to-all-done.1.refs_1_.refs_0_ = f32[64,24,128]{2,1,0:T(8,128)S(1)} async-done(((f32[64,24,128]{2,1,0:T(8,128)}), f32[64,24,128]{2,1,0:T(8,128)S(1)}, u32[]{:S(2)}, u32[]{:S(2)}) %all-to-all-start.1) | async-done | bytes 786464 | tf_op jit(solution)/shard_map/all_to_all | solution.py:336
  86.1 4.5 %shard_map.34 = (f32[384,256]{1,0:T(8,128)S(1)}, f32[128,128]{1,0:T(8,128)S(1)}) custom-call(s32[4,1]{1,0:T(4,128)S(1)} %copy.3.refs_0_, f32[64,24,128]{2,1,0:T(8,128)S(1)} %all-to-all-done.1.refs_1_.refs_0_, f32[256,256]{1,0:T(8,128)S(1)} %shard_map.33.refs_2_.refs_1_), custom_call_target="tpu_custom_call" | custom-call | flops 1000000 | bytes 1024 | tf_op jit(solution)/shard_map/pallas_call | solution.py:307
  90.6 0.0 collective-permute-start.3
  90.7 0.1 shard_map.36
  90.7 0.5 copy-done.17
  91.2 0.8 copy-done.11
  92.0 6.9 %all-to-all-start.2 = ((f32[64,16,128]{2,1,0:T(8,128)}), f32[64,16,128]{2,1,0:T(8,128)S(1)}, u32[]{:S(2)}, u32[]{:S(2)}) async-start(f32[64,16,128]{2,1,0:T(8,128)} %copy-done.11), calls=%async_computation.2 | async-start | bytes 1048576 | tf_op jit(solution)/shard_map/all_to_all | solution.py:336
  98.9 0.1 collective-permute-done.3.refs_4_.refs_2_.refs_1_
  99.1 0.7 copy-done.6
  99.8 1.0 copy-done.7
  100.8 0.8 copy-done.18
  101.6 4.9 %shard_map.35 = (f32[768,256]{1,0:T(8,128)S(1)}, f32[128,256]{1,0:T(8,128)S(1)}) custom-call(s32[4,1]{1,0:T(4,128)S(1)} %copy.3.refs_0_, f32[64,24,128]{2,1,0:T(8,128)S(1)} %all-to-all-done.1.refs_1_.refs_0_, f32[128,128]{1,0:T(8,128)S(1)} %copy-done.18, f32[384,256]{1,0:T(8,128)S(1)} %get-tuple-element.22.refs_3_.refs_1_.refs_0_, f32[384,256]{1,0:T(8,128)S(1)} %copy-done.7), custom_call_target="tpu_custom_call" | custom-call | flops 1000000 | bytes 1024 | tf_op jit(solution)/shard_map/pallas_call | solution.py:307
  106.5 0.6 copy-done.15
  107.1 0.0 collective-permute-start.4
  107.1 11.7 %all-to-all-done.2.refs_0_ = f32[64,16,128]{2,1,0:T(8,128)S(1)} async-done(((f32[64,16,128]{2,1,0:T(8,128)}), f32[64,16,128]{2,1,0:T(8,128)S(1)}, u32[]{:S(2)}, u32[]{:S(2)}) %all-to-all-start.2) | async-done | bytes 524320 | tf_op jit(solution)/shard_map/all_to_all | solution.py:336
  118.8 0.1 shard_map.41
  118.9 0.7 copy-done.12
  119.6 5.7 %all-to-all-start.3 = ((f32[64,8,128]{2,1,0:T(8,128)}), f32[64,8,128]{2,1,0:T(8,128)}, u32[]{:S(2)}, u32[]{:S(2)}) async-start(f32[64,8,128]{2,1,0:T(8,128)} %copy-done.12), calls=%async_computation.3 | async-start | bytes 524288 | tf_op jit(solution)/shard_map/all_to_all | solution.py:336
  125.3 0.0 collective-permute-done.4.refs_4_.refs_3_.refs_2_
  125.3 0.0 copy-start.8
  125.3 1.0 copy-done.8
  126.3 0.9 copy-done.16
  127.2 1.2 shard_map.37
  128.5 0.0 collective-permute-start.5
  128.5 4.5 %shard_map.38 = (f32[384,128]{1,0:T(8,128)S(1)}, f32[384,128]{1,0:T(8,128)S(1)}) custom-call(s32[4,1]{1,0:T(4,128)S(1)} %copy.3.refs_0_, f32[256,256]{1,0:T(8,128)S(1)} %get-tuple-element.26.refs_1_), custom_call_target="tpu_custom_call" | custom-call | flops 1000000 | bytes 1024 | tf_op jit(solution)/shard_map/pallas_call | solution.py:307
  133.0 1.7 %collective-permute-start.6 = (f32[384,128]{1,0:T(8,128)S(1)}, f32[384,128]{1,0:T(8,128)S(1)}, u32[]{:S(2)}, u32[]{:S(2)}) collective-permute-start(f32[384,128]{1,0:T(8,128)S(1)} %get-tuple-element.33), channel_id=1, source_target_pairs={{7,0},{0,1},{1,2},{2,3},{3,4},{4,5},{5,6},{6,7},{15,8},{8,9},{9,10... | collective-permute-start | bytes 589832 | tf_op jit(solution)/shard_map/ppermute | solution.py:322
  134.7 4.0 %shard_map.39 = (f32[1024,256]{1,0:T(8,128)S(1)}, f32[256,128]{1,0:T(8,128)S(1)}) custom-call(f32[384,256]{1,0:T(8,128)S(1)} %get-tuple-element.22.refs_3_.refs_1_.refs_0_, f32[384,256]{1,0:T(8,128)S(1)} %copy-done.9, f32[768,256]{1,0:T(8,128)S(1)} %get-tuple-element.24.refs_3_.refs_2_.refs_1_, ...), custom_call_target="tpu_custom_call" | custom-call | flops 1000000 | bytes 1024 | tf_op jit(solution)/shard_map/pallas_call | solution.py:307
  138.8 0.0 copy-start.4
  138.8 0.0 collective-permute-done.5.refs_3_
  138.8 3.9 %shard_map.40 = (f32[384,256]{1,0:T(8,128)S(1)}, f32[1024,128]{1,0:T(8,128)S(1)}) custom-call(f32[384,256]{1,0:T(8,128)S(1)} %get-tuple-element.22.refs_3_.refs_1_.refs_0_, f32[768,256]{1,0:T(8,128)S(1)} %get-tuple-element.24.refs_3_.refs_2_.refs_1_, f32[768,256]{1,0:T(8,128)S(1)} %collective-permute-done.4.refs_4_.refs_3_.refs_2_, ...), custom_call_target="tpu_custom_call" | custom-call | flops 1000000 | bytes 1024 | tf_op jit(solution)/shard_map/pallas_call | solution.py:307
  142.8 0.7 copy-done.13
  143.5 0.0 collective-permute-done.6.refs_4_.refs_2_
  143.5 0.0 all-to-all-done.3.refs_1_
  143.5 0.0 copy-start.14
  143.5 1.1 copy-done.14
  144.6 4.9 %shard_map.42.refs_3_ = f32[256,256]{1,0:T(8,128)S(1)} custom-call(s32[4,1]{1,0:T(4,128)S(1)} %copy.3.refs_0_, f32[64,8,128]{2,1,0:T(8,128)} %all-to-all-done.3.refs_1_, f32[384,256]{1,0:T(8,128)S(1)} %copy-done.14, f32[384,128]{1,0:T(8,128)S(1)} %get-tuple-element.27.refs_4_.refs_5_.refs_3_, f32[384,128]{1,0:T(8,128)S(1)} %collective-permute-done.6.refs_4_.refs_2_), custom_call_target="tpu_custom_call" | custom-call | flops 1000000 | bytes 1024 | tf_op jit(solution)/shard_map/pallas_call | solution.py:307
  149.5 0.0 copy-done.5
  149.5 1.0 shard_map.44
  150.4 0.0 collective-permute-start.7
  150.5 1.0 shard_map.43.kept
  151.5 8.8 %collective-permute-done.7.arrived = f32[1024,128]{1,0:T(8,128)S(1)} collective-permute-done((f32[1024,128]{1,0:T(8,128)S(1)}, f32[1024,128]{1,0:T(8,128)S(1)}, u32[]{:S(2)}, u32[]{:S(2)}) %collective-permute-start.7) | collective-permute-done | bytes 524320 | tf_op jit(solution)/shard_map/ppermute | solution.py:322
  160.3 1.0 shard_map.45
  (19 shorter events, 0.0 us)
Async XLA Ops:
  0.0 15.8 %collective-permute-start = (f32[1024,256]{1,0:T(8,128)}, f32[1024,256]{1,0:T(8,128)}, u32[]{:S(2)}, u32[]{:S(2)}) collective-permute-start(f32[1024,256]{1,0:T(8,128)} %refs_5_.1), channel_id=1, source_target_pairs={{7,0},{0,1},{1,2},{2,3},{3,4},{4,5},{5,6},{6,7},{15,8},{8,9},{9,10... | collective-permute-start | bytes 3145736 | tf_op jit(solution)/shard_map/ppermute | solution.py:322
  0.0 1.2 copy-start
  15.8 20.0 %collective-permute-start.1 = (f32[1024,256]{1,0:T(8,128)}, f32[1024,256]{1,0:T(8,128)S(1)}, u32[]{:S(2)}, u32[]{:S(2)}) collective-permute-start(f32[1024,256]{1,0:T(8,128)} %collective-permute-done.refs_1_.refs_6_), channel_id=1, source_target_pairs={{7,0},{0,1},{1,2},{2,3},{3,4},{4,5},{5,6},{6,7},{15,8},{8,9},{9,10... | collective-permute-start | bytes 3145736 | tf_op jit(solution)/shard_map/ppermute | solution.py:322
  18.3 17.4 %copy-start.1 = (f32[1024,256]{1,0:T(8,128)S(1)}, f32[1024,256]{1,0:T(8,128)}, u32[]{:S(2)}) copy-start(f32[1024,256]{1,0:T(8,128)} %refs_5_.1) | copy-start | bytes 3145732
  19.1 36.4 %all-to-all-start = ((f32[64,16,128]{2,1,0:T(8,128)}), f32[64,16,128]{2,1,0:T(8,128)S(1)}, u32[]{:S(2)}, u32[]{:S(2)}) async-start(f32[64,16,128]{2,1,0:T(8,128)} %shard_map.30), calls=%async_computation | async-start | bytes 1048576 | tf_op jit(solution)/shard_map/all_to_all | solution.py:336
  35.7 26.5 %copy-start.2 = (f32[1024,256]{1,0:T(8,128)}, f32[1024,256]{1,0:T(8,128)S(1)}, u32[]{:S(2)}) copy-start(f32[1024,256]{1,0:T(8,128)S(1)} %collective-permute-done.1.refs_1_.refs_7_) | copy-start | bytes 3145732
  55.7 0.9 copy-start.10
  56.6 5.7 %copy-start.19 = (s32[4,1]{0,1:T(1,128)S(1)}, s32[4,1]{0,1:T(1,128)}, u32[]{:S(2)}) copy-start(s32[4,1]{0,1:T(1,128)} %param.3) | copy-start | bytes 52
  56.6 29.6 %all-to-all-start.1 = ((f32[64,24,128]{2,1,0:T(8,128)}), f32[64,24,128]{2,1,0:T(8,128)S(1)}, u32[]{:S(2)}, u32[]{:S(2)}) async-start(f32[64,24,128]{2,1,0:T(8,128)} %copy-done.10), calls=%async_computation.1 | async-start | bytes 1572864 | tf_op jit(solution)/shard_map/all_to_all | solution.py:336
  62.2 15.6 %collective-permute-start.2 = (f32[1024,256]{1,0:T(8,128)S(1)}, f32[1024,256]{1,0:T(8,128)}, u32[]{:S(2)}, u32[]{:S(2)}) collective-permute-start(f32[1024,256]{1,0:T(8,128)S(1)} %collective-permute-done.1.refs_1_.refs_7_), channel_id=1, source_target_pairs={{7,0},{0,1},{1,2},{2,3},{3,4},{4,5},{5,6},{6,7},{15,8},{8,9},{9,10... | collective-permute-start | bytes 3145736 | tf_op jit(solution)/shard_map/ppermute | solution.py:322
  90.6 0.6 copy-start.17
  90.6 8.4 %collective-permute-start.3 = (f32[384,256]{1,0:T(8,128)S(1)}, f32[384,256]{1,0:T(8,128)S(1)}, u32[]{:S(2)}, u32[]{:S(2)}) collective-permute-start(f32[384,256]{1,0:T(8,128)S(1)} %get-tuple-element.22.refs_3_.refs_1_.refs_0_), channel_id=1, source_target_pairs={{7,0},{0,1},{1,2},{2,3},{3,4},{4,5},{5,6},{6,7},{15,8},{8,9},{9,10... | collective-permute-start | bytes 1179656 | tf_op jit(solution)/shard_map/ppermute | solution.py:322
  91.2 0.8 copy-start.11
  92.0 26.8 %all-to-all-start.2 = ((f32[64,16,128]{2,1,0:T(8,128)}), f32[64,16,128]{2,1,0:T(8,128)S(1)}, u32[]{:S(2)}, u32[]{:S(2)}) async-start(f32[64,16,128]{2,1,0:T(8,128)} %copy-done.11), calls=%async_computation.2 | async-start | bytes 1048576 | tf_op jit(solution)/shard_map/all_to_all | solution.py:336
  99.1 0.7 copy-start.6
  99.8 1.0 copy-start.7
  100.8 0.8 copy-start.18
  106.5 0.6 copy-start.15
  107.1 18.2 %collective-permute-start.4 = (f32[768,256]{1,0:T(8,128)S(1)}, f32[768,256]{1,0:T(8,128)S(1)}, u32[]{:S(2)}, u32[]{:S(2)}) collective-permute-start(f32[768,256]{1,0:T(8,128)S(1)} %get-tuple-element.24.refs_3_.refs_2_.refs_1_), channel_id=1, source_target_pairs={{7,0},{0,1},{1,2},{2,3},{3,4},{4,5},{5,6},{6,7},{15,8},{8,9},{9,10... | collective-permute-start | bytes 2359304 | tf_op jit(solution)/shard_map/ppermute | solution.py:322
  118.9 0.7 copy-start.12
  119.6 23.9 %all-to-all-start.3 = ((f32[64,8,128]{2,1,0:T(8,128)}), f32[64,8,128]{2,1,0:T(8,128)}, u32[]{:S(2)}, u32[]{:S(2)}) async-start(f32[64,8,128]{2,1,0:T(8,128)} %copy-done.12), calls=%async_computation.3 | async-start | bytes 524288 | tf_op jit(solution)/shard_map/all_to_all | solution.py:336
  125.3 1.0 copy-start.8
  126.3 0.9 copy-start.16
  127.2 7.5 %copy-start.3 = (f32[1024,256]{1,0:T(8,128)S(1)}, f32[1024,256]{1,0:T(8,128)}, u32[]{:S(2)}) copy-start(f32[1024,256]{1,0:T(8,128)} %copy-done.2) | copy-start | bytes 3145732
  127.2 7.5 %copy-start.9 = (f32[384,256]{1,0:T(8,128)S(1)}, f32[384,256]{1,0:T(8,128)}, u32[]{:S(2)}) copy-start(f32[384,256]{1,0:T(8,128)} %copy-done.6) | copy-start | bytes 1179652
  128.5 10.3 %collective-permute-start.5 = (f32[768,128]{1,0:T(8,128)S(1)}, f32[768,128]{1,0:T(8,128)S(1)}, u32[]{:S(2)}, u32[]{:S(2)}) collective-permute-start(f32[768,128]{1,0:T(8,128)S(1)} %get-tuple-element.29), channel_id=1, source_target_pairs={{7,0},{0,1},{1,2},{2,3},{3,4},{4,5},{5,6},{6,7},{15,8},{8,9},{9,10... | collective-permute-start | bytes 1179656 | tf_op jit(solution)/shard_map/ppermute | solution.py:322
  133.0 10.5 %collective-permute-start.6 = (f32[384,128]{1,0:T(8,128)S(1)}, f32[384,128]{1,0:T(8,128)S(1)}, u32[]{:S(2)}, u32[]{:S(2)}) collective-permute-start(f32[384,128]{1,0:T(8,128)S(1)} %get-tuple-element.33), channel_id=1, source_target_pairs={{7,0},{0,1},{1,2},{2,3},{3,4},{4,5},{5,6},{6,7},{15,8},{8,9},{9,10... | collective-permute-start | bytes 589832 | tf_op jit(solution)/shard_map/ppermute | solution.py:322
  138.8 4.0 %copy-start.4 = (f32[1024,256]{1,0:T(8,128)}, f32[1024,256]{1,0:T(8,128)S(1)}, u32[]{:S(2)}) copy-start(f32[1024,256]{1,0:T(8,128)S(1)} %get-tuple-element.28.refs_0_) | copy-start | bytes 3145732
  142.7 0.7 copy-start.13
  143.5 6.0 %copy-start.5 = (f32[1024,256]{1,0:T(8,128)S(1)}, f32[1024,256]{1,0:T(8,128)}, u32[]{:S(2)}) copy-start(f32[1024,256]{1,0:T(8,128)} %copy-done.4) | copy-start | bytes 3145732
  143.5 1.1 copy-start.14
  150.4 9.8 %collective-permute-start.7 = (f32[1024,128]{1,0:T(8,128)S(1)}, f32[1024,128]{1,0:T(8,128)S(1)}, u32[]{:S(2)}, u32[]{:S(2)}) collective-permute-start(f32[1024,128]{1,0:T(8,128)S(1)} %shard_map.44), channel_id=1, source_target_pairs={{7,0},{0,1},{1,2},{2,3},{3,4},{4,5},{5,6},{6,7},{15,8},{8,9},{9,10... | collective-permute-start | bytes 1572872 | tf_op jit(solution)/shard_map/ppermute | solution.py:322

commit v8 on v7

--- a/solution.py
+++ b/solution.py
@@ -179,18 +179,19 @@
     r1 = cross_dot(cross_dot(out0[:N], square_of(received, 1), (0, 0)), q0_p)
     out[N + HALF : 2 * N] = r1[HALF:]
     out[2 * N :] = q0_p
-    carried[:, HALF:] = r1[:HALF, :HALF]
+    carried[:, HALF:N] = r1[:HALF, :HALF]
+    carried[:, N:] = in0[N:, :HALF]
     q1, h1 = jacobi(joined(h0[...], r1[:HALF, HALF:], in0[N:, HALF:]), ROUNDS, second[1, 0], parts)
     out[:N] = q1
     out[N : N + HALF] = h1[HALF:]
     carried[:, :HALF] = h1[:HALF, :HALF]
 
 
-def cross2_kernel(received, out0, in0, out1, in1, carried, out, kept, gram):
+def cross2_kernel(received, out0, out1, in1, carried, out, kept, gram):
     q0_pp = in1[2 * N :]
     r2 = cross_dot(cross_dot(out0[:N], square_of(received, 0), (0, 0)), q0_pp)
-    upper = jnp.concatenate([carried[:, HALF:], r2[:HALF, HALF:]], axis=1)
-    lower = jnp.concatenate([in0[N:, :HALF], in1[N + HALF : 2 * N, HALF:]], axis=1)
+    upper = jnp.concatenate([carried[:, HALF:N], r2[:HALF, HALF:]], axis=1)
+    lower = jnp.concatenate([carried[:, N:], in1[N + HALF : 2 * N, HALF:]], axis=1)
     s1 = cross_dot(cross_dot(out1[:N], jnp.concatenate([upper, lower], axis=0), (0, 0)), in1[:N])
     gram[...] = joined(carried[:, :HALF], s1[:HALF, HALF:], in1[N : N + HALF, HALF:])
     out[:HALF] = s1[HALF:, HALF:]
@@ -349,7 +350,7 @@
     in0 = onward(out0)
     out1, carried = run(
         step1_kernel,
-        [(3 * N, N), (HALF, N)],
+        [(3 * N, N), (HALF, N + HALF)],
         *(sender_slot, with_c1, h0, out0, in0),
         scratch=JACOBI_PARTS,
     )
@@ -358,7 +359,7 @@
     out2a, kept, gram2 = run(
         cross2_kernel,
         [(3 * N, HALF), (N, HALF), square],
-        *(with_c2, out0, in0, out1, in1, carried),
+        *(with_c2, out0, out1, in1, carried),
     )
     in2a = onward(out2a)
     out2b, own2 = run(step2_kernel, [(N + HALF, HALF)] * 2, sender_slot, gram2, scratch=JACOBI_PARTS)

time: 162 us -> 162 us (level)
  local copies, waits for them, and re-layouts: 11.2 us -> 8.6 us
    unnamed x41 -> x37, local copies, waits for them, and re-layouts: 11.2 us -> 8.6 us
  transfers between devices with their start and end apart: 12 -> 12, of which waited for: 7 -> 7; matrix products, arithmetic and copies ran while one was open for 0% -> 0% of each run, Pallas kernels for 17% -> 18%
where the time goes in v8:
time: 162 us; the launch traced here: 161 us
  waiting for transfers between devices  75 us (46%)
  Pallas kernels  41 us (25%)
  starting transfers between devices  36.2 us (22%)
  local copies, waits for them, and re-layouts  8.6 us (5%)
    pallas_call x17, Pallas kernels, run(): pl.pallas_call(body, out_shape=[jax.ShapeDtypeStruct(shape, jnp.float32)...  40 us
    ppermute x8, waiting for transfers between devices, onward(): lax.ppermute(values, 'blk', [((i - places) % devices, i) for i in range(d...  38.2 us
    all_to_all x4, waiting for transfers between devices, exchange(): return lax.all_to_all(pieces, 'row', 0, 0, tiled=True)  36.8 us
    all_to_all x4, starting transfers between devices, exchange(): return lax.all_to_all(pieces, 'row', 0, 0, tiled=True)  35.2 us
    unnamed x37, local copies, waits for them, and re-layouts  8.6 us
  transfers between devices with their start and end apart: 12, of which 7 were waited for; matrix products, arithmetic and copies ran while one was open for 0% of the time, Pallas kernels for 18%

profile of v8, /device:TPU:8, one launch (start us, length us, event | category | flops | bytes accessed | tf_op | source)
XLA Modules:
  0.0 161.3 jit_solution(17624431810563053852)
XLA Ops:
  0.0 0.0 collective-permute-start
  0.0 1.2 copy-done
  1.2 1.3 shard_map.28.refs_0_
  2.5 13.2 %collective-permute-done.refs_1_.refs_6_ = f32[1024,256]{1,0:T(8,128)} collective-permute-done((f32[1024,256]{1,0:T(8,128)}, f32[1024,256]{1,0:T(8,128)}, u32[]{:S(2)}, u32[]{:S(2)}) %collective-permute-start) | collective-permute-done | bytes 1048608 | tf_op jit(solution)/shard_map/ppermute | solution.py:323
  15.8 0.0 collective-permute-start.1
  15.8 2.5 %shard_map.29.refs_1_ = f32[256,256]{1,0:T(8,128)S(1)} custom-call(f32[1024,256]{1,0:T(8,128)S(1)} %copy-done, f32[1024,256]{1,0:T(8,128)} %collective-permute-done.refs_1_.refs_6_), custom_call_target="tpu_custom_call" | custom-call | flops 1000000 | bytes 1024 | tf_op jit(solution)/shard_map/pallas_call | solution.py:308
  18.3 0.0 copy-start.1
  18.3 0.8 shard_map.30
  19.1 16.6 %all-to-all-start = ((f32[64,16,128]{2,1,0:T(8,128)}), f32[64,16,128]{2,1,0:T(8,128)S(1)}, u32[]{:S(2)}, u32[]{:S(2)}) async-start(f32[64,16,128]{2,1,0:T(8,128)} %shard_map.30), calls=%async_computation | async-start | bytes 1048576 | tf_op jit(solution)/shard_map/all_to_all | solution.py:337
  35.7 0.0 collective-permute-done.1.refs_1_.refs_7_
  35.7 0.0 copy-done.1
  35.7 0.0 copy-start.2
  35.8 1.3 shard_map.31.refs_1_
  37.1 18.5 %all-to-all-done.refs_0_ = f32[64,16,128]{2,1,0:T(8,128)S(1)} async-done(((f32[64,16,128]{2,1,0:T(8,128)}), f32[64,16,128]{2,1,0:T(8,128)S(1)}, u32[]{:S(2)}, u32[]{:S(2)}) %all-to-all-start) | async-done | bytes 524320 | tf_op jit(solution)/shard_map/all_to_all | solution.py:337
  55.6 0.1 shard_map.32
  55.7 0.0 copy-start.6
  55.7 0.9 copy-done.6
  56.6 5.6 %all-to-all-start.1 = ((f32[64,24,128]{2,1,0:T(8,128)}), f32[64,24,128]{2,1,0:T(8,128)S(1)}, u32[]{:S(2)}, u32[]{:S(2)}) async-start(f32[64,24,128]{2,1,0:T(8,128)} %copy-done.6), calls=%async_computation.1 | async-start | bytes 1572864 | tf_op jit(solution)/shard_map/all_to_all | solution.py:337
  62.2 0.0 copy-done.2
  62.2 0.0 collective-permute-start.2
  62.2 0.0 copy-done.17
  62.3 0.1 copy.3.refs_0_
  62.4 15.4 %collective-permute-done.2.refs_1_.refs_8_ = f32[1024,256]{1,0:T(8,128)} collective-permute-done((f32[1024,256]{1,0:T(8,128)S(1)}, f32[1024,256]{1,0:T(8,128)}, u32[]{:S(2)}, u32[]{:S(2)}) %collective-permute-start.2) | collective-permute-done | bytes 1048608 | tf_op jit(solution)/shard_map/ppermute | solution.py:323
  77.8 2.5 %shard_map.33.refs_2_.refs_1_ = f32[256,256]{1,0:T(8,128)S(1)} custom-call(f32[1024,256]{1,0:T(8,128)S(1)} %copy-done.1, f32[1024,256]{1,0:T(8,128)} %collective-permute-done.2.refs_1_.refs_8_), custom_call_target="tpu_custom_call" | custom-call | flops 1000000 | bytes 1024 | tf_op jit(solution)/shard_map/pallas_call | solution.py:308
  80.3 5.8 %all-to-all-done.1.refs_1_.refs_0_ = f32[64,24,128]{2,1,0:T(8,128)S(1)} async-done(((f32[64,24,128]{2,1,0:T(8,128)}), f32[64,24,128]{2,1,0:T(8,128)S(1)}, u32[]{:S(2)}, u32[]{:S(2)}) %all-to-all-start.1) | async-done | bytes 786464 | tf_op jit(solution)/shard_map/all_to_all | solution.py:337
  86.1 4.5 %shard_map.34 = (f32[384,256]{1,0:T(8,128)S(1)}, f32[128,128]{1,0:T(8,128)S(1)}) custom-call(s32[4,1]{1,0:T(4,128)S(1)} %copy.3.refs_0_, f32[64,24,128]{2,1,0:T(8,128)S(1)} %all-to-all-done.1.refs_1_.refs_0_, f32[256,256]{1,0:T(8,128)S(1)} %shard_map.33.refs_2_.refs_1_), custom_call_target="tpu_custom_call" | custom-call | flops 1000000 | bytes 1024 | tf_op jit(solution)/shard_map/pallas_call | solution.py:308
  90.6 0.0 copy-start.15
  90.6 0.6 copy-done.15
  91.2 0.0 collective-permute-start.3
  91.2 0.9 shard_map.36
  92.1 6.9 %all-to-all-start.2 = ((f32[64,16,128]{2,1,0:T(8,128)}), f32[64,16,128]{2,1,0:T(8,128)S(1)}, u32[]{:S(2)}, u32[]{:S(2)}) async-start(f32[64,16,128]{2,1,0:T(8,128)} %shard_map.36), calls=%async_computation.2 | async-start | bytes 1048576 | tf_op jit(solution)/shard_map/all_to_all | solution.py:337
  99.0 0.7 collective-permute-done.3.refs_4_.refs_1_
  99.8 0.8 copy-done.16
  100.6 5.3 %shard_map.35 = (f32[768,256]{1,0:T(8,128)S(1)}, f32[128,384]{1,0:T(8,128)S(1)}) custom-call(s32[4,1]{1,0:T(4,128)S(1)} %copy.3.refs_0_, f32[64,24,128]{2,1,0:T(8,128)S(1)} %all-to-all-done.1.refs_1_.refs_0_, f32[128,128]{1,0:T(8,128)S(1)} %copy-done.16, f32[384,256]{1,0:T(8,128)S(1)} %get-tuple-element.22.refs_3_.refs_1_.refs_0_, ...), custom_call_target="tpu_custom_call" | custom-call | flops 1000000 | bytes 1024 | tf_op jit(solution)/shard_map/pallas_call | solution.py:308
  105.9 0.7 copy-done.13
  106.6 0.0 collective-permute-start.4
  106.6 12.5 %all-to-all-done.2.refs_0_ = f32[64,16,128]{2,1,0:T(8,128)S(1)} async-done(((f32[64,16,128]{2,1,0:T(8,128)}), f32[64,16,128]{2,1,0:T(8,128)S(1)}, u32[]{:S(2)}, u32[]{:S(2)}) %all-to-all-start.2) | async-done | bytes 524320 | tf_op jit(solution)/shard_map/all_to_all | solution.py:337
  119.1 0.1 shard_map.41
  119.2 0.7 copy-done.12
  119.9 6.1 %all-to-all-start.3 = ((f32[64,8,128]{2,1,0:T(8,128)}), f32[64,8,128]{2,1,0:T(8,128)}, u32[]{:S(2)}, u32[]{:S(2)}) async-start(f32[64,8,128]{2,1,0:T(8,128)} %copy-done.12), calls=%async_computation.3 | async-start | bytes 524288 | tf_op jit(solution)/shard_map/all_to_all | solution.py:337
  125.9 0.0 collective-permute-done.4.refs_3_.refs_2_
  126.0 0.0 copy-start.14
  126.0 0.9 copy-done.14
  126.9 1.2 shard_map.37
  128.1 0.0 collective-permute-start.5
  128.1 4.5 %shard_map.38 = (f32[384,128]{1,0:T(8,128)S(1)}, f32[384,128]{1,0:T(8,128)S(1)}) custom-call(s32[4,1]{1,0:T(4,128)S(1)} %copy.3.refs_0_, f32[256,256]{1,0:T(8,128)S(1)} %get-tuple-element.26.refs_1_), custom_call_target="tpu_custom_call" | custom-call | flops 1000000 | bytes 1024 | tf_op jit(solution)/shard_map/pallas_call | solution.py:308
  132.6 0.9 collective-permute-start.6
  133.6 0.0 copy-done.3
  133.6 4.2 %shard_map.39 = (f32[1024,256]{1,0:T(8,128)S(1)}, f32[256,128]{1,0:T(8,128)S(1)}) custom-call(f32[384,256]{1,0:T(8,128)S(1)} %get-tuple-element.22.refs_3_.refs_1_.refs_0_, f32[384,256]{1,0:T(8,128)} %collective-permute-done.3.refs_4_.refs_1_, f32[768,256]{1,0:T(8,128)S(1)} %get-tuple-element.24.refs_2_.refs_1_, ...), custom_call_target="tpu_custom_call" | custom-call | flops 1000000 | bytes 1024 | tf_op jit(solution)/shard_map/pallas_call | solution.py:308
  137.7 0.0 copy-start.4
  137.8 0.0 collective-permute-done.5.refs_3_
  137.8 3.9 %shard_map.40 = (f32[384,256]{1,0:T(8,128)S(1)}, f32[1024,128]{1,0:T(8,128)S(1)}) custom-call(f32[384,256]{1,0:T(8,128)S(1)} %get-tuple-element.22.refs_3_.refs_1_.refs_0_, f32[768,256]{1,0:T(8,128)S(1)} %get-tuple-element.24.refs_2_.refs_1_, f32[768,256]{1,0:T(8,128)S(1)} %collective-permute-done.4.refs_3_.refs_2_, ...), custom_call_target="tpu_custom_call" | custom-call | flops 1000000 | bytes 1024 | tf_op jit(solution)/shard_map/pallas_call | solution.py:308
  141.7 0.0 collective-permute-done.6.refs_4_.refs_2_
  141.7 0.0 copy-start.9
  141.7 0.7 copy-done.9
  142.4 0.0 all-to-all-done.3.refs_1_
  142.4 1.0 copy-done.8
  143.4 0.9 copy-done.10
  144.4 4.9 %shard_map.42.refs_3_ = f32[256,256]{1,0:T(8,128)S(1)} custom-call(s32[4,1]{1,0:T(4,128)S(1)} %copy.3.refs_0_, f32[64,8,128]{2,1,0:T(8,128)} %all-to-all-done.3.refs_1_, f32[384,256]{1,0:T(8,128)S(1)} %get-tuple-element.34.refs_2_, f32[384,128]{1,0:T(8,128)S(1)} %copy-done.8, f32[384,128]{1,0:T(8,128)S(1)} %copy-done.10), custom_call_target="tpu_custom_call" | custom-call | flops 1000000 | bytes 1024 | tf_op jit(solution)/shard_map/pallas_call | solution.py:308
  149.3 1.0 shard_map.44
  150.3 0.1 collective-permute-start.7
  150.3 1.0 shard_map.43.kept
  151.3 8.8 %collective-permute-done.7.arrived = f32[1024,128]{1,0:T(8,128)S(1)} collective-permute-done((f32[1024,128]{1,0:T(8,128)S(1)}, f32[1024,128]{1,0:T(8,128)S(1)}, u32[]{:S(2)}, u32[]{:S(2)}) %collective-permute-start.7) | collective-permute-done | bytes 524320 | tf_op jit(solution)/shard_map/ppermute | solution.py:323
  160.1 1.0 shard_map.45
  (15 shorter events, 0.0 us)
Async XLA Ops:
  0.0 15.8 %collective-permute-start = (f32[1024,256]{1,0:T(8,128)}, f32[1024,256]{1,0:T(8,128)}, u32[]{:S(2)}, u32[]{:S(2)}) collective-permute-start(f32[1024,256]{1,0:T(8,128)} %refs_5_.1), channel_id=1, source_target_pairs={{7,0},{0,1},{1,2},{2,3},{3,4},{4,5},{5,6},{6,7},{15,8},{8,9},{9,10... | collective-permute-start | bytes 3145736 | tf_op jit(solution)/shard_map/ppermute | solution.py:323
  0.0 1.2 copy-start
  15.8 20.0 %collective-permute-start.1 = (f32[1024,256]{1,0:T(8,128)}, f32[1024,256]{1,0:T(8,128)S(1)}, u32[]{:S(2)}, u32[]{:S(2)}) collective-permute-start(f32[1024,256]{1,0:T(8,128)} %collective-permute-done.refs_1_.refs_6_), channel_id=1, source_target_pairs={{7,0},{0,1},{1,2},{2,3},{3,4},{4,5},{5,6},{6,7},{15,8},{8,9},{9,10... | collective-permute-start | bytes 3145736 | tf_op jit(solution)/shard_map/ppermute | solution.py:323
  18.3 17.5 %copy-start.1 = (f32[1024,256]{1,0:T(8,128)S(1)}, f32[1024,256]{1,0:T(8,128)}, u32[]{:S(2)}) copy-start(f32[1024,256]{1,0:T(8,128)} %refs_5_.1) | copy-start | bytes 3145732
  19.1 36.4 %all-to-all-start = ((f32[64,16,128]{2,1,0:T(8,128)}), f32[64,16,128]{2,1,0:T(8,128)S(1)}, u32[]{:S(2)}, u32[]{:S(2)}) async-start(f32[64,16,128]{2,1,0:T(8,128)} %shard_map.30), calls=%async_computation | async-start | bytes 1048576 | tf_op jit(solution)/shard_map/all_to_all | solution.py:337
  35.7 26.5 %copy-start.2 = (f32[1024,256]{1,0:T(8,128)}, f32[1024,256]{1,0:T(8,128)S(1)}, u32[]{:S(2)}) copy-start(f32[1024,256]{1,0:T(8,128)S(1)} %collective-permute-done.1.refs_1_.refs_7_) | copy-start | bytes 3145732
  55.7 0.9 copy-start.6
  56.6 5.7 %copy-start.17 = (s32[4,1]{0,1:T(1,128)S(1)}, s32[4,1]{0,1:T(1,128)}, u32[]{:S(2)}) copy-start(s32[4,1]{0,1:T(1,128)} %param.3) | copy-start | bytes 52
  56.6 29.6 %all-to-all-start.1 = ((f32[64,24,128]{2,1,0:T(8,128)}), f32[64,24,128]{2,1,0:T(8,128)S(1)}, u32[]{:S(2)}, u32[]{:S(2)}) async-start(f32[64,24,128]{2,1,0:T(8,128)} %copy-done.6), calls=%async_computation.1 | async-start | bytes 1572864 | tf_op jit(solution)/shard_map/all_to_all | solution.py:337
  62.2 15.6 %collective-permute-start.2 = (f32[1024,256]{1,0:T(8,128)S(1)}, f32[1024,256]{1,0:T(8,128)}, u32[]{:S(2)}, u32[]{:S(2)}) collective-permute-start(f32[1024,256]{1,0:T(8,128)S(1)} %collective-permute-done.1.refs_1_.refs_7_), channel_id=1, source_target_pairs={{7,0},{0,1},{1,2},{2,3},{3,4},{4,5},{5,6},{6,7},{15,8},{8,9},{9,10... | collective-permute-start | bytes 3145736 | tf_op jit(solution)/shard_map/ppermute | solution.py:323
  90.6 0.6 copy-start.15
  91.2 8.5 %collective-permute-start.3 = (f32[384,256]{1,0:T(8,128)S(1)}, f32[384,256]{1,0:T(8,128)}, u32[]{:S(2)}, u32[]{:S(2)}) collective-permute-start(f32[384,256]{1,0:T(8,128)S(1)} %get-tuple-element.22.refs_3_.refs_1_.refs_0_), channel_id=1, source_target_pairs={{7,0},{0,1},{1,2},{2,3},{3,4},{4,5},{5,6},{6,7},{15,8},{8,9},{9,10... | collective-permute-start | bytes 1179656 | tf_op jit(solution)/shard_map/ppermute | solution.py:323
  92.1 26.9 %all-to-all-start.2 = ((f32[64,16,128]{2,1,0:T(8,128)}), f32[64,16,128]{2,1,0:T(8,128)S(1)}, u32[]{:S(2)}, u32[]{:S(2)}) async-start(f32[64,16,128]{2,1,0:T(8,128)} %shard_map.36), calls=%async_computation.2 | async-start | bytes 1048576 | tf_op jit(solution)/shard_map/all_to_all | solution.py:337
  99.8 0.8 copy-start.16
  105.9 0.7 copy-start.13
  106.6 19.4 %collective-permute-start.4 = (f32[768,256]{1,0:T(8,128)S(1)}, f32[768,256]{1,0:T(8,128)S(1)}, u32[]{:S(2)}, u32[]{:S(2)}) collective-permute-start(f32[768,256]{1,0:T(8,128)S(1)} %get-tuple-element.24.refs_2_.refs_1_), channel_id=1, source_target_pairs={{7,0},{0,1},{1,2},{2,3},{3,4},{4,5},{5,6},{6,7},{15,8},{8,9},{9,10... | collective-permute-start | bytes 2359304 | tf_op jit(solution)/shard_map/ppermute | solution.py:323
  119.1 0.7 copy-start.12
  119.9 22.5 %all-to-all-start.3 = ((f32[64,8,128]{2,1,0:T(8,128)}), f32[64,8,128]{2,1,0:T(8,128)}, u32[]{:S(2)}, u32[]{:S(2)}) async-start(f32[64,8,128]{2,1,0:T(8,128)} %copy-done.12), calls=%async_computation.3 | async-start | bytes 524288 | tf_op jit(solution)/shard_map/all_to_all | solution.py:337
  126.0 0.9 copy-start.14
  126.9 6.7 %copy-start.3 = (f32[1024,256]{1,0:T(8,128)S(1)}, f32[1024,256]{1,0:T(8,128)}, u32[]{:S(2)}) copy-start(f32[1024,256]{1,0:T(8,128)} %copy-done.2) | copy-start | bytes 3145732
  128.1 9.6 %collective-permute-start.5 = (f32[768,128]{1,0:T(8,128)S(1)}, f32[768,128]{1,0:T(8,128)S(1)}, u32[]{:S(2)}, u32[]{:S(2)}) collective-permute-start(f32[768,128]{1,0:T(8,128)S(1)} %get-tuple-element.29), channel_id=1, source_target_pairs={{7,0},{0,1},{1,2},{2,3},{3,4},{4,5},{5,6},{6,7},{15,8},{8,9},{9,10... | collective-permute-start | bytes 1179656 | tf_op jit(solution)/shard_map/ppermute | solution.py:323
  132.6 5.1 %copy-start.7 = (f32[384,128]{1,0:T(8,128)}, f32[384,128]{1,0:T(8,128)S(1)}, u32[]{:S(2)}) copy-start(f32[384,128]{1,0:T(8,128)S(1)} %get-tuple-element.27.refs_4_.refs_5_.refs_3_) | copy-start | bytes 589828
  132.6 9.1 %collective-permute-start.6 = (f32[384,128]{1,0:T(8,128)S(1)}, f32[384,128]{1,0:T(8,128)S(1)}, u32[]{:S(2)}, u32[]{:S(2)}) collective-permute-start(f32[384,128]{1,0:T(8,128)S(1)} %get-tuple-element.33), channel_id=1, source_target_pairs={{7,0},{0,1},{1,2},{2,3},{3,4},{4,5},{5,6},{6,7},{15,8},{8,9},{9,10... | collective-permute-start | bytes 589832 | tf_op jit(solution)/shard_map/ppermute | solution.py:323
  137.7 4.0 %copy-start.4 = (f32[1024,256]{1,0:T(8,128)}, f32[1024,256]{1,0:T(8,128)S(1)}, u32[]{:S(2)}) copy-start(f32[1024,256]{1,0:T(8,128)S(1)} %get-tuple-element.28.refs_0_) | copy-start | bytes 3145732
  141.7 0.7 copy-start.9
  142.4 6.9 %copy-start.5 = (f32[1024,256]{1,0:T(8,128)S(1)}, f32[1024,256]{1,0:T(8,128)}, u32[]{:S(2)}) copy-start(f32[1024,256]{1,0:T(8,128)} %copy-done.4) | copy-start | bytes 3145732
  142.4 1.0 copy-start.8
  143.4 0.9 copy-start.10
  144.3 4.9 %copy-start.11 = (f32[384,128]{1,0:T(8,128)S(1)}, f32[384,128]{1,0:T(8,128)}, u32[]{:S(2)}) copy-start(f32[384,128]{1,0:T(8,128)} %copy-done.9) | copy-start | bytes 589828
  150.3 9.8 %collective-permute-start.7 = (f32[1024,128]{1,0:T(8,128)S(1)}, f32[1024,128]{1,0:T(8,128)S(1)}, u32[]{:S(2)}, u32[]{:S(2)}) collective-permute-start(f32[1024,128]{1,0:T(8,128)S(1)} %shard_map.44), channel_id=1, source_target_pairs={{7,0},{0,1},{1,2},{2,3},{3,4},{4,5},{5,6},{6,7},{15,8},{8,9},{9,10... | collective-permute-start | bytes 1572872 | tf_op jit(solution)/shard_map/ppermute | solution.py:323
